TPU v7x, 256 devices: a whole 4x4x8 slice. The times are simulated.
256 devices in a mesh: pool: 32 (over x, z), tp: 8 (over y, core).
Axes of the slice: x: 4, y: 4, z: 8, core: 2. Of those that a mesh axis runs over, the one named last changes fastest.
Arguments:
- hidden_rows: bfloat16 [512, 16384], P('pool', 'tp'), may hold values from -6 to 6
- queries: bfloat16 [512, 16384], P('pool', 'tp'), may hold values from -64 to 64
- cache_keys: bfloat16 [512, 128, 1024], P('pool', None, 'tp'), may hold values from -64 to 64
- cache_values: bfloat16 [512, 128, 1024], P('pool', None, 'tp'), may hold values from -6 to 6
- new_keys: bfloat16 [512, 1024], P('pool', 'tp'), may hold values from -6 to 6
- new_values: bfloat16 [512, 1024], P('pool', 'tp'), may hold values from -6 to 6
- lengths: int32 [512], P('pool'), may hold values from 2 to 128, as said below
- norm_gain: bfloat16 [16384], P('tp'), may hold values from 0.099609375 to 1.8984375
- w_gate: bfloat16 [16384, 28672], P('tp', 'pool'), may hold values from -0.046875 to 0.046875
- w_up: bfloat16 [16384, 28672], P('tp', 'pool'), may hold values from -0.046875 to 0.046875
- w_down: bfloat16 [28672, 16384], P('pool', 'tp'), may hold values from -0.03125 to 0.03125
Outputs:
- layer_out: bfloat16 [512, 16384], P('pool', 'tp')
Inputs may be any that keep to these rules, and one draw needn't show every extreme that they name: `lengths`: every draw has a request with all 128 slots live.
All inputs are finite; a program needn't handle non-finite values.
Results may differ from a plain program's by a relative error of at most 0.007.
Values may be sent and summed in bfloat16 or wider, within the bound.
No kernel may reach another device: no remote copies, remote signals or barrier semaphores. Data moves between devices by JAX's collectives and lax.ppermute only.
A program may use at most 64 MiB of HBM per device.

v0:
```python
import functools

import jax
import jax.numpy as jnp
from jax import lax
from jax.experimental import pallas as pl
from jax.experimental.pallas import tpu as pltpu
from jax.sharding import Mesh
from jax.sharding import PartitionSpec as P

D = 16384
HEAD_DIM = 128
NX, NZ, NY, NC = 4, 8, 4, 2
TP = ("y", "core")
MARKS = 128
MIB = 1 << 20
ORDER = (0, -1, 1, -2, 2, -3, 3, 4)
EARLY = 5


def shift(v, axis, by, n):
    return lax.ppermute(v, axis, [(i, (i + by) % n) for i in range(n)])


def rows_at(start, count):
    return pl.ds(pl.multiple_of(start, count), count)


def call(kernel, outs, args, kinds, scratch=(), flops=0, moved=0, limit=16 * MIB, alias=None):
    spaces = {"s": pltpu.SMEM, "v": pltpu.VMEM, "h": pltpu.HBM}
    single = not isinstance(outs, (list, tuple))
    whole = [outs] if single else list(outs)
    got = pl.pallas_call(
        kernel,
        out_shape=whole,
        in_specs=[pl.BlockSpec(memory_space=spaces[k]) for k in kinds],
        out_specs=[pl.BlockSpec(memory_space=pltpu.VMEM)] * len(whole),
        scratch_shapes=list(scratch),
        input_output_aliases=alias or {},
        compiler_params=pltpu.CompilerParams(vmem_limit_bytes=limit),
        cost_estimate=pl.CostEstimate(flops=flops, bytes_accessed=moved, transcendentals=0),
    )(*args)
    return got[0] if single else got


def shape(*dims, kind=jnp.bfloat16):
    return jax.ShapeDtypeStruct(dims, kind)


def copy_in(pairs, sems):
    copies = [pltpu.make_async_copy(src, dst, sems.at[i]) for i, (src, dst) in enumerate(pairs)]
    for copy in copies:
        copy.start()
    for copy in copies:
        copy.wait()


def copy_in(pairs, sems):
    copies = [pltpu.make_async_copy(src, dst, sems.at[i]) for i, (src, dst) in enumerate(pairs)]
    for copy in copies:
        copy.start()
    for copy in copies:
        copy.wait()


def start_rows(scale, lengths_in, hidden_in, queries_in, keys_in, values_in, own_keys_in, own_values_in, gain_in, *rest):
    stream, inv_gain2, out, lengths, hidden, queries, keys, values, own_keys, own_values, gain, heads, work, low, sems = rest
    copy_in(
        [
            (queries_in, queries),
            (lengths_in, lengths),
            (keys_in, keys),
            (values_in, values),
            (own_keys_in, own_keys),
            (own_values_in, own_values),
            (hidden_in, hidden),
            (gain_in, gain),
        ],
        sems,
    )
    rows, feats = hidden.shape
    per = feats // HEAD_DIM
    ctx = keys.shape[1]
    f32, bf16 = jnp.float32, jnp.bfloat16
    wide = queries[...].astype(f32)
    for h in range(per):
        heads[pl.ds(h, rows, stride=per), :] = wide[:, h * HEAD_DIM : (h + 1) * HEAD_DIM]
    slot = lax.broadcasted_iota(jnp.int32, (per, ctx), 1)

    def spread(ref):
        each = ref[...].astype(f32)
        return jnp.concatenate(
            [jnp.broadcast_to(each[r : r + 1, :], (per, HEAD_DIM)) for r in range(rows)], axis=0
        )

    for r in range(rows):
        score = lax.dot_general(
            heads[pl.ds(r * per, per), :].astype(bf16),
            keys[r],
            (((1,), (1,)), ((), ())),
            preferred_element_type=f32,
        )
        work[pl.ds(r * per, per), :] = jnp.where(slot < lengths[r], score * scale, -1e30)
    own = jnp.sum(heads[...] * spread(own_keys), axis=1, keepdims=True) * scale
    score = work[...]
    top = jnp.maximum(jnp.max(score, axis=1, keepdims=True), own)
    weight = jnp.exp(score - top)
    own_weight = jnp.exp(own - top)
    total = jnp.sum(weight, axis=1, keepdims=True) + own_weight
    low[...] = weight.astype(bf16)
    for r in range(rows):
        work[pl.ds(r * per, per), :] = jnp.dot(low[pl.ds(r * per, per), :], values[r], preferred_element_type=f32)
    work[...] = (work[...] + own_weight.astype(bf16).astype(f32) * spread(own_values)) / total
    scales = gain[...].astype(f32)
    inv_gain2[...] = 1.0 / (scales * scales)
    for h in range(per):
        cols = slice(h * HEAD_DIM, (h + 1) * HEAD_DIM)
        got = hidden[:, cols].astype(f32) + work[pl.ds(h, rows, stride=per), :]
        stream[:, cols] = got
        out[:, cols] = (got * scales[h : h + 1, :]).astype(bf16)


def join(*refs):
    parts, out = refs[:-1], refs[-1]
    size = parts[0].shape[0]
    for k, part in enumerate(parts):
        out[pl.ds(k * size, size), :] = part[...]


def place(core, pieces, part):
    top = part.shape[0] // 2
    at = 0
    spare = []
    for piece in pieces:
        half = piece.shape[0] // 2
        if piece.shape[0] < pieces[0].shape[0]:
            spare.append(piece)
            continue
        part[pl.ds(at, half), :] = piece[rows_at(core * half, half), :]
        part[pl.ds(top + at, half), :] = piece[rows_at((1 - core) * half, half), :]
        at += half
    for i, piece in enumerate(spare):
        half = piece.shape[0]
        part[rows_at(lax.rem(core + i, NC) * top + at, half), :] = piece[...]


def squares(width, part, inv_gain2, keep, send):
    top = part.shape[0] // 2
    step = 32
    lane = lax.broadcasted_iota(jnp.int32, (step, MARKS), 1)
    for i in range(2 * top // step):
        sums = 0.0
        for h in range(part.shape[1] // HEAD_DIM):
            wide = part[pl.ds(i * step, step), pl.ds(h * HEAD_DIM, HEAD_DIM)].astype(jnp.float32)
            sums = sums + wide * wide * inv_gain2[pl.ds(h, 1), :]
        sums = jnp.sum(sums, axis=1, keepdims=True)
        high = sums.astype(jnp.bfloat16).astype(jnp.float32)
        marks = jnp.where(lane == 0, high, jnp.where(lane == 1, sums - high, 0.0))
        out = keep if i * step < top else send
        out[pl.ds(i * step % top, step), pl.ds(2 * width, MARKS)] = marks.astype(jnp.bfloat16)


def project(weights, base, part, keep, send):
    top, width = part.shape[0] // 2, weights.shape[1]

    def tile(start, size):
        terms = jnp.dot(part[...], weights[:, pl.ds(start, size)], preferred_element_type=jnp.float32)
        keep[:, pl.ds(base + start, size)] = terms[:top].astype(jnp.bfloat16)
        send[:, pl.ds(base + start, size)] = terms[top:].astype(jnp.bfloat16)

    pl.loop(0, width // 256)(lambda t: tile(pl.multiple_of(t * 256, 256), 256))
    if width % 256:
        tile(width // 256 * 256, width % 256)


def gate_matmul(width, idx, *refs):
    pieces, (inv_gain2, w_gate, keep, send, part, done) = refs[:-6], refs[-6:]
    place(idx[3], pieces, part)
    squares(width, part, inv_gain2, keep, send)
    project(w_gate, 0, part, keep, send)
    done[...] = jnp.zeros_like(done)


def up_matmul(width, part, w_up, keep_in, send_in, keep, send):
    project(w_up, width, part, keep, send)


def both_matmul(width, idx, *refs):
    pieces, (inv_gain2, w_gate, w_up, keep, send, part) = refs[:-6], refs[-6:]
    place(idx[3], pieces, part)
    squares(width, part, inv_gain2, keep, send)
    project(w_gate, 0, part, keep, send)
    project(w_up, width, part, keep, send)


def halves(up, down, _, up_half, down_half):
    size = up_half.shape[0]
    up_half[...] = up[pl.ds(0, size), :]
    down_half[...] = down[pl.ds(size, size), :]


def core_sum(block, idx, keep, keep_late, came, came_late, own, *rest):
    outs, total = rest[:-1], rest[-1]
    mine = idx[2]
    first = keep.shape[0]
    total[pl.ds(0, first), :] = keep[...].astype(jnp.float32) + came[...].astype(jnp.float32)
    total[pl.ds(first, keep_late.shape[0]), :] = keep_late[...].astype(jnp.float32) + came_late[...].astype(jnp.float32)
    own[...] = total[rows_at(mine * block, block), :]
    for k, out in enumerate(outs, 1):
        out[...] = total[rows_at(lax.rem(mine + k, NY) * block, block), :].astype(jnp.bfloat16)


def activate(width, own, one, two, three, hidden):
    sums = own[...] + one[...].astype(jnp.float32) + two[...].astype(jnp.float32) + three[...].astype(jnp.float32)
    meansq = jnp.sum(sums[:, 2 * width :], axis=1, keepdims=True) / D
    inv = lax.rsqrt(meansq + 1e-05)
    gate = sums[:, :width] * inv
    up = sums[:, width : 2 * width] * inv
    hidden[...] = (gate / (1.0 + jnp.exp(-gate)) * up).astype(jnp.bfloat16)


def second_matmul(first, last, idx, *refs):
    same, refs = refs[:NY], refs[NY:]
    other, refs = refs[:NY], refs[NY:]
    weights, outs, (hidden, terms) = refs[0], refs[1:-2], refs[-2:]
    mine, core = idx[2], idx[3]
    block = same[0].shape[0]
    half = block // 2
    for k in range(NY):
        at = lax.rem(mine - k + NY, NY) * 2 * block
        for i in range(2):
            hidden[rows_at(at + i * block + core * half, half), :] = same[k][pl.ds(i * half, half), :]
            hidden[rows_at(at + i * block + (1 - core) * half, half), :] = other[k][pl.ds(i * half, half), :]

    @pl.loop(0, weights.shape[1] // 256)
    def _(t):
        cols = pl.ds(pl.multiple_of(t * 256, 256), 256)
        some = hidden[pl.ds(first * block, (last - first) * block), :]
        terms[:, cols] = jnp.dot(some, weights[:, cols], preferred_element_type=jnp.float32).astype(jnp.bfloat16)

    at = 0
    for out in outs:
        size = out.shape[0]
        out[...] = terms[pl.ds(at, size), :]
        at += size


def add(came, own, out):
    out[...] = (came[...].astype(jnp.float32) + own[...].astype(jnp.float32)).astype(jnp.bfloat16)


def z_sum(own, one, two, *outs):
    rows = outs[0].shape[0]
    for k, out in enumerate(outs):
        at = pl.ds(k * rows, rows)
        total = own[at, :].astype(jnp.float32) + one[at, :].astype(jnp.float32) + two[at, :].astype(jnp.float32)
        out[...] = total.astype(out.dtype)


def finish(stream, mine, one, two, three, out):
    total = stream[...] + mine[...]
    for ref in (one, two, three):
        total = total + ref[...].astype(jnp.float32)
    out[...] = total.astype(jnp.bfloat16)


def shards(
    hidden_rows,
    queries,
    cache_keys,
    cache_values,
    new_keys,
    new_values,
    lengths,
    norm_gain,
    w_gate,
    w_up,
    w_down,
):
    f32, bf16 = jnp.float32, jnp.bfloat16
    rows, feats = hidden_rows.shape
    width = w_gate.shape[1]
    piece = rows * NX
    total = piece * NZ
    block = total // (NY * NC)
    wide = 2 * width + MARKS
    per = feats // HEAD_DIM
    idx = jnp.stack([lax.axis_index(a) for a in ("x", "z", "y", "core")]).astype(jnp.int32)
    given = [lengths, hidden_rows, queries, cache_keys, cache_values, new_keys, new_values, norm_gain.reshape(per, HEAD_DIM)]
    stream, inv_gain2, scaled = call(
        functools.partial(start_rows, HEAD_DIM ** (-0.5)),
        [shape(rows, feats, kind=f32), shape(per, HEAD_DIM, kind=f32), shape(rows, feats)],
        given,
        "h" * 8,
        scratch=[pltpu.SMEM(lengths.shape, jnp.int32)]
        + [pltpu.VMEM(v.shape, v.dtype) for v in given[1:]]
        + [pltpu.VMEM((rows * per, HEAD_DIM), f32)] * 2
        + [pltpu.VMEM((rows * per, HEAD_DIM), bf16)]
        + [pltpu.SemaphoreType.DMA((8,))],
        moved=4 * cache_keys.size,
        limit=60 * MIB,
    )

    own = call(
        join,
        shape(piece, feats),
        [scaled] + [shift(scaled, "x", k, NX) for k in range(1, NX)],
        "v" * NX,
        moved=4 * piece * feats,
    )
    pieces = {0: own}
    up = down = own
    for step in range(1, NZ // 2):
        up = shift(up, "z", 1, NZ)
        down = shift(down, "z", -1, NZ)
        pieces[-step], pieces[step] = up, down

    some = [pieces[j] for j in ORDER[:EARLY]]
    size = EARLY * piece
    keep, send, part, done = call(
        functools.partial(gate_matmul, width),
        [shape(size // 2, wide)] * 2 + [shape(size, feats), shape(8, 128, kind=f32)],
        [idx] + some + [inv_gain2, w_gate],
        "s" + "v" * (EARLY + 2),
        flops=2 * size * feats * width,
        moved=2 * feats * width,
    )
    up, down = call(halves, [shape(piece // 2, feats)] * 2, [up, down, done], "vvh", moved=4 * piece * feats)
    up = shift(up, "z", 1, NZ)
    down = shift(down, "z", -1, NZ)
    keep, send = call(
        functools.partial(up_matmul, width),
        [shape(size // 2, wide)] * 2,
        [part, w_up, keep, send],
        "vvvv",
        flops=2 * size * feats * width,
        moved=2 * feats * width,
        alias={2: 0, 3: 1},
    )
    came = shift(send, "core", 1, NC)
    some = [pieces[j] for j in ORDER[EARLY:-1]] + [up, down]
    size = (NZ - EARLY) * piece
    keep_late, send_late = call(
        functools.partial(both_matmul, width),
        [shape(size // 2, wide)] * 2,
        [idx] + some + [inv_gain2, w_gate, w_up],
        "s" + "v" * (len(some) + 3),
        scratch=[pltpu.VMEM((size, feats), bf16)],
        flops=4 * size * feats * width,
        moved=4 * feats * width,
    )
    came_late = shift(send_late, "core", 1, NC)
    own, *parts = call(
        functools.partial(core_sum, block),
        [shape(block, wide, kind=f32)] + [shape(block, wide)] * (NY - 1),
        [idx, keep, keep_late, came, came_late],
        "svvvv",
        scratch=[pltpu.VMEM((total // 2, wide), f32)],
        moved=4 * total * wide,
    )
    parts = [shift(v, "y", k, NY) for k, v in enumerate(parts, 1)]
    hidden = call(functools.partial(activate, width), shape(block, width), [own] + parts, "vvvv", moved=10 * block * wide)
    same = [hidden] + [shift(hidden, "y", k, NY) for k in range(1, NY)]
    other = [shift(v, "core", 1, NC) for v in same]

    def expand(first, last):
        got = call(
            functools.partial(second_matmul, first, last),
            [shape(piece // 2, feats)] * (2 * (last - first)),
            [idx] + same + other + [w_down],
            "s" + "v" * (2 * NY + 1),
            scratch=[pltpu.VMEM((total, width), bf16), pltpu.VMEM(((last - first) * piece, feats), bf16)],
            flops=2 * (last - first) * piece * feats * width,
            moved=2 * feats * width,
        )
        return {j: got[2 * i : 2 * i + 2] for i, j in enumerate(ORDER[first:last])}

    terms = {**expand(EARLY, NZ), **expand(0, EARLY)}

    def chain(half, way, steps):
        got = terms[way * steps if steps < NZ // 2 else steps][half]
        for step in range(steps, 1, -1):
            got = shift(got, "z", way, NZ)
            own = terms[way * (step - 1)][half]
            got = call(add, shape(piece // 2, feats), [got, own], "vv", moved=6 * piece * feats // 2)
        return shift(got, "z", way, NZ)

    far = NZ // 2
    low = [chain(0, -1, far), chain(0, 1, far - 1)]
    high = [chain(1, 1, far), chain(1, -1, far - 1)]
    mine, one = call(
        z_sum, [shape(rows, feats, kind=f32), shape(rows, feats)], [terms[0][0]] + low, "vvv", moved=4 * piece * feats
    )
    two, three = call(z_sum, [shape(rows, feats)] * 2, [terms[0][1]] + high, "vvv", moved=4 * piece * feats)
    parts = [shift(v, "x", -k, NX) for k, v in enumerate([one, two, three], 1)]
    return call(finish, shape(rows, feats), [stream, mine] + parts, "v" * 5, moved=20 * rows * feats)


def solution(mesh):
    fine = Mesh(mesh.devices.reshape(NX, NZ, NY, NC), ("x", "z", "y", "core"))
    pool = ("x", "z")
    placed = (
        P(pool, TP),
        P(pool, TP),
        P(pool, None, TP),
        P(pool, None, TP),
        P(pool, TP),
        P(pool, TP),
        P(pool),
        P(TP),
        P(TP, pool),
        P(TP, pool),
        P(pool, TP),
    )
    return jax.shard_map(shards, mesh=fine, in_specs=placed, out_specs=P(pool, TP), check_vma=False)
```

profile of v0, /device:TPU:32, one launch (start us, length us, event | category | flops | bytes accessed | tf_op | source)
XLA Modules:
  0.0 122.2 jit_solution(393663997477096686)
XLA Ops:
  0.0 2.6 %shard_map.109 = (f32[16,2048]{1,0:T(8,128)}, f32[16,128]{1,0:T(8,128)}, bf16[16,2048]{1,0:T(8,128)(2,1)}) custom-call(s32[16]{0:T(128)} %lengths_in.1, bf16[16,2048]{1,0:T(8,128)(2,1)} %hidden_in.1, bf16[16,2048]{1,0:T(8,128)(2,1)} %queries_in.1, bf16[16,128,128]{2,1,0:T(8,128)(2,1)} %keys_in.1, bf16[16,128,128]{2,1,0:T(8,128)(2,1)} %values_in.1, ...), custom_call_target="tpu_custom_call" | custom-call | bytes 1048576 | tf_op jit(solution)/shard_map/pallas_call | solution.py:33
  4.2 2.7 %collective-permute-start.1 = (bf16[16,2048]{1,0:T(8,128)(2,1)}, bf16[16,2048]{1,0:T(8,128)(2,1)S(1)}, u32[]{:S(2)}, u32[]{:S(2)}) collective-permute-start(bf16[16,2048]{1,0:T(8,128)(2,1)} %get-tuple-element.43.refs_0_), channel_id=1, source_target_pairs={{0,128},{64,192},{128,0},{192,64},{1,129},{65,193},{129,1},{193,65... | collective-permute-start | bytes 196616 | tf_op jit(solution)/shard_map/ppermute | solution.py:22
  14.4 4.8 %collective-permute-done.3.refs_1_ = bf16[64,2048]{1,0:T(8,128)(2,1)S(1)} collective-permute-done((bf16[64,2048]{1,0:T(8,128)(2,1)S(1)}, bf16[64,2048]{1,0:T(8,128)(2,1)S(1)}, u32[]{:S(2)}, u32[]{:S(2)}) %collective-permute-start.3) | collective-permute-done | bytes 262176 | tf_op jit(solution)/shard_map/ppermute | solution.py:22
  21.1 2.3 %collective-permute-start.6 = (bf16[64,2048]{1,0:T(8,128)(2,1)S(1)}, bf16[64,2048]{1,0:T(8,128)(2,1)S(1)}, u32[]{:S(2)}, u32[]{:S(2)}) collective-permute-start(bf16[64,2048]{1,0:T(8,128)(2,1)S(1)} %collective-permute-done.4.refs_2_), channel_id=1, source_target_pairs={{0,56},{8,0},{16,8},{24,16},{32,24},{40,32},{48,40},{56,48},{1,57}... | collective-permute-start | bytes 786440 | tf_op jit(solution)/shard_map/ppermute | solution.py:22
  23.4 4.5 %collective-permute-done.5.refs_3_ = bf16[64,2048]{1,0:T(8,128)(2,1)S(1)} collective-permute-done((bf16[64,2048]{1,0:T(8,128)(2,1)S(1)}, bf16[64,2048]{1,0:T(8,128)(2,1)S(1)}, u32[]{:S(2)}, u32[]{:S(2)}) %collective-permute-start.5) | collective-permute-done | bytes 262176 | tf_op jit(solution)/shard_map/ppermute | solution.py:22
  28.5 2.5 %collective-permute-start.8 = (bf16[64,2048]{1,0:T(8,128)(2,1)S(1)}, bf16[64,2048]{1,0:T(8,128)(2,1)S(1)}, u32[]{:S(2)}, u32[]{:S(2)}) collective-permute-start(bf16[64,2048]{1,0:T(8,128)(2,1)S(1)} %collective-permute-done.6.refs_4_), channel_id=1, source_target_pairs={{0,56},{8,0},{16,8},{24,16},{32,24},{40,32},{48,40},{56,48},{1,57}... | collective-permute-start | bytes 786440 | tf_op jit(solution)/shard_map/ppermute | solution.py:22
  33.8 3.0 %shard_map.111 = (bf16[160,1920]{1,0:T(8,128)(2,1)S(1)}, bf16[160,1920]{1,0:T(8,128)(2,1)S(1)}, bf16[320,2048]{1,0:T(8,128)(2,1)S(1)}, f32[8,128]{1,0:T(8,128)S(1)}) custom-call(s32[4]{0:T(128)S(1)} %pad_add_fusion.idx, bf16[64,2048]{1,0:T(8,128)(2,1)S(1)} %shard_map.110.refs_0_, bf16[64,2048]{1,0:T(8,128)(2,1)S(1)} %collective-permute-done.3.refs_1_, ...), custom_call_target="tpu_custom_call" | custom-call | flops 1174405120 | bytes 3670016 | tf_op jit(solution)/shard_map/pallas_call | solution.py:33
  37.0 2.5 %collective-permute-start.9 = (bf16[32,2048]{1,0:T(8,128)(2,1)S(1)}, bf16[32,2048]{1,0:T(8,128)(2,1)S(1)}, u32[]{:S(2)}, u32[]{:S(2)}) collective-permute-start(bf16[32,2048]{1,0:T(8,128)(2,1)S(1)} %get-tuple-element.50), channel_id=1, source_target_pairs={{0,8},{8,16},{16,24},{24,32},{32,40},{40,48},{48,56},{56,0},{1,9},... | collective-permute-start | bytes 393224 | tf_op jit(solution)/shard_map/ppermute | solution.py:22
  43.2 2.4 %collective-permute-done.10.refs_3_ = bf16[32,2048]{1,0:T(8,128)(2,1)S(1)} collective-permute-done((bf16[32,2048]{1,0:T(8,128)(2,1)S(1)}, bf16[32,2048]{1,0:T(8,128)(2,1)S(1)}, u32[]{:S(2)}, u32[]{:S(2)}) %collective-permute-start.10) | collective-permute-done | bytes 131104 | tf_op jit(solution)/shard_map/ppermute | solution.py:22
  45.6 3.9 %shard_map.114 = (bf16[96,1920]{1,0:T(8,128)(2,1)S(1)}, bf16[96,1920]{1,0:T(8,128)(2,1)S(1)}) custom-call(s32[4]{0:T(128)S(1)} %pad_add_fusion.idx, bf16[64,2048]{1,0:T(8,128)(2,1)S(1)} %collective-permute-done.7.up.refs_0_, bf16[64,2048]{1,0:T(8,128)(2,1)S(1)} %collective-permute-done.8.down.refs_1_, bf16[32,2048]{1,0:T(8,128)(2,1)S(1)} %collective-permute-done.9.refs_2_, ...), custom_call_target="tpu_custom_call" | custom-call | flops 1409286144 | bytes 7340032 | tf_op jit(solution)/shard_map/pallas_call | solution.py:33
  54.0 2.9 %collective-permute-start.14 = (bf16[64,1920]{1,0:T(8,128)(2,1)S(1)}, bf16[64,1920]{1,0:T(8,128)(2,1)S(1)}, u32[]{:S(2)}, u32[]{:S(2)}) collective-permute-start(bf16[64,1920]{1,0:T(8,128)(2,1)S(1)} %get-tuple-element.57), channel_id=1, source_target_pairs={{0,4},{2,6},{4,0},{6,2},{1,5},{3,7},{5,1},{7,3},{8,12},{10,14},{12... | collective-permute-start | bytes 737288 | tf_op jit(solution)/shard_map/ppermute | solution.py:22
  58.2 3.4 %collective-permute-done.13.one = bf16[64,1920]{1,0:T(8,128)(2,1)S(1)} collective-permute-done((bf16[64,1920]{1,0:T(8,128)(2,1)S(1)}, bf16[64,1920]{1,0:T(8,128)(2,1)S(1)}, u32[]{:S(2)}, u32[]{:S(2)}) %collective-permute-start.13) | collective-permute-done | bytes 245792 | tf_op jit(solution)/shard_map/ppermute | solution.py:22
  61.6 6.4 %collective-permute-done.14.two = bf16[64,1920]{1,0:T(8,128)(2,1)S(1)} collective-permute-done((bf16[64,1920]{1,0:T(8,128)(2,1)S(1)}, bf16[64,1920]{1,0:T(8,128)(2,1)S(1)}, u32[]{:S(2)}, u32[]{:S(2)}) %collective-permute-start.14) | collective-permute-done | bytes 245792 | tf_op jit(solution)/shard_map/ppermute | solution.py:22
  69.6 2.4 %collective-permute-start.17 = (bf16[64,896]{1,0:T(8,128)(2,1)S(1)}, bf16[64,896]{1,0:T(8,128)(2,1)S(1)}, u32[]{:S(2)}, u32[]{:S(2)}) collective-permute-start(bf16[64,896]{1,0:T(8,128)(2,1)S(1)} %shard_map.116.refs_0_), channel_id=1, source_target_pairs={{0,4},{2,6},{4,0},{6,2},{1,5},{3,7},{5,1},{7,3},{8,12},{10,14},{12... | collective-permute-start | bytes 344072 | tf_op jit(solution)/shard_map/ppermute | solution.py:22
  74.7 2.9 %collective-permute-done.17.refs_2_ = bf16[64,896]{1,0:T(8,128)(2,1)S(1)} collective-permute-done((bf16[64,896]{1,0:T(8,128)(2,1)S(1)}, bf16[64,896]{1,0:T(8,128)(2,1)S(1)}, u32[]{:S(2)}, u32[]{:S(2)}) %collective-permute-start.17) | collective-permute-done | bytes 114720 | tf_op jit(solution)/shard_map/ppermute | solution.py:22
  79.1 2.9 %shard_map.118 = (bf16[32,2048]{1,0:T(8,128)(2,1)S(1)}, bf16[32,2048]{1,0:T(8,128)(2,1)S(1)}, bf16[32,2048]{1,0:T(8,128)(2,1)S(1)}, bf16[32,2048]{1,0:T(8,128)(2...) custom-call(s32[4]{0:T(128)S(1)} %pad_add_fusion.idx, bf16[64,896]{1,0:T(8,128)(2,1)S(1)} %shard_map.116.refs_0_, ...), custom_call_target="tpu_custom_call" | custom-call | flops 704643072 | bytes 3670016 | tf_op jit(solution)/shard_map/pallas_call | solution.py:33
  84.1 2.8 %collective-permute-start.27 = (bf16[32,2048]{1,0:T(8,128)(2,1)S(1)}, bf16[32,2048]{1,0:T(8,128)(2,1)S(1)}, u32[]{:S(2)}, u32[]{:S(2)}) collective-permute-start(bf16[32,2048]{1,0:T(8,128)(2,1)S(1)} %get-tuple-element.64), channel_id=1, source_target_pairs={{0,8},{8,16},{16,24},{24,32},{32,40},{40,48},{48,56},{56,0},{1,9},... | collective-permute-start | bytes 393224 | tf_op jit(solution)/shard_map/ppermute | solution.py:22
  89.7 3.7 %collective-permute-start.35 = (bf16[32,2048]{1,0:T(8,128)(2,1)S(1)}, bf16[32,2048]{1,0:T(8,128)(2,1)S(1)}, u32[]{:S(2)}, u32[]{:S(2)}) collective-permute-start(bf16[32,2048]{1,0:T(8,128)(2,1)S(1)} %get-tuple-element.74), channel_id=1, source_target_pairs={{0,56},{8,0},{16,8},{24,16},{32,24},{40,32},{48,40},{56,48},{1,57}... | collective-permute-start | bytes 393224 | tf_op jit(solution)/shard_map/ppermute | solution.py:22
  93.5 3.5 %shard_map.117 = (bf16[32,2048]{1,0:T(8,128)(2,1)S(1)}, bf16[32,2048]{1,0:T(8,128)(2,1)S(1)}, bf16[32,2048]{1,0:T(8,128)(2,1)S(1)}, bf16[32,2048]{1,0:T(8,128)(2...) custom-call(s32[4]{0:T(128)S(1)} %pad_add_fusion.idx, ...), custom_call_target="tpu_custom_call" | custom-call | flops 1174405120 | bytes 3670016 | tf_op jit(solution)/shard_map/pallas_call | solution.py:33
  99.3 3.3 %collective-permute-start.36 = (bf16[32,2048]{1,0:T(8,128)(2,1)S(1)}, bf16[32,2048]{1,0:T(8,128)(2,1)S(1)}, u32[]{:S(2)}, u32[]{:S(2)}) collective-permute-start(bf16[32,2048]{1,0:T(8,128)(2,1)S(1)} %shard_map.128), channel_id=1, source_target_pairs={{0,56},{8,0},{16,8},{24,16},{32,24},{40,32},{48,40},{56,48},{1,57}... | collective-permute-start | bytes 393224 | tf_op jit(solution)/shard_map/ppermute | solution.py:22
  102.8 2.2 %collective-permute-start.29 = (bf16[32,2048]{1,0:T(8,128)(2,1)S(1)}, bf16[32,2048]{1,0:T(8,128)(2,1)S(1)}, u32[]{:S(2)}, u32[]{:S(2)}) collective-permute-start(bf16[32,2048]{1,0:T(8,128)(2,1)S(1)} %shard_map.123), channel_id=1, source_target_pairs={{0,8},{8,16},{16,24},{24,32},{32,40},{40,48},{48,56},{56,0},{1,9},... | collective-permute-start | bytes 393224 | tf_op jit(solution)/shard_map/ppermute | solution.py:22
  107.4 2.1 %collective-permute-start.37 = (bf16[32,2048]{1,0:T(8,128)(2,1)S(1)}, bf16[32,2048]{1,0:T(8,128)(2,1)S(1)}, u32[]{:S(2)}, u32[]{:S(2)}) collective-permute-start(bf16[32,2048]{1,0:T(8,128)(2,1)S(1)} %shard_map.129), channel_id=1, source_target_pairs={{0,56},{8,0},{16,8},{24,16},{32,24},{40,32},{48,40},{56,48},{1,57}... | collective-permute-start | bytes 393224 | tf_op jit(solution)/shard_map/ppermute | solution.py:22
  110.7 2.5 %collective-permute-start.30 = (bf16[16,2048]{1,0:T(8,128)(2,1)S(1)}, bf16[16,2048]{1,0:T(8,128)(2,1)S(1)}, u32[]{:S(2)}, u32[]{:S(2)}) collective-permute-start(bf16[16,2048]{1,0:T(8,128)(2,1)S(1)} %get-tuple-element.68), channel_id=1, source_target_pairs={{0,192},{64,0},{128,64},{192,128},{1,193},{65,1},{129,65},{193,129... | collective-permute-start | bytes 196616 | tf_op jit(solution)/shard_map/ppermute | solution.py:22
  118.0 2.5 %collective-permute-done.38.two = bf16[16,2048]{1,0:T(8,128)(2,1)S(1)} collective-permute-done((bf16[16,2048]{1,0:T(8,128)(2,1)S(1)}, bf16[16,2048]{1,0:T(8,128)(2,1)S(1)}, u32[]{:S(2)}, u32[]{:S(2)}) %collective-permute-start.38) | collective-permute-done | bytes 65568 | tf_op jit(solution)/shard_map/ppermute | solution.py:22
  (96 shorter events, 47.1 us)
Async XLA Ops:
  2.6 6.4 %collective-permute-start = (bf16[16,2048]{1,0:T(8,128)(2,1)}, bf16[16,2048]{1,0:T(8,128)(2,1)S(1)}, u32[]{:S(2)}, u32[]{:S(2)}) collective-permute-start(bf16[16,2048]{1,0:T(8,128)(2,1)} %get-tuple-element.43.refs_0_), channel_id=1, source_target_pairs={{0,64},{64,128},{128,192},{192,0},{1,65},{65,129},{129,193},{193,1... | collective-permute-start | bytes 196616 | tf_op jit(solution)/shard_map/ppermute | solution.py:22
  12.3 7.0 %collective-permute-start.3 = (bf16[64,2048]{1,0:T(8,128)(2,1)S(1)}, bf16[64,2048]{1,0:T(8,128)(2,1)S(1)}, u32[]{:S(2)}, u32[]{:S(2)}) collective-permute-start(bf16[64,2048]{1,0:T(8,128)(2,1)S(1)} %shard_map.110.refs_0_), channel_id=1, source_target_pairs={{0,8},{8,16},{16,24},{24,32},{32,40},{40,48},{48,56},{56,0},{1,9},... | collective-permute-start | bytes 786440 | tf_op jit(solution)/shard_map/ppermute | solution.py:22
  14.3 6.9 %collective-permute-start.4 = (bf16[64,2048]{1,0:T(8,128)(2,1)S(1)}, bf16[64,2048]{1,0:T(8,128)(2,1)S(1)}, u32[]{:S(2)}, u32[]{:S(2)}) collective-permute-start(bf16[64,2048]{1,0:T(8,128)(2,1)S(1)} %shard_map.110.refs_0_), channel_id=1, source_target_pairs={{0,56},{8,0},{16,8},{24,16},{32,24},{40,32},{48,40},{56,48},{1,57}... | collective-permute-start | bytes 786440 | tf_op jit(solution)/shard_map/ppermute | solution.py:22
  19.2 8.7 %collective-permute-start.5 = (bf16[64,2048]{1,0:T(8,128)(2,1)S(1)}, bf16[64,2048]{1,0:T(8,128)(2,1)S(1)}, u32[]{:S(2)}, u32[]{:S(2)}) collective-permute-start(bf16[64,2048]{1,0:T(8,128)(2,1)S(1)} %collective-permute-done.3.refs_1_), channel_id=1, source_target_pairs={{0,8},{8,16},{16,24},{24,32},{32,40},{40,48},{48,56},{56,0},{1,9},... | collective-permute-start | bytes 786440 | tf_op jit(solution)/shard_map/ppermute | solution.py:22
  21.1 7.4 %collective-permute-start.6 = (bf16[64,2048]{1,0:T(8,128)(2,1)S(1)}, bf16[64,2048]{1,0:T(8,128)(2,1)S(1)}, u32[]{:S(2)}, u32[]{:S(2)}) collective-permute-start(bf16[64,2048]{1,0:T(8,128)(2,1)S(1)} %collective-permute-done.4.refs_2_), channel_id=1, source_target_pairs={{0,56},{8,0},{16,8},{24,16},{32,24},{40,32},{48,40},{56,48},{1,57}... | collective-permute-start | bytes 786440 | tf_op jit(solution)/shard_map/ppermute | solution.py:22
  27.9 9.0 %collective-permute-start.7 = (bf16[64,2048]{1,0:T(8,128)(2,1)S(1)}, bf16[64,2048]{1,0:T(8,128)(2,1)S(1)}, u32[]{:S(2)}, u32[]{:S(2)}) collective-permute-start(bf16[64,2048]{1,0:T(8,128)(2,1)S(1)} %collective-permute-done.5.refs_3_), channel_id=1, source_target_pairs={{0,8},{8,16},{16,24},{24,32},{32,40},{40,48},{48,56},{56,0},{1,9},... | collective-permute-start | bytes 786440 | tf_op jit(solution)/shard_map/ppermute | solution.py:22
  28.5 8.4 %collective-permute-start.8 = (bf16[64,2048]{1,0:T(8,128)(2,1)S(1)}, bf16[64,2048]{1,0:T(8,128)(2,1)S(1)}, u32[]{:S(2)}, u32[]{:S(2)}) collective-permute-start(bf16[64,2048]{1,0:T(8,128)(2,1)S(1)} %collective-permute-done.6.refs_4_), channel_id=1, source_target_pairs={{0,56},{8,0},{16,8},{24,16},{32,24},{40,32},{48,40},{56,48},{1,57}... | collective-permute-start | bytes 786440 | tf_op jit(solution)/shard_map/ppermute | solution.py:22
  37.0 6.3 %collective-permute-start.9 = (bf16[32,2048]{1,0:T(8,128)(2,1)S(1)}, bf16[32,2048]{1,0:T(8,128)(2,1)S(1)}, u32[]{:S(2)}, u32[]{:S(2)}) collective-permute-start(bf16[32,2048]{1,0:T(8,128)(2,1)S(1)} %get-tuple-element.50), channel_id=1, source_target_pairs={{0,8},{8,16},{16,24},{24,32},{32,40},{40,48},{48,56},{56,0},{1,9},... | collective-permute-start | bytes 393224 | tf_op jit(solution)/shard_map/ppermute | solution.py:22
  42.4 7.2 %collective-permute-start.11 = (bf16[160,1920]{1,0:T(8,128)(2,1)S(1)}, bf16[160,1920]{1,0:T(8,128)(2,1)S(1)}, u32[]{:S(2)}, u32[]{:S(2)}) collective-permute-start(bf16[160,1920]{1,0:T(8,128)(2,1)S(1)} %get-tuple-element.53), channel_id=1, source_target_pairs={{0,1},{1,0},{2,3},{3,2},{4,5},{5,4},{6,7},{7,6},{8,9},{9,8},{10,11... | collective-permute-start | bytes 1843208 | tf_op jit(solution)/shard_map/ppermute | solution.py:22
  52.3 9.4 %collective-permute-start.13 = (bf16[64,1920]{1,0:T(8,128)(2,1)S(1)}, bf16[64,1920]{1,0:T(8,128)(2,1)S(1)}, u32[]{:S(2)}, u32[]{:S(2)}) collective-permute-start(bf16[64,1920]{1,0:T(8,128)(2,1)S(1)} %get-tuple-element.56), channel_id=1, source_target_pairs={{0,2},{2,4},{4,6},{6,0},{1,3},{3,5},{5,7},{7,1},{8,10},{10,12},{12... | collective-permute-start | bytes 737288 | tf_op jit(solution)/shard_map/ppermute | solution.py:22
  54.0 14.1 %collective-permute-start.14 = (bf16[64,1920]{1,0:T(8,128)(2,1)S(1)}, bf16[64,1920]{1,0:T(8,128)(2,1)S(1)}, u32[]{:S(2)}, u32[]{:S(2)}) collective-permute-start(bf16[64,1920]{1,0:T(8,128)(2,1)S(1)} %get-tuple-element.57), channel_id=1, source_target_pairs={{0,4},{2,6},{4,0},{6,2},{1,5},{3,7},{5,1},{7,3},{8,12},{10,14},{12... | collective-permute-start | bytes 737288 | tf_op jit(solution)/shard_map/ppermute | solution.py:22
  56.9 11.2 %collective-permute-start.15 = (bf16[64,1920]{1,0:T(8,128)(2,1)S(1)}, bf16[64,1920]{1,0:T(8,128)(2,1)S(1)}, u32[]{:S(2)}, u32[]{:S(2)}) collective-permute-start(bf16[64,1920]{1,0:T(8,128)(2,1)S(1)} %get-tuple-element.58), channel_id=1, source_target_pairs={{0,6},{2,0},{4,2},{6,4},{1,7},{3,1},{5,3},{7,5},{8,14},{10,8},{12,... | collective-permute-start | bytes 737288 | tf_op jit(solution)/shard_map/ppermute | solution.py:22
  68.3 6.3 %collective-permute-start.16 = (bf16[64,896]{1,0:T(8,128)(2,1)S(1)}, bf16[64,896]{1,0:T(8,128)(2,1)S(1)}, u32[]{:S(2)}, u32[]{:S(2)}) collective-permute-start(bf16[64,896]{1,0:T(8,128)(2,1)S(1)} %shard_map.116.refs_0_), channel_id=1, source_target_pairs={{0,2},{2,4},{4,6},{6,0},{1,3},{3,5},{5,7},{7,1},{8,10},{10,12},{12... | collective-permute-start | bytes 344072 | tf_op jit(solution)/shard_map/ppermute | solution.py:22
  69.6 7.9 %collective-permute-start.17 = (bf16[64,896]{1,0:T(8,128)(2,1)S(1)}, bf16[64,896]{1,0:T(8,128)(2,1)S(1)}, u32[]{:S(2)}, u32[]{:S(2)}) collective-permute-start(bf16[64,896]{1,0:T(8,128)(2,1)S(1)} %shard_map.116.refs_0_), channel_id=1, source_target_pairs={{0,4},{2,6},{4,0},{6,2},{1,5},{3,7},{5,1},{7,3},{8,12},{10,14},{12... | collective-permute-start | bytes 344072 | tf_op jit(solution)/shard_map/ppermute | solution.py:22
  82.9 10.5 %collective-permute-start.31 = (bf16[32,2048]{1,0:T(8,128)(2,1)S(1)}, bf16[32,2048]{1,0:T(8,128)(2,1)S(1)}, u32[]{:S(2)}, u32[]{:S(2)}) collective-permute-start(bf16[32,2048]{1,0:T(8,128)(2,1)S(1)} %get-tuple-element.70), channel_id=1, source_target_pairs={{0,8},{8,16},{16,24},{24,32},{32,40},{40,48},{48,56},{56,0},{1,9},... | collective-permute-start | bytes 393224 | tf_op jit(solution)/shard_map/ppermute | solution.py:22
  84.1 12.9 %collective-permute-start.27 = (bf16[32,2048]{1,0:T(8,128)(2,1)S(1)}, bf16[32,2048]{1,0:T(8,128)(2,1)S(1)}, u32[]{:S(2)}, u32[]{:S(2)}) collective-permute-start(bf16[32,2048]{1,0:T(8,128)(2,1)S(1)} %get-tuple-element.64), channel_id=1, source_target_pairs={{0,8},{8,16},{16,24},{24,32},{32,40},{40,48},{48,56},{56,0},{1,9},... | collective-permute-start | bytes 393224 | tf_op jit(solution)/shard_map/ppermute | solution.py:22
  88.0 9.9 %collective-permute-start.24 = (bf16[32,2048]{1,0:T(8,128)(2,1)S(1)}, bf16[32,2048]{1,0:T(8,128)(2,1)S(1)}, u32[]{:S(2)}, u32[]{:S(2)}) collective-permute-start(bf16[32,2048]{1,0:T(8,128)(2,1)S(1)} %shard_map.119), channel_id=1, source_target_pairs={{0,56},{8,0},{16,8},{24,16},{32,24},{40,32},{48,40},{56,48},{1,57}... | collective-permute-start | bytes 393224 | tf_op jit(solution)/shard_map/ppermute | solution.py:22
  89.7 9.6 %collective-permute-start.35 = (bf16[32,2048]{1,0:T(8,128)(2,1)S(1)}, bf16[32,2048]{1,0:T(8,128)(2,1)S(1)}, u32[]{:S(2)}, u32[]{:S(2)}) collective-permute-start(bf16[32,2048]{1,0:T(8,128)(2,1)S(1)} %get-tuple-element.74), channel_id=1, source_target_pairs={{0,56},{8,0},{16,8},{24,16},{32,24},{40,32},{48,40},{56,48},{1,57}... | collective-permute-start | bytes 393224 | tf_op jit(solution)/shard_map/ppermute | solution.py:22
  93.4 9.2 %collective-permute-start.32 = (bf16[32,2048]{1,0:T(8,128)(2,1)S(1)}, bf16[32,2048]{1,0:T(8,128)(2,1)S(1)}, u32[]{:S(2)}, u32[]{:S(2)}) collective-permute-start(bf16[32,2048]{1,0:T(8,128)(2,1)S(1)} %shard_map.125), channel_id=1, source_target_pairs={{0,8},{8,16},{16,24},{24,32},{32,40},{40,48},{48,56},{56,0},{1,9},... | collective-permute-start | bytes 393224 | tf_op jit(solution)/shard_map/ppermute | solution.py:22
  98.0 7.0 %collective-permute-start.25 = (bf16[32,2048]{1,0:T(8,128)(2,1)S(1)}, bf16[32,2048]{1,0:T(8,128)(2,1)S(1)}, u32[]{:S(2)}, u32[]{:S(2)}) collective-permute-start(bf16[32,2048]{1,0:T(8,128)(2,1)S(1)} %shard_map.120), channel_id=1, source_target_pairs={{0,56},{8,0},{16,8},{24,16},{32,24},{40,32},{48,40},{56,48},{1,57}... | collective-permute-start | bytes 393224 | tf_op jit(solution)/shard_map/ppermute | solution.py:22
  99.3 8.0 %collective-permute-start.36 = (bf16[32,2048]{1,0:T(8,128)(2,1)S(1)}, bf16[32,2048]{1,0:T(8,128)(2,1)S(1)}, u32[]{:S(2)}, u32[]{:S(2)}) collective-permute-start(bf16[32,2048]{1,0:T(8,128)(2,1)S(1)} %shard_map.128), channel_id=1, source_target_pairs={{0,56},{8,0},{16,8},{24,16},{32,24},{40,32},{48,40},{56,48},{1,57}... | collective-permute-start | bytes 393224 | tf_op jit(solution)/shard_map/ppermute | solution.py:22
  102.7 6.9 %collective-permute-start.33 = (bf16[32,2048]{1,0:T(8,128)(2,1)S(1)}, bf16[32,2048]{1,0:T(8,128)(2,1)S(1)}, u32[]{:S(2)}, u32[]{:S(2)}) collective-permute-start(bf16[32,2048]{1,0:T(8,128)(2,1)S(1)} %shard_map.126), channel_id=1, source_target_pairs={{0,8},{8,16},{16,24},{24,32},{32,40},{40,48},{48,56},{56,0},{1,9},... | collective-permute-start | bytes 393224 | tf_op jit(solution)/shard_map/ppermute | solution.py:22
  102.8 6.9 %collective-permute-start.29 = (bf16[32,2048]{1,0:T(8,128)(2,1)S(1)}, bf16[32,2048]{1,0:T(8,128)(2,1)S(1)}, u32[]{:S(2)}, u32[]{:S(2)}) collective-permute-start(bf16[32,2048]{1,0:T(8,128)(2,1)S(1)} %shard_map.123), channel_id=1, source_target_pairs={{0,8},{8,16},{16,24},{24,32},{32,40},{40,48},{48,56},{56,0},{1,9},... | collective-permute-start | bytes 393224 | tf_op jit(solution)/shard_map/ppermute | solution.py:22
  110.7 7.3 %collective-permute-start.30 = (bf16[16,2048]{1,0:T(8,128)(2,1)S(1)}, bf16[16,2048]{1,0:T(8,128)(2,1)S(1)}, u32[]{:S(2)}, u32[]{:S(2)}) collective-permute-start(bf16[16,2048]{1,0:T(8,128)(2,1)S(1)} %get-tuple-element.68), channel_id=1, source_target_pairs={{0,192},{64,0},{128,64},{192,128},{1,193},{65,1},{129,65},{193,129... | collective-permute-start | bytes 196616 | tf_op jit(solution)/shard_map/ppermute | solution.py:22
  (24 other events, 163.3 us)
where the time goes:
time: 124 us; the launch traced here: 122 us
  starting transfers between devices  57.1 us (46%)
  waiting for transfers between devices  40.8 us (33%)
  Pallas kernels  20.3 us (16%)
  local copies, waits for them, and re-layouts  3.6 us (3%)
    ppermute x40, starting transfers between devices, shift(): return lax.ppermute(v, axis, [(i, (i + by) % n) for i in range(n)])  57.1 us
    ppermute x40, waiting for transfers between devices, shift(): return lax.ppermute(v, axis, [(i, (i + by) % n) for i in range(n)])  40.8 us
    pallas_call x23, Pallas kernels, call(): pl.pallas_call(kernel, out_shape=whole, in_specs=[pl.BlockSpec(memory_spa...  20.3 us
    unnamed x16, local copies, waits for them, and re-layouts  3.6 us
  transfers between devices with their start and end apart: 40, of which 22 were waited for; matrix products, arithmetic and copies ran while one was open for 0% of the time, Pallas kernels for 11%

commit v1 on v0

--- a/solution.py
+++ b/solution.py
@@ -15,7 +15,9 @@
 MARKS = 128
 MIB = 1 << 20
 ORDER = (0, -1, 1, -2, 2, -3, 3, 4)
-EARLY = 5
+EARLY = 4
+FAR = 5
+AWAY = (2, 1, 3)
 
 
 def shift(v, axis, by, n):
@@ -120,10 +122,14 @@
         out[:, cols] = (got * scales[h : h + 1, :]).astype(bf16)
 
 
-def join(*refs):
+def seat(own, out):
+    out[pl.ds(0, own.shape[0]), :] = own[...]
+
+
+def join(first, *refs):
     parts, out = refs[:-1], refs[-1]
     size = parts[0].shape[0]
-    for k, part in enumerate(parts):
+    for k, part in enumerate(parts, 1):
         out[pl.ds(k * size, size), :] = part[...]
 
 
@@ -174,22 +180,14 @@
 
 
 def gate_matmul(width, idx, *refs):
-    pieces, (inv_gain2, w_gate, keep, send, part, done) = refs[:-6], refs[-6:]
+    pieces, (_, inv_gain2, w_gate, keep, send, part, done) = refs[:-7], refs[-7:]
     place(idx[3], pieces, part)
     squares(width, part, inv_gain2, keep, send)
     project(w_gate, 0, part, keep, send)
     done[...] = jnp.zeros_like(done)
 
 
-def up_matmul(width, part, w_up, keep_in, send_in, keep, send):
-    project(w_up, width, part, keep, send)
-
-
-def both_matmul(width, idx, *refs):
-    pieces, (inv_gain2, w_gate, w_up, keep, send, part) = refs[:-6], refs[-6:]
-    place(idx[3], pieces, part)
-    squares(width, part, inv_gain2, keep, send)
-    project(w_gate, 0, part, keep, send)
+def up_matmul(width, _, part, w_up, keep_in, send_in, keep, send):
     project(w_up, width, part, keep, send)
 
 
@@ -199,24 +197,29 @@
     down_half[...] = down[pl.ds(size, size), :]
 
 
-def core_sum(block, idx, keep, keep_late, came, came_late, own, *rest):
-    outs, total = rest[:-1], rest[-1]
+def core_sum(block, idx, keep, came, own, *outs):
     mine = idx[2]
-    first = keep.shape[0]
-    total[pl.ds(0, first), :] = keep[...].astype(jnp.float32) + came[...].astype(jnp.float32)
-    total[pl.ds(first, keep_late.shape[0]), :] = keep_late[...].astype(jnp.float32) + came_late[...].astype(jnp.float32)
-    own[...] = total[rows_at(mine * block, block), :]
+
+    def summed(y):
+        at = rows_at(y * block, block)
+        return keep[at, :].astype(jnp.float32) + came[at, :].astype(jnp.float32)
+
+    own[...] = summed(mine)
     for k, out in enumerate(outs, 1):
-        out[...] = total[rows_at(lax.rem(mine + k, NY) * block, block), :].astype(jnp.bfloat16)
-
-
-def activate(width, own, one, two, three, hidden):
-    sums = own[...] + one[...].astype(jnp.float32) + two[...].astype(jnp.float32) + three[...].astype(jnp.float32)
-    meansq = jnp.sum(sums[:, 2 * width :], axis=1, keepdims=True) / D
-    inv = lax.rsqrt(meansq + 1e-05)
-    gate = sums[:, :width] * inv
-    up = sums[:, width : 2 * width] * inv
-    hidden[...] = (gate / (1.0 + jnp.exp(-gate)) * up).astype(jnp.bfloat16)
+        out[...] = summed(lax.rem(mine + k, NY)).astype(jnp.bfloat16)
+
+
+def activate(width, *refs):
+    parts, hidden = refs[:-1], refs[-1]
+    block = parts[0].shape[0]
+    for i in range(2):
+        own, one, two, three = parts[i * NY : (i + 1) * NY]
+        sums = own[...] + one[...].astype(jnp.float32) + two[...].astype(jnp.float32) + three[...].astype(jnp.float32)
+        meansq = jnp.sum(sums[:, 2 * width :], axis=1, keepdims=True) / D
+        inv = lax.rsqrt(meansq + 1e-05)
+        gate = sums[:, :width] * inv
+        up = sums[:, width : 2 * width] * inv
+        hidden[pl.ds(i * block, block), :] = (gate / (1.0 + jnp.exp(-gate)) * up).astype(jnp.bfloat16)
 
 
 def second_matmul(first, last, idx, *refs):
@@ -227,10 +230,11 @@
     block = same[0].shape[0]
     half = block // 2
     for k in range(NY):
-        at = lax.rem(mine - k + NY, NY) * 2 * block
+        y = lax.rem(mine - k + NY, NY)
         for i in range(2):
-            hidden[rows_at(at + i * block + core * half, half), :] = same[k][pl.ds(i * half, half), :]
-            hidden[rows_at(at + i * block + (1 - core) * half, half), :] = other[k][pl.ds(i * half, half), :]
+            at = (i * NY + y) * block
+            hidden[rows_at(at + core * half, half), :] = same[k][pl.ds(i * half, half), :]
+            hidden[rows_at(at + (1 - core) * half, half), :] = other[k][pl.ds(i * half, half), :]
 
     @pl.loop(0, weights.shape[1] // 256)
     def _(t):
@@ -245,7 +249,8 @@
         at += size
 
 
-def add(came, own, out):
+def add(came, own, *refs):
+    out = refs[-1]
     out[...] = (came[...].astype(jnp.float32) + own[...].astype(jnp.float32)).astype(jnp.bfloat16)
 
 
@@ -301,12 +306,15 @@
         limit=60 * MIB,
     )
 
+    own = call(seat, shape(piece, feats), [scaled], "v", moved=2 * rows * feats)
+    from_x = {k: shift(scaled, "x", k, NX) for k in AWAY}
     own = call(
         join,
         shape(piece, feats),
-        [scaled] + [shift(scaled, "x", k, NX) for k in range(1, NX)],
+        [own] + [from_x[k] for k in range(1, NX)],
         "v" * NX,
         moved=4 * piece * feats,
+        alias={0: 0},
     )
     pieces = {0: own}
     up = down = own
@@ -315,53 +323,54 @@
         down = shift(down, "z", -1, NZ)
         pieces[-step], pieces[step] = up, down
 
-    some = [pieces[j] for j in ORDER[:EARLY]]
-    size = EARLY * piece
-    keep, send, part, done = call(
-        functools.partial(gate_matmul, width),
-        [shape(size // 2, wide)] * 2 + [shape(size, feats), shape(8, 128, kind=f32)],
-        [idx] + some + [inv_gain2, w_gate],
-        "s" + "v" * (EARLY + 2),
-        flops=2 * size * feats * width,
-        moved=2 * feats * width,
-    )
+    def gates(some, after):
+        size = sum(v.shape[0] for v in some)
+        return call(
+            functools.partial(gate_matmul, width),
+            [shape(size // 2, wide)] * 2 + [shape(size, feats), shape(8, 128, kind=f32)],
+            [idx] + some + [after, inv_gain2, w_gate],
+            "s" + "v" * len(some) + "hvv",
+            flops=2 * size * feats * width,
+            moved=2 * feats * width,
+        )
+
+    def ups(keep, send, part, after):
+        return call(
+            functools.partial(up_matmul, width),
+            [shape(*keep.shape)] * 2,
+            [after, part, w_up, keep, send],
+            "hvvvv",
+            flops=2 * part.size * width,
+            moved=2 * feats * width,
+            alias={3: 0, 4: 1},
+        )
+
+    keep, send, part, done = gates([pieces[j] for j in ORDER[:EARLY]], pieces[2])
     up, down = call(halves, [shape(piece // 2, feats)] * 2, [up, down, done], "vvh", moved=4 * piece * feats)
+    keep, send = ups(keep, send, part, up)
     up = shift(up, "z", 1, NZ)
     down = shift(down, "z", -1, NZ)
-    keep, send = call(
-        functools.partial(up_matmul, width),
-        [shape(size // 2, wide)] * 2,
-        [part, w_up, keep, send],
-        "vvvv",
-        flops=2 * size * feats * width,
-        moved=2 * feats * width,
-        alias={2: 0, 3: 1},
-    )
-    came = shift(send, "core", 1, NC)
-    some = [pieces[j] for j in ORDER[EARLY:-1]] + [up, down]
-    size = (NZ - EARLY) * piece
-    keep_late, send_late = call(
-        functools.partial(both_matmul, width),
-        [shape(size // 2, wide)] * 2,
-        [idx] + some + [inv_gain2, w_gate, w_up],
-        "s" + "v" * (len(some) + 3),
-        scratch=[pltpu.VMEM((size, feats), bf16)],
-        flops=4 * size * feats * width,
-        moved=4 * feats * width,
-    )
-    came_late = shift(send_late, "core", 1, NC)
-    own, *parts = call(
-        functools.partial(core_sum, block),
-        [shape(block, wide, kind=f32)] + [shape(block, wide)] * (NY - 1),
-        [idx, keep, keep_late, came, came_late],
-        "svvvv",
-        scratch=[pltpu.VMEM((total // 2, wide), f32)],
-        moved=4 * total * wide,
-    )
-    parts = [shift(v, "y", k, NY) for k, v in enumerate(parts, 1)]
-    hidden = call(functools.partial(activate, width), shape(block, width), [own] + parts, "vvvv", moved=10 * block * wide)
-    same = [hidden] + [shift(hidden, "y", k, NY) for k in range(1, NY)]
-    other = [shift(v, "core", 1, NC) for v in same]
+
+    def across(keep, send):
+        came = shift(send, "core", 1, NC)
+        own, *parts = call(
+            functools.partial(core_sum, block // 2),
+            [shape(block // 2, wide, kind=f32)] + [shape(block // 2, wide)] * (NY - 1),
+            [idx, keep, came],
+            "svv",
+            moved=2 * total * wide,
+        )
+        got = {k: shift(parts[k - 1], "y", k, NY) for k in AWAY}
+        return [own] + [got[k] for k in range(1, NY)]
+
+    early = across(keep, send)
+    keep, send, part, _ = gates([pieces[j] for j in ORDER[EARLY:-1]] + [up, down], early[0])
+    keep, send = ups(keep, send, part, early[2])
+    late = across(keep, send)
+    hidden = call(functools.partial(activate, width), shape(block, width), early + late, "v" * 2 * NY, moved=10 * block * wide)
+    same = {0: hidden, **{k: shift(hidden, "y", k, NY) for k in AWAY}}
+    other = {k: shift(v, "core", 1, NC) for k, v in same.items()}
+    same, other = ([v[k] for k in range(NY)] for v in (same, other))
 
     def expand(first, last):
         got = call(
@@ -375,14 +384,15 @@
         )
         return {j: got[2 * i : 2 * i + 2] for i, j in enumerate(ORDER[first:last])}
 
-    terms = {**expand(EARLY, NZ), **expand(0, EARLY)}
+    terms = {**expand(FAR, NZ), **expand(0, FAR)}
 
     def chain(half, way, steps):
         got = terms[way * steps if steps < NZ // 2 else steps][half]
         for step in range(steps, 1, -1):
             got = shift(got, "z", way, NZ)
             own = terms[way * (step - 1)][half]
-            got = call(add, shape(piece // 2, feats), [got, own], "vv", moved=6 * piece * feats // 2)
+            after = [terms[0][0]] if step == steps else []
+            got = call(add, shape(piece // 2, feats), [got, own] + after, "vvh"[: 2 + len(after)], moved=3 * piece * feats)
         return shift(got, "z", way, NZ)
 
     far = NZ // 2
@@ -392,8 +402,9 @@
         z_sum, [shape(rows, feats, kind=f32), shape(rows, feats)], [terms[0][0]] + low, "vvv", moved=4 * piece * feats
     )
     two, three = call(z_sum, [shape(rows, feats)] * 2, [terms[0][1]] + high, "vvv", moved=4 * piece * feats)
-    parts = [shift(v, "x", -k, NX) for k, v in enumerate([one, two, three], 1)]
-    return call(finish, shape(rows, feats), [stream, mine] + parts, "v" * 5, moved=20 * rows * feats)
+    sent = {1: one, 2: two, 3: three}
+    parts = {k: shift(sent[k], "x", -k, NX) for k in AWAY}
+    return call(finish, shape(rows, feats), [stream, mine] + [parts[k] for k in range(1, NX)], "v" * 5, moved=20 * rows * feats)
 
 
 def solution(mesh):

time: 124 us -> 121 us (0.976); the launches traced: 122 us -> 121 us
  starting transfers between devices: 57.1 us -> 52.7 us
  waiting for transfers between devices: 40.8 us -> 43 us
    ppermute x40 -> x43, starting transfers between devices: 57.1 us -> 52.7 us  [shift(): return lax.ppermute(v, axis, [(i, (i + by) % n) for i in range(n)])]
    ppermute x40 -> x43, waiting for transfers between devices: 40.8 us -> 43 us  [shift(): return lax.ppermute(v, axis, [(i, (i + by) % n) for i in range(n)])]
    pallas_call x23 -> x26, Pallas kernels: 20.3 us -> 21.1 us  [call(): pl.pallas_call(kernel, out_shape=whole, in_specs=[pl.BlockSpec(memory_spa...]
  transfers between devices with their start and end apart: 40 -> 43, of which waited for: 22 -> 25; matrix products, arithmetic and copies ran while one was open for 0% -> 0% of each run, Pallas kernels for 11% -> 9%
where the time goes in v1:
time: 121 us
  starting transfers between devices  52.7 us (44%)
  waiting for transfers between devices  43 us (36%)
  Pallas kernels  21.1 us (17%)
  local copies, waits for them, and re-layouts  3.63 us (3%)
    ppermute x43, starting transfers between devices, shift(): return lax.ppermute(v, axis, [(i, (i + by) % n) for i in range(n)])  52.7 us
    ppermute x43, waiting for transfers between devices, shift(): return lax.ppermute(v, axis, [(i, (i + by) % n) for i in range(n)])  43 us
    pallas_call x26, Pallas kernels, call(): pl.pallas_call(kernel, out_shape=whole, in_specs=[pl.BlockSpec(memory_spa...  21.1 us
    unnamed x16, local copies, waits for them, and re-layouts  3.63 us
  transfers between devices with their start and end apart: 43, of which 25 were waited for; matrix products, arithmetic and copies ran while one was open for 0% of the time, Pallas kernels for 9%

profile of v1, /device:TPU:32, one launch (start us, length us, event | category | flops | bytes accessed | tf_op | source)
XLA Modules:
  0.0 120.8 jit_solution(12491004449254103733)
XLA Ops:
  0.0 2.6 %shard_map.109 = (f32[16,2048]{1,0:T(8,128)}, f32[16,128]{1,0:T(8,128)}, bf16[16,2048]{1,0:T(8,128)(2,1)}) custom-call(s32[16]{0:T(128)} %lengths_in.1, bf16[16,2048]{1,0:T(8,128)(2,1)} %hidden_in.1, bf16[16,2048]{1,0:T(8,128)(2,1)} %queries_in.1, bf16[16,128,128]{2,1,0:T(8,128)(2,1)} %keys_in.1, bf16[16,128,128]{2,1,0:T(8,128)(2,1)} %values_in.1, ...), custom_call_target="tpu_custom_call" | custom-call | bytes 1048576 | tf_op jit(solution)/shard_map/pallas_call | solution.py:35
  2.6 2.8 %collective-permute-start.2 = (bf16[16,2048]{1,0:T(8,128)(2,1)}, bf16[16,2048]{1,0:T(8,128)(2,1)S(1)}, u32[]{:S(2)}, u32[]{:S(2)}) collective-permute-start(bf16[16,2048]{1,0:T(8,128)(2,1)} %get-tuple-element.50.own), channel_id=1, source_target_pairs={{0,192},{64,0},{128,64},{192,128},{1,193},{65,1},{129,65},{193,129... | collective-permute-start | bytes 196616 | tf_op jit(solution)/shard_map/ppermute | solution.py:24
  8.0 3.4 %collective-permute-done.1.refs_1_ = bf16[16,2048]{1,0:T(8,128)(2,1)S(1)} collective-permute-done((bf16[16,2048]{1,0:T(8,128)(2,1)}, bf16[16,2048]{1,0:T(8,128)(2,1)S(1)}, u32[]{:S(2)}, u32[]{:S(2)}) %collective-permute-start.1) | collective-permute-done | bytes 65568 | tf_op jit(solution)/shard_map/ppermute | solution.py:24
  14.3 4.8 %collective-permute-done.6.refs_2_ = bf16[64,2048]{1,0:T(8,128)(2,1)S(1)} collective-permute-done((bf16[64,2048]{1,0:T(8,128)(2,1)S(1)}, bf16[64,2048]{1,0:T(8,128)(2,1)S(1)}, u32[]{:S(2)}, u32[]{:S(2)}) %collective-permute-start.6) | collective-permute-done | bytes 262176 | tf_op jit(solution)/shard_map/ppermute | solution.py:24
  19.0 3.3 %collective-permute-start.7 = (bf16[64,2048]{1,0:T(8,128)(2,1)S(1)}, bf16[64,2048]{1,0:T(8,128)(2,1)S(1)}, u32[]{:S(2)}, u32[]{:S(2)}) collective-permute-start(bf16[64,2048]{1,0:T(8,128)(2,1)S(1)} %collective-permute-done.6.refs_2_), channel_id=1, source_target_pairs={{0,56},{8,0},{16,8},{24,16},{32,24},{40,32},{48,40},{56,48},{1,57}... | collective-permute-start | bytes 786440 | tf_op jit(solution)/shard_map/ppermute | solution.py:24
  22.8 3.4 %collective-permute-done.7.refs_4_.refs_0_ = bf16[64,2048]{1,0:T(8,128)(2,1)S(1)} collective-permute-done((bf16[64,2048]{1,0:T(8,128)(2,1)S(1)}, bf16[64,2048]{1,0:T(8,128)(2,1)S(1)}, u32[]{:S(2)}, u32[]{:S(2)}) %collective-permute-start.7) | collective-permute-done | bytes 262176 | tf_op jit(solution)/shard_map/ppermute | solution.py:24
  26.2 3.7 %collective-permute-start.8 = (bf16[64,2048]{1,0:T(8,128)(2,1)S(1)}, bf16[64,2048]{1,0:T(8,128)(2,1)S(1)}, u32[]{:S(2)}, u32[]{:S(2)}) collective-permute-start(bf16[64,2048]{1,0:T(8,128)(2,1)S(1)} %collective-permute-done.7.refs_4_.refs_0_), channel_id=1, source_target_pairs={{0,56},{8,0},{16,8},{24,16},{32,24},{40,32},{48,40},{56,48},{1,57}... | collective-permute-start | bytes 786440 | tf_op jit(solution)/shard_map/ppermute | solution.py:24
  33.2 2.7 %shard_map.112 = (bf16[128,1920]{1,0:T(8,128)(2,1)S(1)}, bf16[128,1920]{1,0:T(8,128)(2,1)S(1)}, bf16[256,2048]{1,0:T(8,128)(2,1)S(1)}, f32[8,128]{1,0:T(8,128)S(1)}) custom-call(s32[4]{0:T(128)S(1)} %pad_add_fusion.idx, bf16[64,2048]{1,0:T(8,128)(2,1)S(1)} %shard_map.111.refs_0_, bf16[64,2048]{1,0:T(8,128)(2,1)S(1)} %collective-permute-done.3.refs_1_, ...), custom_call_target="tpu_custom_call" | custom-call | flops 939524096 | bytes 3670016 | tf_op jit(solution)/shard_map/pallas_call | solution.py:35
  35.9 2.2 %collective-permute-done.5.up.refs_1_ = bf16[64,2048]{1,0:T(8,128)(2,1)S(1)} collective-permute-done((bf16[64,2048]{1,0:T(8,128)(2,1)S(1)}, bf16[64,2048]{1,0:T(8,128)(2,1)S(1)}, u32[]{:S(2)}, u32[]{:S(2)}) %collective-permute-start.5) | collective-permute-done | bytes 262176 | tf_op jit(solution)/shard_map/ppermute | solution.py:24
  39.9 3.3 %collective-permute-start.14 = (bf16[32,2048]{1,0:T(8,128)(2,1)S(1)}, bf16[32,2048]{1,0:T(8,128)(2,1)S(1)}, u32[]{:S(2)}, u32[]{:S(2)}) collective-permute-start(bf16[32,2048]{1,0:T(8,128)(2,1)S(1)} %get-tuple-element.63), channel_id=1, source_target_pairs={{0,56},{8,0},{16,8},{24,16},{32,24},{40,32},{48,40},{56,48},{1,57}... | collective-permute-start | bytes 393224 | tf_op jit(solution)/shard_map/ppermute | solution.py:24
  43.9 3.5 %collective-permute-start.11 = (bf16[32,1920]{1,0:T(8,128)(2,1)S(1)}, bf16[32,1920]{1,0:T(8,128)(2,1)S(1)}, u32[]{:S(2)}, u32[]{:S(2)}) collective-permute-start(bf16[32,1920]{1,0:T(8,128)(2,1)S(1)} %get-tuple-element.61), channel_id=1, source_target_pairs={{0,4},{2,6},{4,0},{6,2},{1,5},{3,7},{5,1},{7,3},{8,12},{10,14},{12... | collective-permute-start | bytes 368648 | tf_op jit(solution)/shard_map/ppermute | solution.py:24
  48.8 3.3 %shard_map.116 = (bf16[128,1920]{1,0:T(8,128)(2,1)S(1)}, bf16[128,1920]{1,0:T(8,128)(2,1)S(1)}, bf16[256,2048]{1,0:T(8,128)(2,1)S(1)}, f32[8,128]{1,0:T(8,128)}) custom-call(s32[4]{0:T(128)S(1)} %pad_add_fusion.idx, bf16[64,2048]{1,0:T(8,128)(2,1)S(1)} %collective-permute-done.7.refs_4_.refs_0_, bf16[64,2048]{1,0:T(8,128)(2,1)S(1)} %collective-permute-done.5.up.refs_1_, ...), custom_call_target="tpu_custom_call" | custom-call | flops 939524096 | bytes 3670016 | tf_op jit(solution)/shard_map/pallas_call | solution.py:35
  58.4 2.9 %collective-permute-start.17 = (bf16[32,1920]{1,0:T(8,128)(2,1)S(1)}, bf16[32,1920]{1,0:T(8,128)(2,1)S(1)}, u32[]{:S(2)}, u32[]{:S(2)}) collective-permute-start(bf16[32,1920]{1,0:T(8,128)(2,1)S(1)} %get-tuple-element.71), channel_id=1, source_target_pairs={{0,4},{2,6},{4,0},{6,2},{1,5},{3,7},{5,1},{7,3},{8,12},{10,14},{12... | collective-permute-start | bytes 368648 | tf_op jit(solution)/shard_map/ppermute | solution.py:24
  64.7 2.8 %collective-permute-done.17.refs_6_ = bf16[32,1920]{1,0:T(8,128)(2,1)S(1)} collective-permute-done((bf16[32,1920]{1,0:T(8,128)(2,1)S(1)}, bf16[32,1920]{1,0:T(8,128)(2,1)S(1)}, u32[]{:S(2)}, u32[]{:S(2)}) %collective-permute-start.17) | collective-permute-done | bytes 122912 | tf_op jit(solution)/shard_map/ppermute | solution.py:24
  67.8 2.7 %collective-permute-start.21 = (bf16[64,896]{1,0:T(8,128)(2,1)S(1)}, bf16[64,896]{1,0:T(8,128)(2,1)S(1)}, u32[]{:S(2)}, u32[]{:S(2)}) collective-permute-start(bf16[64,896]{1,0:T(8,128)(2,1)S(1)} %shard_map.119.refs_0_), channel_id=1, source_target_pairs={{0,6},{2,0},{4,2},{6,4},{1,7},{3,1},{5,3},{7,5},{8,14},{10,8},{12,... | collective-permute-start | bytes 344072 | tf_op jit(solution)/shard_map/ppermute | solution.py:24
  71.5 3.6 %collective-permute-done.21.refs_3_ = bf16[64,896]{1,0:T(8,128)(2,1)S(1)} collective-permute-done((bf16[64,896]{1,0:T(8,128)(2,1)S(1)}, bf16[64,896]{1,0:T(8,128)(2,1)S(1)}, u32[]{:S(2)}, u32[]{:S(2)}) %collective-permute-start.21) | collective-permute-done | bytes 114720 | tf_op jit(solution)/shard_map/ppermute | solution.py:24
  75.1 2.5 %collective-permute-done.20.refs_2_ = bf16[64,896]{1,0:T(8,128)(2,1)S(1)} collective-permute-done((bf16[64,896]{1,0:T(8,128)(2,1)S(1)}, bf16[64,896]{1,0:T(8,128)(2,1)S(1)}, u32[]{:S(2)}, u32[]{:S(2)}) %collective-permute-start.20) | collective-permute-done | bytes 114720 | tf_op jit(solution)/shard_map/ppermute | solution.py:24
  80.1 2.9 %shard_map.121 = (bf16[32,2048]{1,0:T(8,128)(2,1)S(1)}, bf16[32,2048]{1,0:T(8,128)(2,1)S(1)}, bf16[32,2048]{1,0:T(8,128)(2,1)S(1)}, bf16[32,2048]{1,0:T(8,128)(2...) custom-call(s32[4]{0:T(128)S(1)} %pad_add_fusion.idx, bf16[64,896]{1,0:T(8,128)(2,1)S(1)} %shard_map.119.refs_0_, ...), custom_call_target="tpu_custom_call" | custom-call | flops 704643072 | bytes 3670016 | tf_op jit(solution)/shard_map/pallas_call | solution.py:35
  83.0 2.5 %collective-permute-start.26 = (bf16[32,2048]{1,0:T(8,128)(2,1)S(1)}, bf16[32,2048]{1,0:T(8,128)(2,1)S(1)}, u32[]{:S(2)}, u32[]{:S(2)}) collective-permute-start(bf16[32,2048]{1,0:T(8,128)(2,1)S(1)} %get-tuple-element.74), channel_id=1, source_target_pairs={{0,56},{8,0},{16,8},{24,16},{32,24},{40,32},{48,40},{56,48},{1,57}... | collective-permute-start | bytes 393224 | tf_op jit(solution)/shard_map/ppermute | solution.py:24
  87.5 3.5 %shard_map.120 = (bf16[32,2048]{1,0:T(8,128)(2,1)S(1)}, bf16[32,2048]{1,0:T(8,128)(2,1)S(1)}, bf16[32,2048]{1,0:T(8,128)(2,1)S(1)}, bf16[32,2048]{1,0:T(8,128)(2...) custom-call(s32[4]{0:T(128)S(1)} %pad_add_fusion.idx, ...), custom_call_target="tpu_custom_call" | custom-call | flops 1174405120 | bytes 3670016 | tf_op jit(solution)/shard_map/pallas_call | solution.py:35
  91.1 3.3 %collective-permute-start.27 = (bf16[32,2048]{1,0:T(8,128)(2,1)S(1)}, bf16[32,2048]{1,0:T(8,128)(2,1)S(1)}, u32[]{:S(2)}, u32[]{:S(2)}) collective-permute-start(bf16[32,2048]{1,0:T(8,128)(2,1)S(1)} %shard_map.122), channel_id=1, source_target_pairs={{0,56},{8,0},{16,8},{24,16},{32,24},{40,32},{48,40},{56,48},{1,57}... | collective-permute-start | bytes 393224 | tf_op jit(solution)/shard_map/ppermute | solution.py:24
  98.2 2.6 %collective-permute-start.28 = (bf16[32,2048]{1,0:T(8,128)(2,1)S(1)}, bf16[32,2048]{1,0:T(8,128)(2,1)S(1)}, u32[]{:S(2)}, u32[]{:S(2)}) collective-permute-start(bf16[32,2048]{1,0:T(8,128)(2,1)S(1)} %shard_map.123), channel_id=1, source_target_pairs={{0,56},{8,0},{16,8},{24,16},{32,24},{40,32},{48,40},{56,48},{1,57}... | collective-permute-start | bytes 393224 | tf_op jit(solution)/shard_map/ppermute | solution.py:24
  103.3 2.5 %collective-permute-start.29 = (bf16[32,2048]{1,0:T(8,128)(2,1)S(1)}, bf16[32,2048]{1,0:T(8,128)(2,1)S(1)}, u32[]{:S(2)}, u32[]{:S(2)}) collective-permute-start(bf16[32,2048]{1,0:T(8,128)(2,1)S(1)} %shard_map.124), channel_id=1, source_target_pairs={{0,56},{8,0},{16,8},{24,16},{32,24},{40,32},{48,40},{56,48},{1,57}... | collective-permute-start | bytes 393224 | tf_op jit(solution)/shard_map/ppermute | solution.py:24
  114.7 4.0 %collective-permute-done.41.two = bf16[16,2048]{1,0:T(8,128)(2,1)S(1)} collective-permute-done((bf16[16,2048]{1,0:T(8,128)(2,1)S(1)}, bf16[16,2048]{1,0:T(8,128)(2,1)S(1)}, u32[]{:S(2)}, u32[]{:S(2)}) %collective-permute-start.41) | collective-permute-done | bytes 65568 | tf_op jit(solution)/shard_map/ppermute | solution.py:24
  (105 shorter events, 45.9 us)
Async XLA Ops:
  12.2 6.9 %collective-permute-start.6 = (bf16[64,2048]{1,0:T(8,128)(2,1)S(1)}, bf16[64,2048]{1,0:T(8,128)(2,1)S(1)}, u32[]{:S(2)}, u32[]{:S(2)}) collective-permute-start(bf16[64,2048]{1,0:T(8,128)(2,1)S(1)} %shard_map.111.refs_0_), channel_id=1, source_target_pairs={{0,56},{8,0},{16,8},{24,16},{32,24},{40,32},{48,40},{56,48},{1,57}... | collective-permute-start | bytes 786440 | tf_op jit(solution)/shard_map/ppermute | solution.py:24
  12.3 10.4 %collective-permute-start.3 = (bf16[64,2048]{1,0:T(8,128)(2,1)S(1)}, bf16[64,2048]{1,0:T(8,128)(2,1)S(1)}, u32[]{:S(2)}, u32[]{:S(2)}) collective-permute-start(bf16[64,2048]{1,0:T(8,128)(2,1)S(1)} %shard_map.111.refs_0_), channel_id=1, source_target_pairs={{0,8},{8,16},{16,24},{24,32},{32,40},{40,48},{48,56},{56,0},{1,9},... | collective-permute-start | bytes 786440 | tf_op jit(solution)/shard_map/ppermute | solution.py:24
  19.0 7.2 %collective-permute-start.7 = (bf16[64,2048]{1,0:T(8,128)(2,1)S(1)}, bf16[64,2048]{1,0:T(8,128)(2,1)S(1)}, u32[]{:S(2)}, u32[]{:S(2)}) collective-permute-start(bf16[64,2048]{1,0:T(8,128)(2,1)S(1)} %collective-permute-done.6.refs_2_), channel_id=1, source_target_pairs={{0,56},{8,0},{16,8},{24,16},{32,24},{40,32},{48,40},{56,48},{1,57}... | collective-permute-start | bytes 786440 | tf_op jit(solution)/shard_map/ppermute | solution.py:24
  22.8 7.6 %collective-permute-start.4 = (bf16[64,2048]{1,0:T(8,128)(2,1)S(1)}, bf16[64,2048]{1,0:T(8,128)(2,1)S(1)}, u32[]{:S(2)}, u32[]{:S(2)}) collective-permute-start(bf16[64,2048]{1,0:T(8,128)(2,1)S(1)} %collective-permute-done.3.refs_1_), channel_id=1, source_target_pairs={{0,8},{8,16},{16,24},{24,32},{32,40},{40,48},{48,56},{56,0},{1,9},... | collective-permute-start | bytes 786440 | tf_op jit(solution)/shard_map/ppermute | solution.py:24
  26.2 9.7 %collective-permute-start.8 = (bf16[64,2048]{1,0:T(8,128)(2,1)S(1)}, bf16[64,2048]{1,0:T(8,128)(2,1)S(1)}, u32[]{:S(2)}, u32[]{:S(2)}) collective-permute-start(bf16[64,2048]{1,0:T(8,128)(2,1)S(1)} %collective-permute-done.7.refs_4_.refs_0_), channel_id=1, source_target_pairs={{0,56},{8,0},{16,8},{24,16},{32,24},{40,32},{48,40},{56,48},{1,57}... | collective-permute-start | bytes 786440 | tf_op jit(solution)/shard_map/ppermute | solution.py:24
  30.4 7.7 %collective-permute-start.5 = (bf16[64,2048]{1,0:T(8,128)(2,1)S(1)}, bf16[64,2048]{1,0:T(8,128)(2,1)S(1)}, u32[]{:S(2)}, u32[]{:S(2)}) collective-permute-start(bf16[64,2048]{1,0:T(8,128)(2,1)S(1)} %collective-permute-done.4.refs_3_), channel_id=1, source_target_pairs={{0,8},{8,16},{16,24},{24,32},{32,40},{40,48},{48,56},{56,0},{1,9},... | collective-permute-start | bytes 786440 | tf_op jit(solution)/shard_map/ppermute | solution.py:24
  39.9 7.4 %collective-permute-start.14 = (bf16[32,2048]{1,0:T(8,128)(2,1)S(1)}, bf16[32,2048]{1,0:T(8,128)(2,1)S(1)}, u32[]{:S(2)}, u32[]{:S(2)}) collective-permute-start(bf16[32,2048]{1,0:T(8,128)(2,1)S(1)} %get-tuple-element.63), channel_id=1, source_target_pairs={{0,56},{8,0},{16,8},{24,16},{32,24},{40,32},{48,40},{56,48},{1,57}... | collective-permute-start | bytes 393224 | tf_op jit(solution)/shard_map/ppermute | solution.py:24
  43.9 8.2 %collective-permute-start.11 = (bf16[32,1920]{1,0:T(8,128)(2,1)S(1)}, bf16[32,1920]{1,0:T(8,128)(2,1)S(1)}, u32[]{:S(2)}, u32[]{:S(2)}) collective-permute-start(bf16[32,1920]{1,0:T(8,128)(2,1)S(1)} %get-tuple-element.61), channel_id=1, source_target_pairs={{0,4},{2,6},{4,0},{6,2},{1,5},{3,7},{5,1},{7,3},{8,12},{10,14},{12... | collective-permute-start | bytes 368648 | tf_op jit(solution)/shard_map/ppermute | solution.py:24
  54.0 8.7 %collective-permute-start.10 = (bf16[32,1920]{1,0:T(8,128)(2,1)S(1)}, bf16[32,1920]{1,0:T(8,128)(2,1)S(1)}, u32[]{:S(2)}, u32[]{:S(2)}) collective-permute-start(bf16[32,1920]{1,0:T(8,128)(2,1)S(1)} %get-tuple-element.60), channel_id=1, source_target_pairs={{0,2},{2,4},{4,6},{6,0},{1,3},{3,5},{5,7},{7,1},{8,10},{10,12},{12... | collective-permute-start | bytes 368648 | tf_op jit(solution)/shard_map/ppermute | solution.py:24
  55.6 7.0 %collective-permute-start.12 = (bf16[32,1920]{1,0:T(8,128)(2,1)S(1)}, bf16[32,1920]{1,0:T(8,128)(2,1)S(1)}, u32[]{:S(2)}, u32[]{:S(2)}) collective-permute-start(bf16[32,1920]{1,0:T(8,128)(2,1)S(1)} %get-tuple-element.62), channel_id=1, source_target_pairs={{0,6},{2,0},{4,2},{6,4},{1,7},{3,1},{5,3},{7,5},{8,14},{10,8},{12,... | collective-permute-start | bytes 368648 | tf_op jit(solution)/shard_map/ppermute | solution.py:24
  58.0 6.7 %collective-permute-start.16 = (bf16[32,1920]{1,0:T(8,128)(2,1)S(1)}, bf16[32,1920]{1,0:T(8,128)(2,1)S(1)}, u32[]{:S(2)}, u32[]{:S(2)}) collective-permute-start(bf16[32,1920]{1,0:T(8,128)(2,1)S(1)} %get-tuple-element.70), channel_id=1, source_target_pairs={{0,2},{2,4},{4,6},{6,0},{1,3},{3,5},{5,7},{7,1},{8,10},{10,12},{12... | collective-permute-start | bytes 368648 | tf_op jit(solution)/shard_map/ppermute | solution.py:24
  58.4 9.0 %collective-permute-start.17 = (bf16[32,1920]{1,0:T(8,128)(2,1)S(1)}, bf16[32,1920]{1,0:T(8,128)(2,1)S(1)}, u32[]{:S(2)}, u32[]{:S(2)}) collective-permute-start(bf16[32,1920]{1,0:T(8,128)(2,1)S(1)} %get-tuple-element.71), channel_id=1, source_target_pairs={{0,4},{2,6},{4,0},{6,2},{1,5},{3,7},{5,1},{7,3},{8,12},{10,14},{12... | collective-permute-start | bytes 368648 | tf_op jit(solution)/shard_map/ppermute | solution.py:24
  67.8 7.3 %collective-permute-start.21 = (bf16[64,896]{1,0:T(8,128)(2,1)S(1)}, bf16[64,896]{1,0:T(8,128)(2,1)S(1)}, u32[]{:S(2)}, u32[]{:S(2)}) collective-permute-start(bf16[64,896]{1,0:T(8,128)(2,1)S(1)} %shard_map.119.refs_0_), channel_id=1, source_target_pairs={{0,6},{2,0},{4,2},{6,4},{1,7},{3,1},{5,3},{7,5},{8,14},{10,8},{12,... | collective-permute-start | bytes 344072 | tf_op jit(solution)/shard_map/ppermute | solution.py:24
  70.6 7.0 %collective-permute-start.20 = (bf16[64,896]{1,0:T(8,128)(2,1)S(1)}, bf16[64,896]{1,0:T(8,128)(2,1)S(1)}, u32[]{:S(2)}, u32[]{:S(2)}) collective-permute-start(bf16[64,896]{1,0:T(8,128)(2,1)S(1)} %shard_map.119.refs_0_), channel_id=1, source_target_pairs={{0,4},{2,6},{4,0},{6,2},{1,5},{3,7},{5,1},{7,3},{8,12},{10,14},{12... | collective-permute-start | bytes 344072 | tf_op jit(solution)/shard_map/ppermute | solution.py:24
  71.3 7.5 %collective-permute-start.19 = (bf16[64,896]{1,0:T(8,128)(2,1)S(1)}, bf16[64,896]{1,0:T(8,128)(2,1)S(1)}, u32[]{:S(2)}, u32[]{:S(2)}) collective-permute-start(bf16[64,896]{1,0:T(8,128)(2,1)S(1)} %shard_map.119.refs_0_), channel_id=1, source_target_pairs={{0,2},{2,4},{4,6},{6,0},{1,3},{3,5},{5,7},{7,1},{8,10},{10,12},{12... | collective-permute-start | bytes 344072 | tf_op jit(solution)/shard_map/ppermute | solution.py:24
  71.5 7.3 %collective-permute-start.22 = (bf16[64,896]{1,0:T(8,128)(2,1)S(1)}, bf16[64,896]{1,0:T(8,128)(2,1)S(1)}, u32[]{:S(2)}, u32[]{:S(2)}) collective-permute-start(bf16[64,896]{1,0:T(8,128)(2,1)S(1)} %shard_map.119.refs_0_), channel_id=1, source_target_pairs={{0,1},{1,0},{2,3},{3,2},{4,5},{5,4},{6,7},{7,6},{8,9},{9,8},{10,11... | collective-permute-start | bytes 344072 | tf_op jit(solution)/shard_map/ppermute | solution.py:24
  83.0 8.0 %collective-permute-start.26 = (bf16[32,2048]{1,0:T(8,128)(2,1)S(1)}, bf16[32,2048]{1,0:T(8,128)(2,1)S(1)}, u32[]{:S(2)}, u32[]{:S(2)}) collective-permute-start(bf16[32,2048]{1,0:T(8,128)(2,1)S(1)} %get-tuple-element.74), channel_id=1, source_target_pairs={{0,56},{8,0},{16,8},{24,16},{32,24},{40,32},{48,40},{56,48},{1,57}... | collective-permute-start | bytes 393224 | tf_op jit(solution)/shard_map/ppermute | solution.py:24
  85.5 8.9 %collective-permute-start.34 = (bf16[32,2048]{1,0:T(8,128)(2,1)S(1)}, bf16[32,2048]{1,0:T(8,128)(2,1)S(1)}, u32[]{:S(2)}, u32[]{:S(2)}) collective-permute-start(bf16[32,2048]{1,0:T(8,128)(2,1)S(1)} %get-tuple-element.84), channel_id=1, source_target_pairs={{0,8},{8,16},{16,24},{24,32},{32,40},{40,48},{48,56},{56,0},{1,9},... | collective-permute-start | bytes 393224 | tf_op jit(solution)/shard_map/ppermute | solution.py:24
  85.5 9.0 %collective-permute-start.30 = (bf16[32,2048]{1,0:T(8,128)(2,1)S(1)}, bf16[32,2048]{1,0:T(8,128)(2,1)S(1)}, u32[]{:S(2)}, u32[]{:S(2)}) collective-permute-start(bf16[32,2048]{1,0:T(8,128)(2,1)S(1)} %get-tuple-element.78), channel_id=1, source_target_pairs={{0,8},{8,16},{16,24},{24,32},{32,40},{40,48},{48,56},{56,0},{1,9},... | collective-permute-start | bytes 393224 | tf_op jit(solution)/shard_map/ppermute | solution.py:24
  85.5 9.2 %collective-permute-start.38 = (bf16[32,2048]{1,0:T(8,128)(2,1)S(1)}, bf16[32,2048]{1,0:T(8,128)(2,1)S(1)}, u32[]{:S(2)}, u32[]{:S(2)}) collective-permute-start(bf16[32,2048]{1,0:T(8,128)(2,1)S(1)} %get-tuple-element.88), channel_id=1, source_target_pairs={{0,56},{8,0},{16,8},{24,16},{32,24},{40,32},{48,40},{56,48},{1,57}... | collective-permute-start | bytes 393224 | tf_op jit(solution)/shard_map/ppermute | solution.py:24
  91.1 7.1 %collective-permute-start.27 = (bf16[32,2048]{1,0:T(8,128)(2,1)S(1)}, bf16[32,2048]{1,0:T(8,128)(2,1)S(1)}, u32[]{:S(2)}, u32[]{:S(2)}) collective-permute-start(bf16[32,2048]{1,0:T(8,128)(2,1)S(1)} %shard_map.122), channel_id=1, source_target_pairs={{0,56},{8,0},{16,8},{24,16},{32,24},{40,32},{48,40},{56,48},{1,57}... | collective-permute-start | bytes 393224 | tf_op jit(solution)/shard_map/ppermute | solution.py:24
  94.6 7.8 %collective-permute-start.31 = (bf16[32,2048]{1,0:T(8,128)(2,1)S(1)}, bf16[32,2048]{1,0:T(8,128)(2,1)S(1)}, u32[]{:S(2)}, u32[]{:S(2)}) collective-permute-start(bf16[32,2048]{1,0:T(8,128)(2,1)S(1)} %shard_map.125), channel_id=1, source_target_pairs={{0,8},{8,16},{16,24},{24,32},{32,40},{40,48},{48,56},{56,0},{1,9},... | collective-permute-start | bytes 393224 | tf_op jit(solution)/shard_map/ppermute | solution.py:24
  94.7 8.1 %collective-permute-start.39 = (bf16[32,2048]{1,0:T(8,128)(2,1)S(1)}, bf16[32,2048]{1,0:T(8,128)(2,1)S(1)}, u32[]{:S(2)}, u32[]{:S(2)}) collective-permute-start(bf16[32,2048]{1,0:T(8,128)(2,1)S(1)} %shard_map.131), channel_id=1, source_target_pairs={{0,56},{8,0},{16,8},{24,16},{32,24},{40,32},{48,40},{56,48},{1,57}... | collective-permute-start | bytes 393224 | tf_op jit(solution)/shard_map/ppermute | solution.py:24
  100.8 6.9 %collective-permute-start.36 = (bf16[32,2048]{1,0:T(8,128)(2,1)S(1)}, bf16[32,2048]{1,0:T(8,128)(2,1)S(1)}, u32[]{:S(2)}, u32[]{:S(2)}) collective-permute-start(bf16[32,2048]{1,0:T(8,128)(2,1)S(1)} %shard_map.129), channel_id=1, source_target_pairs={{0,8},{8,16},{16,24},{24,32},{32,40},{40,48},{48,56},{56,0},{1,9},... | collective-permute-start | bytes 393224 | tf_op jit(solution)/shard_map/ppermute | solution.py:24
  (27 other events, 179.2 us)

commit v2 on v1

--- a/solution.py
+++ b/solution.py
@@ -225,28 +225,25 @@
 def second_matmul(first, last, idx, *refs):
     same, refs = refs[:NY], refs[NY:]
     other, refs = refs[:NY], refs[NY:]
-    weights, outs, (hidden, terms) = refs[0], refs[1:-2], refs[-2:]
+    weights, outs, hidden = refs[0], refs[1:-1], refs[-1]
     mine, core = idx[2], idx[3]
     block = same[0].shape[0]
     half = block // 2
+    groups = range(first // NY, 2)
     for k in range(NY):
         y = lax.rem(mine - k + NY, NY)
-        for i in range(2):
-            at = (i * NY + y) * block
+        for i in groups:
+            at = ((i - groups[0]) * NY + y) * block
             hidden[rows_at(at + core * half, half), :] = same[k][pl.ds(i * half, half), :]
             hidden[rows_at(at + (1 - core) * half, half), :] = other[k][pl.ds(i * half, half), :]
+    some = pl.ds((first - groups[0] * NY) * block, (last - first) * block)
 
     @pl.loop(0, weights.shape[1] // 256)
     def _(t):
         cols = pl.ds(pl.multiple_of(t * 256, 256), 256)
-        some = hidden[pl.ds(first * block, (last - first) * block), :]
-        terms[:, cols] = jnp.dot(some, weights[:, cols], preferred_element_type=jnp.float32).astype(jnp.bfloat16)
-
-    at = 0
-    for out in outs:
-        size = out.shape[0]
-        out[...] = terms[pl.ds(at, size), :]
-        at += size
+        terms = jnp.dot(hidden[some, :], weights[:, cols], preferred_element_type=jnp.float32).astype(jnp.bfloat16)
+        for i, out in enumerate(outs):
+            out[:, cols] = terms[i * half : (i + 1) * half]
 
 
 def add(came, own, *refs):
@@ -364,8 +361,8 @@
         return [own] + [got[k] for k in range(1, NY)]
 
     early = across(keep, send)
-    keep, send, part, _ = gates([pieces[j] for j in ORDER[EARLY:-1]] + [up, down], early[0])
-    keep, send = ups(keep, send, part, early[2])
+    keep, send, part, _ = gates([pieces[j] for j in ORDER[EARLY:-1]] + [up, down], idx)
+    keep, send = ups(keep, send, part, idx)
     late = across(keep, send)
     hidden = call(functools.partial(activate, width), shape(block, width), early + late, "v" * 2 * NY, moved=10 * block * wide)
     same = {0: hidden, **{k: shift(hidden, "y", k, NY) for k in AWAY}}
@@ -378,7 +375,7 @@
             [shape(piece // 2, feats)] * (2 * (last - first)),
             [idx] + same + other + [w_down],
             "s" + "v" * (2 * NY + 1),
-            scratch=[pltpu.VMEM((total, width), bf16), pltpu.VMEM(((last - first) * piece, feats), bf16)],
+            scratch=[pltpu.VMEM((total - first // NY * NY * piece, width), bf16)],
             flops=2 * (last - first) * piece * feats * width,
             moved=2 * feats * width,
         )

time: 121 us -> 122 us (level)
  waiting for transfers between devices: 43 us -> 45.3 us
  starting transfers between devices: 52.7 us -> 51.2 us
    ppermute x43, waiting for transfers between devices: 43 us -> 45.3 us  [shift(): return lax.ppermute(v, axis, [(i, (i + by) % n) for i in range(n)])]
    ppermute x43, starting transfers between devices: 52.7 us -> 51.2 us  [shift(): return lax.ppermute(v, axis, [(i, (i + by) % n) for i in range(n)])]
  transfers between devices with their start and end apart: 43 -> 43, of which waited for: 25 -> 26; matrix products, arithmetic and copies ran while one was open for 0% -> 0% of each run, Pallas kernels for 9% -> 12%
where the time goes in v2:
time: 122 us; the launch traced here: 121 us
  starting transfers between devices  51.2 us (42%)
  waiting for transfers between devices  45.3 us (37%)
  Pallas kernels  21 us (17%)
  local copies, waits for them, and re-layouts  3.63 us (3%)
    ppermute x43, starting transfers between devices, shift(): return lax.ppermute(v, axis, [(i, (i + by) % n) for i in range(n)])  51.2 us
    ppermute x43, waiting for transfers between devices, shift(): return lax.ppermute(v, axis, [(i, (i + by) % n) for i in range(n)])  45.3 us
    pallas_call x26, Pallas kernels, call(): pl.pallas_call(kernel, out_shape=whole, in_specs=[pl.BlockSpec(memory_spa...  21 us
    unnamed x16, local copies, waits for them, and re-layouts  3.63 us
  transfers between devices with their start and end apart: 43, of which 26 were waited for; matrix products, arithmetic and copies ran while one was open for 0% of the time, Pallas kernels for 12%

profile of v2, /device:TPU:32, one launch (start us, length us, event | category | flops | bytes accessed | tf_op | source)
XLA Modules:
  0.0 121.5 jit_solution(13655124987549285217)
XLA Ops:
  0.0 2.6 %shard_map.109 = (f32[16,2048]{1,0:T(8,128)}, f32[16,128]{1,0:T(8,128)}, bf16[16,2048]{1,0:T(8,128)(2,1)}) custom-call(s32[16]{0:T(128)} %lengths_in.1, bf16[16,2048]{1,0:T(8,128)(2,1)} %hidden_in.1, bf16[16,2048]{1,0:T(8,128)(2,1)} %queries_in.1, bf16[16,128,128]{2,1,0:T(8,128)(2,1)} %keys_in.1, bf16[16,128,128]{2,1,0:T(8,128)(2,1)} %values_in.1, ...), custom_call_target="tpu_custom_call" | custom-call | bytes 1048576 | tf_op jit(solution)/shard_map/pallas_call | solution.py:35
  2.6 2.8 %collective-permute-start.2 = (bf16[16,2048]{1,0:T(8,128)(2,1)}, bf16[16,2048]{1,0:T(8,128)(2,1)S(1)}, u32[]{:S(2)}, u32[]{:S(2)}) collective-permute-start(bf16[16,2048]{1,0:T(8,128)(2,1)} %get-tuple-element.50.own), channel_id=1, source_target_pairs={{0,192},{64,0},{128,64},{192,128},{1,193},{65,1},{129,65},{193,129... | collective-permute-start | bytes 196616 | tf_op jit(solution)/shard_map/ppermute | solution.py:24
  8.0 3.4 %collective-permute-done.1.refs_1_ = bf16[16,2048]{1,0:T(8,128)(2,1)S(1)} collective-permute-done((bf16[16,2048]{1,0:T(8,128)(2,1)}, bf16[16,2048]{1,0:T(8,128)(2,1)S(1)}, u32[]{:S(2)}, u32[]{:S(2)}) %collective-permute-start.1) | collective-permute-done | bytes 65568 | tf_op jit(solution)/shard_map/ppermute | solution.py:24
  14.3 4.8 %collective-permute-done.6.refs_2_ = bf16[64,2048]{1,0:T(8,128)(2,1)S(1)} collective-permute-done((bf16[64,2048]{1,0:T(8,128)(2,1)S(1)}, bf16[64,2048]{1,0:T(8,128)(2,1)S(1)}, u32[]{:S(2)}, u32[]{:S(2)}) %collective-permute-start.6) | collective-permute-done | bytes 262176 | tf_op jit(solution)/shard_map/ppermute | solution.py:24
  19.0 3.3 %collective-permute-start.7 = (bf16[64,2048]{1,0:T(8,128)(2,1)S(1)}, bf16[64,2048]{1,0:T(8,128)(2,1)S(1)}, u32[]{:S(2)}, u32[]{:S(2)}) collective-permute-start(bf16[64,2048]{1,0:T(8,128)(2,1)S(1)} %collective-permute-done.6.refs_2_), channel_id=1, source_target_pairs={{0,56},{8,0},{16,8},{24,16},{32,24},{40,32},{48,40},{56,48},{1,57}... | collective-permute-start | bytes 786440 | tf_op jit(solution)/shard_map/ppermute | solution.py:24
  22.8 3.4 %collective-permute-done.7.refs_4_.refs_0_ = bf16[64,2048]{1,0:T(8,128)(2,1)S(1)} collective-permute-done((bf16[64,2048]{1,0:T(8,128)(2,1)S(1)}, bf16[64,2048]{1,0:T(8,128)(2,1)S(1)}, u32[]{:S(2)}, u32[]{:S(2)}) %collective-permute-start.7) | collective-permute-done | bytes 262176 | tf_op jit(solution)/shard_map/ppermute | solution.py:24
  26.2 3.7 %collective-permute-start.8 = (bf16[64,2048]{1,0:T(8,128)(2,1)S(1)}, bf16[64,2048]{1,0:T(8,128)(2,1)S(1)}, u32[]{:S(2)}, u32[]{:S(2)}) collective-permute-start(bf16[64,2048]{1,0:T(8,128)(2,1)S(1)} %collective-permute-done.7.refs_4_.refs_0_), channel_id=1, source_target_pairs={{0,56},{8,0},{16,8},{24,16},{32,24},{40,32},{48,40},{56,48},{1,57}... | collective-permute-start | bytes 786440 | tf_op jit(solution)/shard_map/ppermute | solution.py:24
  33.2 2.7 %shard_map.112 = (bf16[128,1920]{1,0:T(8,128)(2,1)S(1)}, bf16[128,1920]{1,0:T(8,128)(2,1)S(1)}, bf16[256,2048]{1,0:T(8,128)(2,1)S(1)}, f32[8,128]{1,0:T(8,128)S(1)}) custom-call(s32[4]{0:T(128)S(1)} %pad_add_fusion.idx.refs_5_._, bf16[64,2048]{1,0:T(8,128)(2,1)S(1)} %shard_map.111.refs_0_, bf16[64,2048]{1,0:T(8,128)(2,1)S(1)} %collective-permute-done.3.refs_1_, ...), custom_call_target="tpu_custom_call" | custom-call | flops 939524096 | bytes 3670016 | tf_op jit(solution)/shard_map/pallas_call | solution.py:35
  38.1 3.3 %collective-permute-start.14 = (bf16[32,2048]{1,0:T(8,128)(2,1)S(1)}, bf16[32,2048]{1,0:T(8,128)(2,1)S(1)}, u32[]{:S(2)}, u32[]{:S(2)}) collective-permute-start(bf16[32,2048]{1,0:T(8,128)(2,1)S(1)} %get-tuple-element.63), channel_id=1, source_target_pairs={{0,56},{8,0},{16,8},{24,16},{32,24},{40,32},{48,40},{56,48},{1,57}... | collective-permute-start | bytes 393224 | tf_op jit(solution)/shard_map/ppermute | solution.py:24
  43.9 2.4 %collective-permute-done.13.refs_3_ = bf16[32,2048]{1,0:T(8,128)(2,1)S(1)} collective-permute-done((bf16[32,2048]{1,0:T(8,128)(2,1)S(1)}, bf16[32,2048]{1,0:T(8,128)(2,1)S(1)}, u32[]{:S(2)}, u32[]{:S(2)}) %collective-permute-start.13) | collective-permute-done | bytes 131104 | tf_op jit(solution)/shard_map/ppermute | solution.py:24
  46.3 3.3 %shard_map.116 = (bf16[128,1920]{1,0:T(8,128)(2,1)S(1)}, bf16[128,1920]{1,0:T(8,128)(2,1)S(1)}, bf16[256,2048]{1,0:T(8,128)(2,1)S(1)}, f32[8,128]{1,0:T(8,128)}) custom-call(s32[4]{0:T(128)S(1)} %pad_add_fusion.idx.refs_5_._, bf16[64,2048]{1,0:T(8,128)(2,1)S(1)} %collective-permute-done.7.refs_4_.refs_0_, ...), custom_call_target="tpu_custom_call" | custom-call | flops 939524096 | bytes 3670016 | tf_op jit(solution)/shard_map/pallas_call | solution.py:35
  53.8 2.9 %collective-permute-start.11 = (bf16[32,1920]{1,0:T(8,128)(2,1)S(1)}, bf16[32,1920]{1,0:T(8,128)(2,1)S(1)}, u32[]{:S(2)}, u32[]{:S(2)}) collective-permute-start(bf16[32,1920]{1,0:T(8,128)(2,1)S(1)} %get-tuple-element.61), channel_id=1, source_target_pairs={{0,4},{2,6},{4,0},{6,2},{1,5},{3,7},{5,1},{7,3},{8,12},{10,14},{12... | collective-permute-start | bytes 368648 | tf_op jit(solution)/shard_map/ppermute | solution.py:24
  63.5 2.6 %collective-permute-done.16.refs_5_ = bf16[32,1920]{1,0:T(8,128)(2,1)S(1)} collective-permute-done((bf16[32,1920]{1,0:T(8,128)(2,1)S(1)}, bf16[32,1920]{1,0:T(8,128)(2,1)S(1)}, u32[]{:S(2)}, u32[]{:S(2)}) %collective-permute-start.16) | collective-permute-done | bytes 122912 | tf_op jit(solution)/shard_map/ppermute | solution.py:24
  66.1 2.2 %collective-permute-done.17.refs_6_ = bf16[32,1920]{1,0:T(8,128)(2,1)S(1)} collective-permute-done((bf16[32,1920]{1,0:T(8,128)(2,1)S(1)}, bf16[32,1920]{1,0:T(8,128)(2,1)S(1)}, u32[]{:S(2)}, u32[]{:S(2)}) %collective-permute-start.17) | collective-permute-done | bytes 122912 | tf_op jit(solution)/shard_map/ppermute | solution.py:24
  68.6 2.5 %collective-permute-start.21 = (bf16[64,896]{1,0:T(8,128)(2,1)S(1)}, bf16[64,896]{1,0:T(8,128)(2,1)S(1)}, u32[]{:S(2)}, u32[]{:S(2)}) collective-permute-start(bf16[64,896]{1,0:T(8,128)(2,1)S(1)} %shard_map.119.refs_0_), channel_id=1, source_target_pairs={{0,6},{2,0},{4,2},{6,4},{1,7},{3,1},{5,3},{7,5},{8,14},{10,8},{12,... | collective-permute-start | bytes 344072 | tf_op jit(solution)/shard_map/ppermute | solution.py:24
  72.7 3.2 %collective-permute-done.21.refs_3_ = bf16[64,896]{1,0:T(8,128)(2,1)S(1)} collective-permute-done((bf16[64,896]{1,0:T(8,128)(2,1)S(1)}, bf16[64,896]{1,0:T(8,128)(2,1)S(1)}, u32[]{:S(2)}, u32[]{:S(2)}) %collective-permute-start.21) | collective-permute-done | bytes 114720 | tf_op jit(solution)/shard_map/ppermute | solution.py:24
  75.9 2.5 %collective-permute-done.20.refs_2_ = bf16[64,896]{1,0:T(8,128)(2,1)S(1)} collective-permute-done((bf16[64,896]{1,0:T(8,128)(2,1)S(1)}, bf16[64,896]{1,0:T(8,128)(2,1)S(1)}, u32[]{:S(2)}, u32[]{:S(2)}) %collective-permute-start.20) | collective-permute-done | bytes 114720 | tf_op jit(solution)/shard_map/ppermute | solution.py:24
  80.9 2.8 %shard_map.121 = (bf16[32,2048]{1,0:T(8,128)(2,1)S(1)}, bf16[32,2048]{1,0:T(8,128)(2,1)S(1)}, bf16[32,2048]{1,0:T(8,128)(2,1)S(1)}, bf16[32,2048]{1,0:T(8,128)(2...) custom-call(s32[4]{0:T(128)S(1)} %pad_add_fusion.idx.refs_5_._, ...), custom_call_target="tpu_custom_call" | custom-call | flops 704643072 | bytes 3670016 | tf_op jit(solution)/shard_map/pallas_call | solution.py:35
  83.7 2.5 %collective-permute-start.26 = (bf16[32,2048]{1,0:T(8,128)(2,1)S(1)}, bf16[32,2048]{1,0:T(8,128)(2,1)S(1)}, u32[]{:S(2)}, u32[]{:S(2)}) collective-permute-start(bf16[32,2048]{1,0:T(8,128)(2,1)S(1)} %get-tuple-element.74), channel_id=1, source_target_pairs={{0,56},{8,0},{16,8},{24,16},{32,24},{40,32},{48,40},{56,48},{1,57}... | collective-permute-start | bytes 393224 | tf_op jit(solution)/shard_map/ppermute | solution.py:24
  88.3 3.4 %shard_map.120 = (bf16[32,2048]{1,0:T(8,128)(2,1)S(1)}, bf16[32,2048]{1,0:T(8,128)(2,1)S(1)}, bf16[32,2048]{1,0:T(8,128)(2,1)S(1)}, bf16[32,2048]{1,0:T(8,128)(2...) custom-call(s32[4]{0:T(128)S(1)} %pad_add_fusion.idx.refs_5_._, ...), custom_call_target="tpu_custom_call" | custom-call | flops 1174405120 | bytes 3670016 | tf_op jit(solution)/shard_map/pallas_call | solution.py:35
  91.7 3.3 %collective-permute-start.27 = (bf16[32,2048]{1,0:T(8,128)(2,1)S(1)}, bf16[32,2048]{1,0:T(8,128)(2,1)S(1)}, u32[]{:S(2)}, u32[]{:S(2)}) collective-permute-start(bf16[32,2048]{1,0:T(8,128)(2,1)S(1)} %shard_map.122), channel_id=1, source_target_pairs={{0,56},{8,0},{16,8},{24,16},{32,24},{40,32},{48,40},{56,48},{1,57}... | collective-permute-start | bytes 393224 | tf_op jit(solution)/shard_map/ppermute | solution.py:24
  98.8 2.6 %collective-permute-start.28 = (bf16[32,2048]{1,0:T(8,128)(2,1)S(1)}, bf16[32,2048]{1,0:T(8,128)(2,1)S(1)}, u32[]{:S(2)}, u32[]{:S(2)}) collective-permute-start(bf16[32,2048]{1,0:T(8,128)(2,1)S(1)} %shard_map.123), channel_id=1, source_target_pairs={{0,56},{8,0},{16,8},{24,16},{32,24},{40,32},{48,40},{56,48},{1,57}... | collective-permute-start | bytes 393224 | tf_op jit(solution)/shard_map/ppermute | solution.py:24
  104.0 2.5 %collective-permute-start.29 = (bf16[32,2048]{1,0:T(8,128)(2,1)S(1)}, bf16[32,2048]{1,0:T(8,128)(2,1)S(1)}, u32[]{:S(2)}, u32[]{:S(2)}) collective-permute-start(bf16[32,2048]{1,0:T(8,128)(2,1)S(1)} %shard_map.124), channel_id=1, source_target_pairs={{0,56},{8,0},{16,8},{24,16},{32,24},{40,32},{48,40},{56,48},{1,57}... | collective-permute-start | bytes 393224 | tf_op jit(solution)/shard_map/ppermute | solution.py:24
  115.3 4.0 %collective-permute-done.41.two = bf16[16,2048]{1,0:T(8,128)(2,1)S(1)} collective-permute-done((bf16[16,2048]{1,0:T(8,128)(2,1)S(1)}, bf16[16,2048]{1,0:T(8,128)(2,1)S(1)}, u32[]{:S(2)}, u32[]{:S(2)}) %collective-permute-start.41) | collective-permute-done | bytes 65568 | tf_op jit(solution)/shard_map/ppermute | solution.py:24
  (105 shorter events, 48.4 us)
Async XLA Ops:
  12.2 6.9 %collective-permute-start.6 = (bf16[64,2048]{1,0:T(8,128)(2,1)S(1)}, bf16[64,2048]{1,0:T(8,128)(2,1)S(1)}, u32[]{:S(2)}, u32[]{:S(2)}) collective-permute-start(bf16[64,2048]{1,0:T(8,128)(2,1)S(1)} %shard_map.111.refs_0_), channel_id=1, source_target_pairs={{0,56},{8,0},{16,8},{24,16},{32,24},{40,32},{48,40},{56,48},{1,57}... | collective-permute-start | bytes 786440 | tf_op jit(solution)/shard_map/ppermute | solution.py:24
  12.3 10.4 %collective-permute-start.3 = (bf16[64,2048]{1,0:T(8,128)(2,1)S(1)}, bf16[64,2048]{1,0:T(8,128)(2,1)S(1)}, u32[]{:S(2)}, u32[]{:S(2)}) collective-permute-start(bf16[64,2048]{1,0:T(8,128)(2,1)S(1)} %shard_map.111.refs_0_), channel_id=1, source_target_pairs={{0,8},{8,16},{16,24},{24,32},{32,40},{40,48},{48,56},{56,0},{1,9},... | collective-permute-start | bytes 786440 | tf_op jit(solution)/shard_map/ppermute | solution.py:24
  19.0 7.2 %collective-permute-start.7 = (bf16[64,2048]{1,0:T(8,128)(2,1)S(1)}, bf16[64,2048]{1,0:T(8,128)(2,1)S(1)}, u32[]{:S(2)}, u32[]{:S(2)}) collective-permute-start(bf16[64,2048]{1,0:T(8,128)(2,1)S(1)} %collective-permute-done.6.refs_2_), channel_id=1, source_target_pairs={{0,56},{8,0},{16,8},{24,16},{32,24},{40,32},{48,40},{56,48},{1,57}... | collective-permute-start | bytes 786440 | tf_op jit(solution)/shard_map/ppermute | solution.py:24
  22.8 7.6 %collective-permute-start.4 = (bf16[64,2048]{1,0:T(8,128)(2,1)S(1)}, bf16[64,2048]{1,0:T(8,128)(2,1)S(1)}, u32[]{:S(2)}, u32[]{:S(2)}) collective-permute-start(bf16[64,2048]{1,0:T(8,128)(2,1)S(1)} %collective-permute-done.3.refs_1_), channel_id=1, source_target_pairs={{0,8},{8,16},{16,24},{24,32},{32,40},{40,48},{48,56},{56,0},{1,9},... | collective-permute-start | bytes 786440 | tf_op jit(solution)/shard_map/ppermute | solution.py:24
  26.2 9.7 %collective-permute-start.8 = (bf16[64,2048]{1,0:T(8,128)(2,1)S(1)}, bf16[64,2048]{1,0:T(8,128)(2,1)S(1)}, u32[]{:S(2)}, u32[]{:S(2)}) collective-permute-start(bf16[64,2048]{1,0:T(8,128)(2,1)S(1)} %collective-permute-done.7.refs_4_.refs_0_), channel_id=1, source_target_pairs={{0,56},{8,0},{16,8},{24,16},{32,24},{40,32},{48,40},{56,48},{1,57}... | collective-permute-start | bytes 786440 | tf_op jit(solution)/shard_map/ppermute | solution.py:24
  30.4 7.7 %collective-permute-start.5 = (bf16[64,2048]{1,0:T(8,128)(2,1)S(1)}, bf16[64,2048]{1,0:T(8,128)(2,1)S(1)}, u32[]{:S(2)}, u32[]{:S(2)}) collective-permute-start(bf16[64,2048]{1,0:T(8,128)(2,1)S(1)} %collective-permute-done.4.refs_3_), channel_id=1, source_target_pairs={{0,8},{8,16},{16,24},{24,32},{32,40},{40,48},{48,56},{56,0},{1,9},... | collective-permute-start | bytes 786440 | tf_op jit(solution)/shard_map/ppermute | solution.py:24
  43.1 8.4 %collective-permute-start.9 = (bf16[128,1920]{1,0:T(8,128)(2,1)S(1)}, bf16[128,1920]{1,0:T(8,128)(2,1)S(1)}, u32[]{:S(2)}, u32[]{:S(2)}) collective-permute-start(bf16[128,1920]{1,0:T(8,128)(2,1)S(1)} %get-tuple-element.58), channel_id=1, source_target_pairs={{0,1},{1,0},{2,3},{3,2},{4,5},{5,4},{6,7},{7,6},{8,9},{9,8},{10,11... | collective-permute-start | bytes 1474568 | tf_op jit(solution)/shard_map/ppermute | solution.py:24
  52.2 8.1 %collective-permute-start.10 = (bf16[32,1920]{1,0:T(8,128)(2,1)S(1)}, bf16[32,1920]{1,0:T(8,128)(2,1)S(1)}, u32[]{:S(2)}, u32[]{:S(2)}) collective-permute-start(bf16[32,1920]{1,0:T(8,128)(2,1)S(1)} %get-tuple-element.60), channel_id=1, source_target_pairs={{0,2},{2,4},{4,6},{6,0},{1,3},{3,5},{5,7},{7,1},{8,10},{10,12},{12... | collective-permute-start | bytes 368648 | tf_op jit(solution)/shard_map/ppermute | solution.py:24
  53.8 9.6 %collective-permute-start.11 = (bf16[32,1920]{1,0:T(8,128)(2,1)S(1)}, bf16[32,1920]{1,0:T(8,128)(2,1)S(1)}, u32[]{:S(2)}, u32[]{:S(2)}) collective-permute-start(bf16[32,1920]{1,0:T(8,128)(2,1)S(1)} %get-tuple-element.61), channel_id=1, source_target_pairs={{0,4},{2,6},{4,0},{6,2},{1,5},{3,7},{5,1},{7,3},{8,12},{10,14},{12... | collective-permute-start | bytes 368648 | tf_op jit(solution)/shard_map/ppermute | solution.py:24
  58.8 7.3 %collective-permute-start.16 = (bf16[32,1920]{1,0:T(8,128)(2,1)S(1)}, bf16[32,1920]{1,0:T(8,128)(2,1)S(1)}, u32[]{:S(2)}, u32[]{:S(2)}) collective-permute-start(bf16[32,1920]{1,0:T(8,128)(2,1)S(1)} %get-tuple-element.70), channel_id=1, source_target_pairs={{0,2},{2,4},{4,6},{6,0},{1,3},{3,5},{5,7},{7,1},{8,10},{10,12},{12... | collective-permute-start | bytes 368648 | tf_op jit(solution)/shard_map/ppermute | solution.py:24
  59.5 8.8 %collective-permute-start.17 = (bf16[32,1920]{1,0:T(8,128)(2,1)S(1)}, bf16[32,1920]{1,0:T(8,128)(2,1)S(1)}, u32[]{:S(2)}, u32[]{:S(2)}) collective-permute-start(bf16[32,1920]{1,0:T(8,128)(2,1)S(1)} %get-tuple-element.71), channel_id=1, source_target_pairs={{0,4},{2,6},{4,0},{6,2},{1,5},{3,7},{5,1},{7,3},{8,12},{10,14},{12... | collective-permute-start | bytes 368648 | tf_op jit(solution)/shard_map/ppermute | solution.py:24
  60.3 8.0 %collective-permute-start.18 = (bf16[32,1920]{1,0:T(8,128)(2,1)S(1)}, bf16[32,1920]{1,0:T(8,128)(2,1)S(1)}, u32[]{:S(2)}, u32[]{:S(2)}) collective-permute-start(bf16[32,1920]{1,0:T(8,128)(2,1)S(1)} %get-tuple-element.72), channel_id=1, source_target_pairs={{0,6},{2,0},{4,2},{6,4},{1,7},{3,1},{5,3},{7,5},{8,14},{10,8},{12,... | collective-permute-start | bytes 368648 | tf_op jit(solution)/shard_map/ppermute | solution.py:24
  68.6 7.4 %collective-permute-start.21 = (bf16[64,896]{1,0:T(8,128)(2,1)S(1)}, bf16[64,896]{1,0:T(8,128)(2,1)S(1)}, u32[]{:S(2)}, u32[]{:S(2)}) collective-permute-start(bf16[64,896]{1,0:T(8,128)(2,1)S(1)} %shard_map.119.refs_0_), channel_id=1, source_target_pairs={{0,6},{2,0},{4,2},{6,4},{1,7},{3,1},{5,3},{7,5},{8,14},{10,8},{12,... | collective-permute-start | bytes 344072 | tf_op jit(solution)/shard_map/ppermute | solution.py:24
  71.0 7.4 %collective-permute-start.20 = (bf16[64,896]{1,0:T(8,128)(2,1)S(1)}, bf16[64,896]{1,0:T(8,128)(2,1)S(1)}, u32[]{:S(2)}, u32[]{:S(2)}) collective-permute-start(bf16[64,896]{1,0:T(8,128)(2,1)S(1)} %shard_map.119.refs_0_), channel_id=1, source_target_pairs={{0,4},{2,6},{4,0},{6,2},{1,5},{3,7},{5,1},{7,3},{8,12},{10,14},{12... | collective-permute-start | bytes 344072 | tf_op jit(solution)/shard_map/ppermute | solution.py:24
  72.1 7.5 %collective-permute-start.19 = (bf16[64,896]{1,0:T(8,128)(2,1)S(1)}, bf16[64,896]{1,0:T(8,128)(2,1)S(1)}, u32[]{:S(2)}, u32[]{:S(2)}) collective-permute-start(bf16[64,896]{1,0:T(8,128)(2,1)S(1)} %shard_map.119.refs_0_), channel_id=1, source_target_pairs={{0,2},{2,4},{4,6},{6,0},{1,3},{3,5},{5,7},{7,1},{8,10},{10,12},{12... | collective-permute-start | bytes 344072 | tf_op jit(solution)/shard_map/ppermute | solution.py:24
  72.7 6.9 %collective-permute-start.22 = (bf16[64,896]{1,0:T(8,128)(2,1)S(1)}, bf16[64,896]{1,0:T(8,128)(2,1)S(1)}, u32[]{:S(2)}, u32[]{:S(2)}) collective-permute-start(bf16[64,896]{1,0:T(8,128)(2,1)S(1)} %shard_map.119.refs_0_), channel_id=1, source_target_pairs={{0,1},{1,0},{2,3},{3,2},{4,5},{5,4},{6,7},{7,6},{8,9},{9,8},{10,11... | collective-permute-start | bytes 344072 | tf_op jit(solution)/shard_map/ppermute | solution.py:24
  83.7 8.0 %collective-permute-start.26 = (bf16[32,2048]{1,0:T(8,128)(2,1)S(1)}, bf16[32,2048]{1,0:T(8,128)(2,1)S(1)}, u32[]{:S(2)}, u32[]{:S(2)}) collective-permute-start(bf16[32,2048]{1,0:T(8,128)(2,1)S(1)} %get-tuple-element.74), channel_id=1, source_target_pairs={{0,56},{8,0},{16,8},{24,16},{32,24},{40,32},{48,40},{56,48},{1,57}... | collective-permute-start | bytes 393224 | tf_op jit(solution)/shard_map/ppermute | solution.py:24
  86.2 8.8 %collective-permute-start.34 = (bf16[32,2048]{1,0:T(8,128)(2,1)S(1)}, bf16[32,2048]{1,0:T(8,128)(2,1)S(1)}, u32[]{:S(2)}, u32[]{:S(2)}) collective-permute-start(bf16[32,2048]{1,0:T(8,128)(2,1)S(1)} %get-tuple-element.84), channel_id=1, source_target_pairs={{0,8},{8,16},{16,24},{24,32},{32,40},{40,48},{48,56},{56,0},{1,9},... | collective-permute-start | bytes 393224 | tf_op jit(solution)/shard_map/ppermute | solution.py:24
  86.2 8.9 %collective-permute-start.30 = (bf16[32,2048]{1,0:T(8,128)(2,1)S(1)}, bf16[32,2048]{1,0:T(8,128)(2,1)S(1)}, u32[]{:S(2)}, u32[]{:S(2)}) collective-permute-start(bf16[32,2048]{1,0:T(8,128)(2,1)S(1)} %get-tuple-element.78), channel_id=1, source_target_pairs={{0,8},{8,16},{16,24},{24,32},{32,40},{40,48},{48,56},{56,0},{1,9},... | collective-permute-start | bytes 393224 | tf_op jit(solution)/shard_map/ppermute | solution.py:24
  86.2 9.1 %collective-permute-start.38 = (bf16[32,2048]{1,0:T(8,128)(2,1)S(1)}, bf16[32,2048]{1,0:T(8,128)(2,1)S(1)}, u32[]{:S(2)}, u32[]{:S(2)}) collective-permute-start(bf16[32,2048]{1,0:T(8,128)(2,1)S(1)} %get-tuple-element.88), channel_id=1, source_target_pairs={{0,56},{8,0},{16,8},{24,16},{32,24},{40,32},{48,40},{56,48},{1,57}... | collective-permute-start | bytes 393224 | tf_op jit(solution)/shard_map/ppermute | solution.py:24
  91.7 7.1 %collective-permute-start.27 = (bf16[32,2048]{1,0:T(8,128)(2,1)S(1)}, bf16[32,2048]{1,0:T(8,128)(2,1)S(1)}, u32[]{:S(2)}, u32[]{:S(2)}) collective-permute-start(bf16[32,2048]{1,0:T(8,128)(2,1)S(1)} %shard_map.122), channel_id=1, source_target_pairs={{0,56},{8,0},{16,8},{24,16},{32,24},{40,32},{48,40},{56,48},{1,57}... | collective-permute-start | bytes 393224 | tf_op jit(solution)/shard_map/ppermute | solution.py:24
  95.2 7.8 %collective-permute-start.31 = (bf16[32,2048]{1,0:T(8,128)(2,1)S(1)}, bf16[32,2048]{1,0:T(8,128)(2,1)S(1)}, u32[]{:S(2)}, u32[]{:S(2)}) collective-permute-start(bf16[32,2048]{1,0:T(8,128)(2,1)S(1)} %shard_map.125), channel_id=1, source_target_pairs={{0,8},{8,16},{16,24},{24,32},{32,40},{40,48},{48,56},{56,0},{1,9},... | collective-permute-start | bytes 393224 | tf_op jit(solution)/shard_map/ppermute | solution.py:24
  95.3 8.1 %collective-permute-start.39 = (bf16[32,2048]{1,0:T(8,128)(2,1)S(1)}, bf16[32,2048]{1,0:T(8,128)(2,1)S(1)}, u32[]{:S(2)}, u32[]{:S(2)}) collective-permute-start(bf16[32,2048]{1,0:T(8,128)(2,1)S(1)} %shard_map.131), channel_id=1, source_target_pairs={{0,56},{8,0},{16,8},{24,16},{32,24},{40,32},{48,40},{56,48},{1,57}... | collective-permute-start | bytes 393224 | tf_op jit(solution)/shard_map/ppermute | solution.py:24
  101.4 6.9 %collective-permute-start.36 = (bf16[32,2048]{1,0:T(8,128)(2,1)S(1)}, bf16[32,2048]{1,0:T(8,128)(2,1)S(1)}, u32[]{:S(2)}, u32[]{:S(2)}) collective-permute-start(bf16[32,2048]{1,0:T(8,128)(2,1)S(1)} %shard_map.129), channel_id=1, source_target_pairs={{0,8},{8,16},{16,24},{24,32},{32,40},{40,48},{48,56},{56,0},{1,9},... | collective-permute-start | bytes 393224 | tf_op jit(solution)/shard_map/ppermute | solution.py:24
  (27 other events, 190.7 us)

commit v3 on v2

--- a/solution.py
+++ b/solution.py
@@ -135,22 +135,14 @@
 
 def place(core, pieces, part):
     top = part.shape[0] // 2
-    at = 0
-    spare = []
-    for piece in pieces:
+    for i, piece in enumerate(pieces):
         half = piece.shape[0] // 2
-        if piece.shape[0] < pieces[0].shape[0]:
-            spare.append(piece)
-            continue
+        at = i * half
         part[pl.ds(at, half), :] = piece[rows_at(core * half, half), :]
         part[pl.ds(top + at, half), :] = piece[rows_at((1 - core) * half, half), :]
-        at += half
-    for i, piece in enumerate(spare):
-        half = piece.shape[0]
-        part[rows_at(lax.rem(core + i, NC) * top + at, half), :] = piece[...]
-
-
-def squares(width, part, inv_gain2, keep, send):
+
+
+def squares(width, part, inv_gain2, keep, send, row):
     top = part.shape[0] // 2
     step = 32
     lane = lax.broadcasted_iota(jnp.int32, (step, MARKS), 1)
@@ -163,16 +155,17 @@
         high = sums.astype(jnp.bfloat16).astype(jnp.float32)
         marks = jnp.where(lane == 0, high, jnp.where(lane == 1, sums - high, 0.0))
         out = keep if i * step < top else send
-        out[pl.ds(i * step % top, step), pl.ds(2 * width, MARKS)] = marks.astype(jnp.bfloat16)
-
-
-def project(weights, base, part, keep, send):
+        out[pl.ds(row + i * step % top, step), pl.ds(2 * width, MARKS)] = marks.astype(jnp.bfloat16)
+
+
+def project(weights, base, part, keep, send, row):
     top, width = part.shape[0] // 2, weights.shape[1]
+    to = pl.ds(row, top)
 
     def tile(start, size):
         terms = jnp.dot(part[...], weights[:, pl.ds(start, size)], preferred_element_type=jnp.float32)
-        keep[:, pl.ds(base + start, size)] = terms[:top].astype(jnp.bfloat16)
-        send[:, pl.ds(base + start, size)] = terms[top:].astype(jnp.bfloat16)
+        keep[to, pl.ds(base + start, size)] = terms[:top].astype(jnp.bfloat16)
+        send[to, pl.ds(base + start, size)] = terms[top:].astype(jnp.bfloat16)
 
     pl.loop(0, width // 256)(lambda t: tile(pl.multiple_of(t * 256, 256), 256))
     if width % 256:
@@ -182,13 +175,32 @@
 def gate_matmul(width, idx, *refs):
     pieces, (_, inv_gain2, w_gate, keep, send, part, done) = refs[:-7], refs[-7:]
     place(idx[3], pieces, part)
-    squares(width, part, inv_gain2, keep, send)
-    project(w_gate, 0, part, keep, send)
+    squares(width, part, inv_gain2, keep, send, 0)
+    project(w_gate, 0, part, keep, send, 0)
     done[...] = jnp.zeros_like(done)
 
 
 def up_matmul(width, _, part, w_up, keep_in, send_in, keep, send):
-    project(w_up, width, part, keep, send)
+    project(w_up, width, part, keep, send, 0)
+
+
+def middle_matmul(width, idx, *refs):
+    pieces, (_, inv_gain2, w_gate, w_up, keep, send, _, part) = refs[:-8], refs[-8:]
+    place(idx[3], pieces, part)
+    squares(width, part, inv_gain2, keep, send, 0)
+    project(w_gate, 0, part, keep, send, 0)
+    project(w_up, width, part, keep, send, 0)
+
+
+def last_matmul(width, idx, low, high, inv_gain2, w_gate, w_up, keep_in, send_in, keep, send, part):
+    core = idx[3]
+    half = low.shape[0]
+    part[rows_at(core * half, half), :] = low[...]
+    part[rows_at((1 - core) * half, half), :] = high[...]
+    row = keep.shape[0] - half
+    squares(width, part, inv_gain2, keep, send, row)
+    project(w_gate, 0, part, keep, send, row)
+    project(w_up, width, part, keep, send, row)
 
 
 def halves(up, down, _, up_half, down_half):
@@ -344,7 +356,19 @@
 
     keep, send, part, done = gates([pieces[j] for j in ORDER[:EARLY]], pieces[2])
     up, down = call(halves, [shape(piece // 2, feats)] * 2, [up, down, done], "vvh", moved=4 * piece * feats)
+    late = [pieces[j] for j in ORDER[EARLY:-1]]
+    size = (NZ - EARLY) * piece
     keep, send = ups(keep, send, part, up)
+    later, send_later, send = call(
+        functools.partial(middle_matmul, width),
+        [shape(size // 2, wide)] * 2 + [shape(*send.shape)],
+        [idx] + late + [send, inv_gain2, w_gate, w_up],
+        "s" + "v" * (len(late) + 4),
+        scratch=[pltpu.VMEM((size - piece, feats), bf16)],
+        flops=4 * (size - piece) * feats * width,
+        moved=4 * feats * width,
+        alias={1 + len(late): 2},
+    )
     up = shift(up, "z", 1, NZ)
     down = shift(down, "z", -1, NZ)
 
@@ -361,9 +385,17 @@
         return [own] + [got[k] for k in range(1, NY)]
 
     early = across(keep, send)
-    keep, send, part, _ = gates([pieces[j] for j in ORDER[EARLY:-1]] + [up, down], idx)
-    keep, send = ups(keep, send, part, idx)
-    late = across(keep, send)
+    later, send_later = call(
+        functools.partial(last_matmul, width),
+        [shape(size // 2, wide)] * 2,
+        [idx, up, down, inv_gain2, w_gate, w_up, later, send_later],
+        "svvvvvvv",
+        scratch=[pltpu.VMEM((piece, feats), bf16)],
+        flops=4 * piece * feats * width,
+        moved=4 * feats * width,
+        alias={6: 0, 7: 1},
+    )
+    late = across(later, send_later)
     hidden = call(functools.partial(activate, width), shape(block, width), early + late, "v" * 2 * NY, moved=10 * block * wide)
     same = {0: hidden, **{k: shift(hidden, "y", k, NY) for k in AWAY}}
     other = {k: shift(v, "core", 1, NC) for k, v in same.items()}

time: 122 us -> 121 us (level)
  waiting for transfers between devices: 45.3 us -> 40.3 us
  starting transfers between devices: 51.2 us -> 53.9 us
  Pallas kernels: 21 us -> 22.7 us
    ppermute x43, waiting for transfers between devices: 45.3 us -> 40.3 us  [shift(): return lax.ppermute(v, axis, [(i, (i + by) % n) for i in range(n)])]
    ppermute x43, starting transfers between devices: 51.2 us -> 53.9 us  [shift(): return lax.ppermute(v, axis, [(i, (i + by) % n) for i in range(n)])]
    pallas_call x26, Pallas kernels: 21 us -> 22.7 us  [call(): pl.pallas_call(kernel, out_shape=whole, in_specs=[pl.BlockSpec(memory_spa...]
  transfers between devices with their start and end apart: 43 -> 43, of which waited for: 26 -> 23; matrix products, arithmetic and copies ran while one was open for 0% -> 0% of each run, Pallas kernels for 12% -> 14%
where the time goes in v3:
time: 121 us
  starting transfers between devices  53.9 us (45%)
  waiting for transfers between devices  40.3 us (33%)
  Pallas kernels  22.7 us (19%)
  local copies, waits for them, and re-layouts  3.63 us (3%)
    ppermute x43, starting transfers between devices, shift(): return lax.ppermute(v, axis, [(i, (i + by) % n) for i in range(n)])  53.9 us
    ppermute x43, waiting for transfers between devices, shift(): return lax.ppermute(v, axis, [(i, (i + by) % n) for i in range(n)])  40.3 us
    pallas_call x26, Pallas kernels, call(): pl.pallas_call(kernel, out_shape=whole, in_specs=[pl.BlockSpec(memory_spa...  22.7 us
    unnamed x16, local copies, waits for them, and re-layouts  3.63 us
  transfers between devices with their start and end apart: 43, of which 23 were waited for; matrix products, arithmetic and copies ran while one was open for 0% of the time, Pallas kernels for 14%

profile of v3, /device:TPU:32, one launch (start us, length us, event | category | flops | bytes accessed | tf_op | source)
XLA Modules:
  0.0 120.9 jit_solution(2528623719331827717)
XLA Ops:
  0.0 2.6 %shard_map.109 = (f32[16,2048]{1,0:T(8,128)}, f32[16,128]{1,0:T(8,128)}, bf16[16,2048]{1,0:T(8,128)(2,1)}) custom-call(s32[16]{0:T(128)} %lengths_in.1, bf16[16,2048]{1,0:T(8,128)(2,1)} %hidden_in.1, bf16[16,2048]{1,0:T(8,128)(2,1)} %queries_in.1, bf16[16,128,128]{2,1,0:T(8,128)(2,1)} %keys_in.1, bf16[16,128,128]{2,1,0:T(8,128)(2,1)} %values_in.1, ...), custom_call_target="tpu_custom_call" | custom-call | bytes 1048576 | tf_op jit(solution)/shard_map/pallas_call | solution.py:35
  2.6 2.8 %collective-permute-start.2 = (bf16[16,2048]{1,0:T(8,128)(2,1)}, bf16[16,2048]{1,0:T(8,128)(2,1)S(1)}, u32[]{:S(2)}, u32[]{:S(2)}) collective-permute-start(bf16[16,2048]{1,0:T(8,128)(2,1)} %get-tuple-element.50.own), channel_id=1, source_target_pairs={{0,192},{64,0},{128,64},{192,128},{1,193},{65,1},{129,65},{193,129... | collective-permute-start | bytes 196616 | tf_op jit(solution)/shard_map/ppermute | solution.py:24
  8.0 3.4 %collective-permute-done.1.refs_1_ = bf16[16,2048]{1,0:T(8,128)(2,1)S(1)} collective-permute-done((bf16[16,2048]{1,0:T(8,128)(2,1)}, bf16[16,2048]{1,0:T(8,128)(2,1)S(1)}, u32[]{:S(2)}, u32[]{:S(2)}) %collective-permute-start.1) | collective-permute-done | bytes 65568 | tf_op jit(solution)/shard_map/ppermute | solution.py:24
  14.3 4.8 %collective-permute-done.6.refs_2_ = bf16[64,2048]{1,0:T(8,128)(2,1)S(1)} collective-permute-done((bf16[64,2048]{1,0:T(8,128)(2,1)S(1)}, bf16[64,2048]{1,0:T(8,128)(2,1)S(1)}, u32[]{:S(2)}, u32[]{:S(2)}) %collective-permute-start.6) | collective-permute-done | bytes 262176 | tf_op jit(solution)/shard_map/ppermute | solution.py:24
  19.0 3.3 %collective-permute-start.7 = (bf16[64,2048]{1,0:T(8,128)(2,1)S(1)}, bf16[64,2048]{1,0:T(8,128)(2,1)S(1)}, u32[]{:S(2)}, u32[]{:S(2)}) collective-permute-start(bf16[64,2048]{1,0:T(8,128)(2,1)S(1)} %collective-permute-done.6.refs_2_), channel_id=1, source_target_pairs={{0,56},{8,0},{16,8},{24,16},{32,24},{40,32},{48,40},{56,48},{1,57}... | collective-permute-start | bytes 786440 | tf_op jit(solution)/shard_map/ppermute | solution.py:24
  22.8 3.4 %collective-permute-done.7.refs_4_.refs_0_ = bf16[64,2048]{1,0:T(8,128)(2,1)S(1)} collective-permute-done((bf16[64,2048]{1,0:T(8,128)(2,1)S(1)}, bf16[64,2048]{1,0:T(8,128)(2,1)S(1)}, u32[]{:S(2)}, u32[]{:S(2)}) %collective-permute-start.7) | collective-permute-done | bytes 262176 | tf_op jit(solution)/shard_map/ppermute | solution.py:24
  26.2 3.7 %collective-permute-start.8 = (bf16[64,2048]{1,0:T(8,128)(2,1)S(1)}, bf16[64,2048]{1,0:T(8,128)(2,1)S(1)}, u32[]{:S(2)}, u32[]{:S(2)}) collective-permute-start(bf16[64,2048]{1,0:T(8,128)(2,1)S(1)} %collective-permute-done.7.refs_4_.refs_0_), channel_id=1, source_target_pairs={{0,56},{8,0},{16,8},{24,16},{32,24},{40,32},{48,40},{56,48},{1,57}... | collective-permute-start | bytes 786440 | tf_op jit(solution)/shard_map/ppermute | solution.py:24
  33.2 2.7 %shard_map.112 = (bf16[128,1920]{1,0:T(8,128)(2,1)S(1)}, bf16[128,1920]{1,0:T(8,128)(2,1)S(1)}, bf16[256,2048]{1,0:T(8,128)(2,1)S(1)}, f32[8,128]{1,0:T(8,128)S(1)}) custom-call(s32[4]{0:T(128)S(1)} %pad_add_fusion.idx, bf16[64,2048]{1,0:T(8,128)(2,1)S(1)} %shard_map.111.refs_0_, bf16[64,2048]{1,0:T(8,128)(2,1)S(1)} %collective-permute-done.3.refs_1_, ...), custom_call_target="tpu_custom_call" | custom-call | flops 939524096 | bytes 3670016 | tf_op jit(solution)/shard_map/pallas_call | solution.py:35
  38.1 3.3 %collective-permute-start.14 = (bf16[32,2048]{1,0:T(8,128)(2,1)S(1)}, bf16[32,2048]{1,0:T(8,128)(2,1)S(1)}, u32[]{:S(2)}, u32[]{:S(2)}) collective-permute-start(bf16[32,2048]{1,0:T(8,128)(2,1)S(1)} %get-tuple-element.64), channel_id=1, source_target_pairs={{0,56},{8,0},{16,8},{24,16},{32,24},{40,32},{48,40},{56,48},{1,57}... | collective-permute-start | bytes 393224 | tf_op jit(solution)/shard_map/ppermute | solution.py:24
  43.2 3.9 %shard_map.115 = (bf16[128,1920]{1,0:T(8,128)(2,1)S(1)}, bf16[128,1920]{1,0:T(8,128)(2,1)S(1)}, bf16[128,1920]{1,0:T(8,128)(2,1)S(1)}) custom-call(s32[4]{0:T(128)S(1)} %pad_add_fusion.idx, bf16[64,2048]{1,0:T(8,128)(2,1)S(1)} %collective-permute-done.7.refs_4_.refs_0_, ...), custom_call_target="tpu_custom_call", output_to_operand_aliasing={{2}: (4, {})} | custom-call | flops 1409286144 | bytes 7340032 | tf_op jit(solution)/shard_map/pallas_call | solution.py:35
  47.3 3.0 %shard_map.117 = (bf16[128,1920]{1,0:T(8,128)(2,1)S(1)}, bf16[128,1920]{1,0:T(8,128)(2,1)S(1)}) custom-call(s32[4]{0:T(128)S(1)} %pad_add_fusion.idx, bf16[32,2048]{1,0:T(8,128)(2,1)S(1)} %collective-permute-done.13.low, bf16[32,2048]{1,0:T(8,128)(2,1)S(1)} %collective-permute-done.14.high, ...), custom_call_target="tpu_custom_call", output_to_operand_aliasing={{0}: (6, {}), {1}: (7, {})} | custom-call | flops 469762048 | bytes 7340032 | tf_op jit(solution)/shard_map/pallas_call | solution.py:35
  53.2 2.9 %collective-permute-start.11 = (bf16[32,1920]{1,0:T(8,128)(2,1)S(1)}, bf16[32,1920]{1,0:T(8,128)(2,1)S(1)}, u32[]{:S(2)}, u32[]{:S(2)}) collective-permute-start(bf16[32,1920]{1,0:T(8,128)(2,1)S(1)} %get-tuple-element.62), channel_id=1, source_target_pairs={{0,4},{2,6},{4,0},{6,2},{1,5},{3,7},{5,1},{7,3},{8,12},{10,14},{12... | collective-permute-start | bytes 368648 | tf_op jit(solution)/shard_map/ppermute | solution.py:24
  62.9 2.7 %collective-permute-done.16.refs_5_ = bf16[32,1920]{1,0:T(8,128)(2,1)S(1)} collective-permute-done((bf16[32,1920]{1,0:T(8,128)(2,1)S(1)}, bf16[32,1920]{1,0:T(8,128)(2,1)S(1)}, u32[]{:S(2)}, u32[]{:S(2)}) %collective-permute-start.16) | collective-permute-done | bytes 122912 | tf_op jit(solution)/shard_map/ppermute | solution.py:24
  71.5 2.8 %collective-permute-done.21.refs_3_ = bf16[64,896]{1,0:T(8,128)(2,1)S(1)} collective-permute-done((bf16[64,896]{1,0:T(8,128)(2,1)S(1)}, bf16[64,896]{1,0:T(8,128)(2,1)S(1)}, u32[]{:S(2)}, u32[]{:S(2)}) %collective-permute-start.21) | collective-permute-done | bytes 114720 | tf_op jit(solution)/shard_map/ppermute | solution.py:24
  74.3 2.5 %collective-permute-done.20.refs_2_ = bf16[64,896]{1,0:T(8,128)(2,1)S(1)} collective-permute-done((bf16[64,896]{1,0:T(8,128)(2,1)S(1)}, bf16[64,896]{1,0:T(8,128)(2,1)S(1)}, u32[]{:S(2)}, u32[]{:S(2)}) %collective-permute-start.20) | collective-permute-done | bytes 114720 | tf_op jit(solution)/shard_map/ppermute | solution.py:24
  79.1 2.8 %shard_map.121 = (bf16[32,2048]{1,0:T(8,128)(2,1)S(1)}, bf16[32,2048]{1,0:T(8,128)(2,1)S(1)}, bf16[32,2048]{1,0:T(8,128)(2,1)S(1)}, bf16[32,2048]{1,0:T(8,128)(2...) custom-call(s32[4]{0:T(128)S(1)} %pad_add_fusion.idx, bf16[64,896]{1,0:T(8,128)(2,1)S(1)} %shard_map.119.refs_0_, ...), custom_call_target="tpu_custom_call" | custom-call | flops 704643072 | bytes 3670016 | tf_op jit(solution)/shard_map/pallas_call | solution.py:35
  86.4 3.4 %shard_map.120 = (bf16[32,2048]{1,0:T(8,128)(2,1)S(1)}, bf16[32,2048]{1,0:T(8,128)(2,1)S(1)}, bf16[32,2048]{1,0:T(8,128)(2,1)S(1)}, bf16[32,2048]{1,0:T(8,128)(2...) custom-call(s32[4]{0:T(128)S(1)} %pad_add_fusion.idx, ...), custom_call_target="tpu_custom_call" | custom-call | flops 1174405120 | bytes 3670016 | tf_op jit(solution)/shard_map/pallas_call | solution.py:35
  89.9 3.3 %collective-permute-start.27 = (bf16[32,2048]{1,0:T(8,128)(2,1)S(1)}, bf16[32,2048]{1,0:T(8,128)(2,1)S(1)}, u32[]{:S(2)}, u32[]{:S(2)}) collective-permute-start(bf16[32,2048]{1,0:T(8,128)(2,1)S(1)} %shard_map.122), channel_id=1, source_target_pairs={{0,56},{8,0},{16,8},{24,16},{32,24},{40,32},{48,40},{56,48},{1,57}... | collective-permute-start | bytes 393224 | tf_op jit(solution)/shard_map/ppermute | solution.py:24
  93.6 2.4 %collective-permute-start.39 = (bf16[32,2048]{1,0:T(8,128)(2,1)S(1)}, bf16[32,2048]{1,0:T(8,128)(2,1)S(1)}, u32[]{:S(2)}, u32[]{:S(2)}) collective-permute-start(bf16[32,2048]{1,0:T(8,128)(2,1)S(1)} %shard_map.131), channel_id=1, source_target_pairs={{0,56},{8,0},{16,8},{24,16},{32,24},{40,32},{48,40},{56,48},{1,57}... | collective-permute-start | bytes 393224 | tf_op jit(solution)/shard_map/ppermute | solution.py:24
  96.4 2.9 %collective-permute-start.28 = (bf16[32,2048]{1,0:T(8,128)(2,1)S(1)}, bf16[32,2048]{1,0:T(8,128)(2,1)S(1)}, u32[]{:S(2)}, u32[]{:S(2)}) collective-permute-start(bf16[32,2048]{1,0:T(8,128)(2,1)S(1)} %shard_map.123), channel_id=1, source_target_pairs={{0,56},{8,0},{16,8},{24,16},{32,24},{40,32},{48,40},{56,48},{1,57}... | collective-permute-start | bytes 393224 | tf_op jit(solution)/shard_map/ppermute | solution.py:24
  101.9 2.5 %collective-permute-start.29 = (bf16[32,2048]{1,0:T(8,128)(2,1)S(1)}, bf16[32,2048]{1,0:T(8,128)(2,1)S(1)}, u32[]{:S(2)}, u32[]{:S(2)}) collective-permute-start(bf16[32,2048]{1,0:T(8,128)(2,1)S(1)} %shard_map.124), channel_id=1, source_target_pairs={{0,56},{8,0},{16,8},{24,16},{32,24},{40,32},{48,40},{56,48},{1,57}... | collective-permute-start | bytes 393224 | tf_op jit(solution)/shard_map/ppermute | solution.py:24
  104.4 3.4 %collective-permute-start.40 = (bf16[32,2048]{1,0:T(8,128)(2,1)S(1)}, bf16[32,2048]{1,0:T(8,128)(2,1)S(1)}, u32[]{:S(2)}, u32[]{:S(2)}) collective-permute-start(bf16[32,2048]{1,0:T(8,128)(2,1)S(1)} %shard_map.132), channel_id=1, source_target_pairs={{0,56},{8,0},{16,8},{24,16},{32,24},{40,32},{48,40},{56,48},{1,57}... | collective-permute-start | bytes 393224 | tf_op jit(solution)/shard_map/ppermute | solution.py:24
  110.3 2.6 %collective-permute-done.37.one = bf16[32,2048]{1,0:T(8,128)(2,1)S(1)} collective-permute-done((bf16[32,2048]{1,0:T(8,128)(2,1)S(1)}, bf16[32,2048]{1,0:T(8,128)(2,1)S(1)}, u32[]{:S(2)}, u32[]{:S(2)}) %collective-permute-start.37) | collective-permute-done | bytes 131104 | tf_op jit(solution)/shard_map/ppermute | solution.py:24
  114.8 4.0 %collective-permute-done.41.two = bf16[16,2048]{1,0:T(8,128)(2,1)S(1)} collective-permute-done((bf16[16,2048]{1,0:T(8,128)(2,1)S(1)}, bf16[16,2048]{1,0:T(8,128)(2,1)S(1)}, u32[]{:S(2)}, u32[]{:S(2)}) %collective-permute-start.41) | collective-permute-done | bytes 65568 | tf_op jit(solution)/shard_map/ppermute | solution.py:24
  (105 shorter events, 45.4 us)
Async XLA Ops:
  12.2 6.9 %collective-permute-start.6 = (bf16[64,2048]{1,0:T(8,128)(2,1)S(1)}, bf16[64,2048]{1,0:T(8,128)(2,1)S(1)}, u32[]{:S(2)}, u32[]{:S(2)}) collective-permute-start(bf16[64,2048]{1,0:T(8,128)(2,1)S(1)} %shard_map.111.refs_0_), channel_id=1, source_target_pairs={{0,56},{8,0},{16,8},{24,16},{32,24},{40,32},{48,40},{56,48},{1,57}... | collective-permute-start | bytes 786440 | tf_op jit(solution)/shard_map/ppermute | solution.py:24
  12.3 10.4 %collective-permute-start.3 = (bf16[64,2048]{1,0:T(8,128)(2,1)S(1)}, bf16[64,2048]{1,0:T(8,128)(2,1)S(1)}, u32[]{:S(2)}, u32[]{:S(2)}) collective-permute-start(bf16[64,2048]{1,0:T(8,128)(2,1)S(1)} %shard_map.111.refs_0_), channel_id=1, source_target_pairs={{0,8},{8,16},{16,24},{24,32},{32,40},{40,48},{48,56},{56,0},{1,9},... | collective-permute-start | bytes 786440 | tf_op jit(solution)/shard_map/ppermute | solution.py:24
  19.0 7.2 %collective-permute-start.7 = (bf16[64,2048]{1,0:T(8,128)(2,1)S(1)}, bf16[64,2048]{1,0:T(8,128)(2,1)S(1)}, u32[]{:S(2)}, u32[]{:S(2)}) collective-permute-start(bf16[64,2048]{1,0:T(8,128)(2,1)S(1)} %collective-permute-done.6.refs_2_), channel_id=1, source_target_pairs={{0,56},{8,0},{16,8},{24,16},{32,24},{40,32},{48,40},{56,48},{1,57}... | collective-permute-start | bytes 786440 | tf_op jit(solution)/shard_map/ppermute | solution.py:24
  22.8 7.6 %collective-permute-start.4 = (bf16[64,2048]{1,0:T(8,128)(2,1)S(1)}, bf16[64,2048]{1,0:T(8,128)(2,1)S(1)}, u32[]{:S(2)}, u32[]{:S(2)}) collective-permute-start(bf16[64,2048]{1,0:T(8,128)(2,1)S(1)} %collective-permute-done.3.refs_1_), channel_id=1, source_target_pairs={{0,8},{8,16},{16,24},{24,32},{32,40},{40,48},{48,56},{56,0},{1,9},... | collective-permute-start | bytes 786440 | tf_op jit(solution)/shard_map/ppermute | solution.py:24
  26.2 9.7 %collective-permute-start.8 = (bf16[64,2048]{1,0:T(8,128)(2,1)S(1)}, bf16[64,2048]{1,0:T(8,128)(2,1)S(1)}, u32[]{:S(2)}, u32[]{:S(2)}) collective-permute-start(bf16[64,2048]{1,0:T(8,128)(2,1)S(1)} %collective-permute-done.7.refs_4_.refs_0_), channel_id=1, source_target_pairs={{0,56},{8,0},{16,8},{24,16},{32,24},{40,32},{48,40},{56,48},{1,57}... | collective-permute-start | bytes 786440 | tf_op jit(solution)/shard_map/ppermute | solution.py:24
  30.4 7.7 %collective-permute-start.5 = (bf16[64,2048]{1,0:T(8,128)(2,1)S(1)}, bf16[64,2048]{1,0:T(8,128)(2,1)S(1)}, u32[]{:S(2)}, u32[]{:S(2)}) collective-permute-start(bf16[64,2048]{1,0:T(8,128)(2,1)S(1)} %collective-permute-done.4.refs_3_), channel_id=1, source_target_pairs={{0,8},{8,16},{16,24},{24,32},{32,40},{40,48},{48,56},{56,0},{1,9},... | collective-permute-start | bytes 786440 | tf_op jit(solution)/shard_map/ppermute | solution.py:24
  38.1 9.2 %collective-permute-start.14 = (bf16[32,2048]{1,0:T(8,128)(2,1)S(1)}, bf16[32,2048]{1,0:T(8,128)(2,1)S(1)}, u32[]{:S(2)}, u32[]{:S(2)}) collective-permute-start(bf16[32,2048]{1,0:T(8,128)(2,1)S(1)} %get-tuple-element.64), channel_id=1, source_target_pairs={{0,56},{8,0},{16,8},{24,16},{32,24},{40,32},{48,40},{56,48},{1,57}... | collective-permute-start | bytes 393224 | tf_op jit(solution)/shard_map/ppermute | solution.py:24
  50.3 7.1 %collective-permute-start.15 = (bf16[128,1920]{1,0:T(8,128)(2,1)S(1)}, bf16[128,1920]{1,0:T(8,128)(2,1)S(1)}, u32[]{:S(2)}, u32[]{:S(2)}) collective-permute-start(bf16[128,1920]{1,0:T(8,128)(2,1)S(1)} %get-tuple-element.68), channel_id=1, source_target_pairs={{0,1},{1,0},{2,3},{3,2},{4,5},{5,4},{6,7},{7,6},{8,9},{9,8},{10,11... | collective-permute-start | bytes 1474568 | tf_op jit(solution)/shard_map/ppermute | solution.py:24
  51.5 8.1 %collective-permute-start.10 = (bf16[32,1920]{1,0:T(8,128)(2,1)S(1)}, bf16[32,1920]{1,0:T(8,128)(2,1)S(1)}, u32[]{:S(2)}, u32[]{:S(2)}) collective-permute-start(bf16[32,1920]{1,0:T(8,128)(2,1)S(1)} %get-tuple-element.61), channel_id=1, source_target_pairs={{0,2},{2,4},{4,6},{6,0},{1,3},{3,5},{5,7},{7,1},{8,10},{10,12},{12... | collective-permute-start | bytes 368648 | tf_op jit(solution)/shard_map/ppermute | solution.py:24
  53.2 9.7 %collective-permute-start.11 = (bf16[32,1920]{1,0:T(8,128)(2,1)S(1)}, bf16[32,1920]{1,0:T(8,128)(2,1)S(1)}, u32[]{:S(2)}, u32[]{:S(2)}) collective-permute-start(bf16[32,1920]{1,0:T(8,128)(2,1)S(1)} %get-tuple-element.62), channel_id=1, source_target_pairs={{0,4},{2,6},{4,0},{6,2},{1,5},{3,7},{5,1},{7,3},{8,12},{10,14},{12... | collective-permute-start | bytes 368648 | tf_op jit(solution)/shard_map/ppermute | solution.py:24
  56.1 6.8 %collective-permute-start.12 = (bf16[32,1920]{1,0:T(8,128)(2,1)S(1)}, bf16[32,1920]{1,0:T(8,128)(2,1)S(1)}, u32[]{:S(2)}, u32[]{:S(2)}) collective-permute-start(bf16[32,1920]{1,0:T(8,128)(2,1)S(1)} %get-tuple-element.63), channel_id=1, source_target_pairs={{0,6},{2,0},{4,2},{6,4},{1,7},{3,1},{5,3},{7,5},{8,14},{10,8},{12,... | collective-permute-start | bytes 368648 | tf_op jit(solution)/shard_map/ppermute | solution.py:24
  58.1 7.5 %collective-permute-start.16 = (bf16[32,1920]{1,0:T(8,128)(2,1)S(1)}, bf16[32,1920]{1,0:T(8,128)(2,1)S(1)}, u32[]{:S(2)}, u32[]{:S(2)}) collective-permute-start(bf16[32,1920]{1,0:T(8,128)(2,1)S(1)} %get-tuple-element.70), channel_id=1, source_target_pairs={{0,2},{2,4},{4,6},{6,0},{1,3},{3,5},{5,7},{7,1},{8,10},{10,12},{12... | collective-permute-start | bytes 368648 | tf_op jit(solution)/shard_map/ppermute | solution.py:24
  58.9 8.4 %collective-permute-start.17 = (bf16[32,1920]{1,0:T(8,128)(2,1)S(1)}, bf16[32,1920]{1,0:T(8,128)(2,1)S(1)}, u32[]{:S(2)}, u32[]{:S(2)}) collective-permute-start(bf16[32,1920]{1,0:T(8,128)(2,1)S(1)} %get-tuple-element.71), channel_id=1, source_target_pairs={{0,4},{2,6},{4,0},{6,2},{1,5},{3,7},{5,1},{7,3},{8,12},{10,14},{12... | collective-permute-start | bytes 368648 | tf_op jit(solution)/shard_map/ppermute | solution.py:24
  59.7 7.6 %collective-permute-start.18 = (bf16[32,1920]{1,0:T(8,128)(2,1)S(1)}, bf16[32,1920]{1,0:T(8,128)(2,1)S(1)}, u32[]{:S(2)}, u32[]{:S(2)}) collective-permute-start(bf16[32,1920]{1,0:T(8,128)(2,1)S(1)} %get-tuple-element.72), channel_id=1, source_target_pairs={{0,6},{2,0},{4,2},{6,4},{1,7},{3,1},{5,3},{7,5},{8,14},{10,8},{12,... | collective-permute-start | bytes 368648 | tf_op jit(solution)/shard_map/ppermute | solution.py:24
  69.9 6.9 %collective-permute-start.20 = (bf16[64,896]{1,0:T(8,128)(2,1)S(1)}, bf16[64,896]{1,0:T(8,128)(2,1)S(1)}, u32[]{:S(2)}, u32[]{:S(2)}) collective-permute-start(bf16[64,896]{1,0:T(8,128)(2,1)S(1)} %shard_map.119.refs_0_), channel_id=1, source_target_pairs={{0,4},{2,6},{4,0},{6,2},{1,5},{3,7},{5,1},{7,3},{8,12},{10,14},{12... | collective-permute-start | bytes 344072 | tf_op jit(solution)/shard_map/ppermute | solution.py:24
  70.8 7.0 %collective-permute-start.19 = (bf16[64,896]{1,0:T(8,128)(2,1)S(1)}, bf16[64,896]{1,0:T(8,128)(2,1)S(1)}, u32[]{:S(2)}, u32[]{:S(2)}) collective-permute-start(bf16[64,896]{1,0:T(8,128)(2,1)S(1)} %shard_map.119.refs_0_), channel_id=1, source_target_pairs={{0,2},{2,4},{4,6},{6,0},{1,3},{3,5},{5,7},{7,1},{8,10},{10,12},{12... | collective-permute-start | bytes 344072 | tf_op jit(solution)/shard_map/ppermute | solution.py:24
  81.9 7.9 %collective-permute-start.26 = (bf16[32,2048]{1,0:T(8,128)(2,1)S(1)}, bf16[32,2048]{1,0:T(8,128)(2,1)S(1)}, u32[]{:S(2)}, u32[]{:S(2)}) collective-permute-start(bf16[32,2048]{1,0:T(8,128)(2,1)S(1)} %get-tuple-element.74), channel_id=1, source_target_pairs={{0,56},{8,0},{16,8},{24,16},{32,24},{40,32},{48,40},{56,48},{1,57}... | collective-permute-start | bytes 393224 | tf_op jit(solution)/shard_map/ppermute | solution.py:24
  84.0 9.2 %collective-permute-start.34 = (bf16[32,2048]{1,0:T(8,128)(2,1)S(1)}, bf16[32,2048]{1,0:T(8,128)(2,1)S(1)}, u32[]{:S(2)}, u32[]{:S(2)}) collective-permute-start(bf16[32,2048]{1,0:T(8,128)(2,1)S(1)} %get-tuple-element.84), channel_id=1, source_target_pairs={{0,8},{8,16},{16,24},{24,32},{32,40},{40,48},{48,56},{56,0},{1,9},... | collective-permute-start | bytes 393224 | tf_op jit(solution)/shard_map/ppermute | solution.py:24
  84.0 9.3 %collective-permute-start.30 = (bf16[32,2048]{1,0:T(8,128)(2,1)S(1)}, bf16[32,2048]{1,0:T(8,128)(2,1)S(1)}, u32[]{:S(2)}, u32[]{:S(2)}) collective-permute-start(bf16[32,2048]{1,0:T(8,128)(2,1)S(1)} %get-tuple-element.78), channel_id=1, source_target_pairs={{0,8},{8,16},{16,24},{24,32},{32,40},{40,48},{48,56},{56,0},{1,9},... | collective-permute-start | bytes 393224 | tf_op jit(solution)/shard_map/ppermute | solution.py:24
  84.5 9.0 %collective-permute-start.38 = (bf16[32,2048]{1,0:T(8,128)(2,1)S(1)}, bf16[32,2048]{1,0:T(8,128)(2,1)S(1)}, u32[]{:S(2)}, u32[]{:S(2)}) collective-permute-start(bf16[32,2048]{1,0:T(8,128)(2,1)S(1)} %get-tuple-element.88), channel_id=1, source_target_pairs={{0,56},{8,0},{16,8},{24,16},{32,24},{40,32},{48,40},{56,48},{1,57}... | collective-permute-start | bytes 393224 | tf_op jit(solution)/shard_map/ppermute | solution.py:24
  93.4 7.5 %collective-permute-start.31 = (bf16[32,2048]{1,0:T(8,128)(2,1)S(1)}, bf16[32,2048]{1,0:T(8,128)(2,1)S(1)}, u32[]{:S(2)}, u32[]{:S(2)}) collective-permute-start(bf16[32,2048]{1,0:T(8,128)(2,1)S(1)} %shard_map.125), channel_id=1, source_target_pairs={{0,8},{8,16},{16,24},{24,32},{32,40},{40,48},{48,56},{56,0},{1,9},... | collective-permute-start | bytes 393224 | tf_op jit(solution)/shard_map/ppermute | solution.py:24
  93.6 7.8 %collective-permute-start.39 = (bf16[32,2048]{1,0:T(8,128)(2,1)S(1)}, bf16[32,2048]{1,0:T(8,128)(2,1)S(1)}, u32[]{:S(2)}, u32[]{:S(2)}) collective-permute-start(bf16[32,2048]{1,0:T(8,128)(2,1)S(1)} %shard_map.131), channel_id=1, source_target_pairs={{0,56},{8,0},{16,8},{24,16},{32,24},{40,32},{48,40},{56,48},{1,57}... | collective-permute-start | bytes 393224 | tf_op jit(solution)/shard_map/ppermute | solution.py:24
  99.4 8.5 %collective-permute-start.36 = (bf16[32,2048]{1,0:T(8,128)(2,1)S(1)}, bf16[32,2048]{1,0:T(8,128)(2,1)S(1)}, u32[]{:S(2)}, u32[]{:S(2)}) collective-permute-start(bf16[32,2048]{1,0:T(8,128)(2,1)S(1)} %shard_map.129), channel_id=1, source_target_pairs={{0,8},{8,16},{16,24},{24,32},{32,40},{40,48},{48,56},{56,0},{1,9},... | collective-permute-start | bytes 393224 | tf_op jit(solution)/shard_map/ppermute | solution.py:24
  101.0 6.9 %collective-permute-start.32 = (bf16[32,2048]{1,0:T(8,128)(2,1)S(1)}, bf16[32,2048]{1,0:T(8,128)(2,1)S(1)}, u32[]{:S(2)}, u32[]{:S(2)}) collective-permute-start(bf16[32,2048]{1,0:T(8,128)(2,1)S(1)} %shard_map.126), channel_id=1, source_target_pairs={{0,8},{8,16},{16,24},{24,32},{32,40},{40,48},{48,56},{56,0},{1,9},... | collective-permute-start | bytes 393224 | tf_op jit(solution)/shard_map/ppermute | solution.py:24
  (27 other events, 187.9 us)

commit v4 on v3

--- a/solution.py
+++ b/solution.py
@@ -16,7 +16,6 @@
 MIB = 1 << 20
 ORDER = (0, -1, 1, -2, 2, -3, 3, 4)
 EARLY = 4
-FAR = 5
 AWAY = (2, 1, 3)
 
 
@@ -122,8 +121,9 @@
         out[:, cols] = (got * scales[h : h + 1, :]).astype(bf16)
 
 
-def seat(own, out):
+def seat(own, inv_gain2, out, kept):
     out[pl.ds(0, own.shape[0]), :] = own[...]
+    kept[...] = inv_gain2[...]
 
 
 def join(first, *refs):
@@ -234,32 +234,30 @@
         hidden[pl.ds(i * block, block), :] = (gate / (1.0 + jnp.exp(-gate)) * up).astype(jnp.bfloat16)
 
 
-def second_matmul(first, last, idx, *refs):
+def second_matmul(groups, ranges, idx, *refs):
     same, refs = refs[:NY], refs[NY:]
     other, refs = refs[:NY], refs[NY:]
     weights, outs, hidden = refs[0], refs[1:-1], refs[-1]
     mine, core = idx[2], idx[3]
     block = same[0].shape[0]
     half = block // 2
-    groups = range(first // NY, 2)
     for k in range(NY):
         y = lax.rem(mine - k + NY, NY)
-        for i in groups:
-            at = ((i - groups[0]) * NY + y) * block
+        for g, i in enumerate(groups):
+            at = (g * NY + y) * block
             hidden[rows_at(at + core * half, half), :] = same[k][pl.ds(i * half, half), :]
             hidden[rows_at(at + (1 - core) * half, half), :] = other[k][pl.ds(i * half, half), :]
-    some = pl.ds((first - groups[0] * NY) * block, (last - first) * block)
 
     @pl.loop(0, weights.shape[1] // 256)
     def _(t):
         cols = pl.ds(pl.multiple_of(t * 256, 256), 256)
-        terms = jnp.dot(hidden[some, :], weights[:, cols], preferred_element_type=jnp.float32).astype(jnp.bfloat16)
+        some = jnp.concatenate([hidden[pl.ds(at, size), :] for at, size in ranges], axis=0)
+        terms = jnp.dot(some, weights[:, cols], preferred_element_type=jnp.float32).astype(jnp.bfloat16)
         for i, out in enumerate(outs):
             out[:, cols] = terms[i * half : (i + 1) * half]
 
 
-def add(came, own, *refs):
-    out = refs[-1]
+def add(came, own, out):
     out[...] = (came[...].astype(jnp.float32) + own[...].astype(jnp.float32)).astype(jnp.bfloat16)
 
 
@@ -315,7 +313,9 @@
         limit=60 * MIB,
     )
 
-    own = call(seat, shape(piece, feats), [scaled], "v", moved=2 * rows * feats)
+    own, inv_gain2 = call(
+        seat, [shape(piece, feats), shape(per, HEAD_DIM, kind=f32)], [scaled, inv_gain2], "vv", moved=2 * rows * feats
+    )
     from_x = {k: shift(scaled, "x", k, NX) for k in AWAY}
     own = call(
         join,
@@ -401,36 +401,49 @@
     other = {k: shift(v, "core", 1, NC) for k, v in same.items()}
     same, other = ([v[k] for k in range(NY)] for v in (same, other))
 
-    def expand(first, last):
+    half = piece // 2
+
+    def expand(groups, halves_of):
+        starts = [(ORDER.index(j) - (groups[0] * NY)) * piece + h * half for j, h in halves_of]
+        ranges = []
+        for at in starts:
+            if ranges and sum(ranges[-1]) == at:
+                ranges[-1] = (ranges[-1][0], ranges[-1][1] + half)
+            else:
+                ranges.append((at, half))
+        size = half * len(starts)
         got = call(
-            functools.partial(second_matmul, first, last),
-            [shape(piece // 2, feats)] * (2 * (last - first)),
+            functools.partial(second_matmul, groups, ranges),
+            [shape(half, feats)] * len(starts),
             [idx] + same + other + [w_down],
             "s" + "v" * (2 * NY + 1),
-            scratch=[pltpu.VMEM((total - first // NY * NY * piece, width), bf16)],
-            flops=2 * (last - first) * piece * feats * width,
+            scratch=[pltpu.VMEM((len(groups) * NY * piece, width), bf16)],
+            flops=2 * size * feats * width,
             moved=2 * feats * width,
         )
-        return {j: got[2 * i : 2 * i + 2] for i, j in enumerate(ORDER[first:last])}
-
-    terms = {**expand(FAR, NZ), **expand(0, FAR)}
+        return dict(zip(halves_of, got))
+
+    terms = {
+        **expand((1,), [(-3, 1), (3, 0), (4, 0), (4, 1)]),
+        **expand((0, 1), [(-2, 0), (-2, 1), (2, 0), (2, 1), (-3, 0), (3, 1)]),
+        **expand((0,), [(0, 0), (0, 1), (-1, 0), (-1, 1), (1, 0), (1, 1)]),
+    }
 
     def chain(half, way, steps):
-        got = terms[way * steps if steps < NZ // 2 else steps][half]
+        got = terms[way * steps if steps < NZ // 2 else steps, half]
         for step in range(steps, 1, -1):
             got = shift(got, "z", way, NZ)
-            own = terms[way * (step - 1)][half]
-            after = [terms[0][0]] if step == steps else []
-            got = call(add, shape(piece // 2, feats), [got, own] + after, "vvh"[: 2 + len(after)], moved=3 * piece * feats)
+            own = terms[way * (step - 1), half]
+            got = call(add, shape(piece // 2, feats), [got, own], "vv", moved=3 * piece * feats)
         return shift(got, "z", way, NZ)
 
     far = NZ // 2
     low = [chain(0, -1, far), chain(0, 1, far - 1)]
     high = [chain(1, 1, far), chain(1, -1, far - 1)]
     mine, one = call(
-        z_sum, [shape(rows, feats, kind=f32), shape(rows, feats)], [terms[0][0]] + low, "vvv", moved=4 * piece * feats
-    )
-    two, three = call(z_sum, [shape(rows, feats)] * 2, [terms[0][1]] + high, "vvv", moved=4 * piece * feats)
+        z_sum, [shape(rows, feats, kind=f32), shape(rows, feats)], [terms[0, 0]] + low, "vvv", moved=4 * piece * feats
+    )
+    two, three = call(z_sum, [shape(rows, feats)] * 2, [terms[0, 1]] + high, "vvv", moved=4 * piece * feats)
     sent = {1: one, 2: two, 3: three}
     parts = {k: shift(sent[k], "x", -k, NX) for k in AWAY}
     return call(finish, shape(rows, feats), [stream, mine] + [parts[k] for k in range(1, NX)], "v" * 5, moved=20 * rows * feats)

time: 121 us -> 123 us (1.017); the launches traced: 121 us -> 122 us
  Pallas kernels: 22.7 us -> 24.8 us
  starting transfers between devices: 53.9 us -> 52.4 us
    pallas_call x26 -> x27, Pallas kernels: 22.7 us -> 24.8 us  [call(): pl.pallas_call(kernel, out_shape=whole, in_specs=[pl.BlockSpec(memory_spa...]
    ppermute x43, starting transfers between devices: 53.9 us -> 52.4 us  [shift(): return lax.ppermute(v, axis, [(i, (i + by) % n) for i in range(n)])]
    unnamed x16 -> x14, local copies, waits for them, and re-layouts: 3.63 us -> 3.63 us
  transfers between devices with their start and end apart: 43 -> 43, of which waited for: 23 -> 23; matrix products, arithmetic and copies ran while one was open for 0% -> 0% of each run, Pallas kernels for 14% -> 15%
where the time goes in v4:
time: 123 us; the launch traced here: 122 us
  starting transfers between devices  52.4 us (43%)
  waiting for transfers between devices  40.5 us (33%)
  Pallas kernels  24.8 us (20%)
  local copies, waits for them, and re-layouts  3.63 us (3%)
    ppermute x43, starting transfers between devices, shift(): return lax.ppermute(v, axis, [(i, (i + by) % n) for i in range(n)])  52.4 us
    ppermute x43, waiting for transfers between devices, shift(): return lax.ppermute(v, axis, [(i, (i + by) % n) for i in range(n)])  40.5 us
    pallas_call x27, Pallas kernels, call(): pl.pallas_call(kernel, out_shape=whole, in_specs=[pl.BlockSpec(memory_spa...  24.8 us
    unnamed x14, local copies, waits for them, and re-layouts  3.63 us
  transfers between devices with their start and end apart: 43, of which 23 were waited for; matrix products, arithmetic and copies ran while one was open for 0% of the time, Pallas kernels for 15%

profile of v4, /device:TPU:32, one launch (start us, length us, event | category | flops | bytes accessed | tf_op | source)
XLA Modules:
  0.0 121.6 jit_solution(12262630782416456311)
XLA Ops:
  0.0 2.6 %shard_map.109 = (f32[16,2048]{1,0:T(8,128)}, f32[16,128]{1,0:T(8,128)}, bf16[16,2048]{1,0:T(8,128)(2,1)}) custom-call(s32[16]{0:T(128)} %lengths_in.1, bf16[16,2048]{1,0:T(8,128)(2,1)} %hidden_in.1, bf16[16,2048]{1,0:T(8,128)(2,1)} %queries_in.1, bf16[16,128,128]{2,1,0:T(8,128)(2,1)} %keys_in.1, bf16[16,128,128]{2,1,0:T(8,128)(2,1)} %values_in.1, ...), custom_call_target="tpu_custom_call" | custom-call | bytes 1048576 | tf_op jit(solution)/shard_map/pallas_call | solution.py:34
  2.6 2.8 %collective-permute-start.2 = (bf16[16,2048]{1,0:T(8,128)(2,1)}, bf16[16,2048]{1,0:T(8,128)(2,1)S(1)}, u32[]{:S(2)}, u32[]{:S(2)}) collective-permute-start(bf16[16,2048]{1,0:T(8,128)(2,1)} %get-tuple-element.52.own), channel_id=1, source_target_pairs={{0,192},{64,0},{128,64},{192,128},{1,193},{65,1},{129,65},{193,129... | collective-permute-start | bytes 196616 | tf_op jit(solution)/shard_map/ppermute | solution.py:23
  8.7 2.7 %collective-permute-done.1.refs_1_ = bf16[16,2048]{1,0:T(8,128)(2,1)S(1)} collective-permute-done((bf16[16,2048]{1,0:T(8,128)(2,1)}, bf16[16,2048]{1,0:T(8,128)(2,1)S(1)}, u32[]{:S(2)}, u32[]{:S(2)}) %collective-permute-start.1) | collective-permute-done | bytes 65568 | tf_op jit(solution)/shard_map/ppermute | solution.py:23
  14.3 4.8 %collective-permute-done.6.refs_2_ = bf16[64,2048]{1,0:T(8,128)(2,1)S(1)} collective-permute-done((bf16[64,2048]{1,0:T(8,128)(2,1)S(1)}, bf16[64,2048]{1,0:T(8,128)(2,1)S(1)}, u32[]{:S(2)}, u32[]{:S(2)}) %collective-permute-start.6) | collective-permute-done | bytes 262176 | tf_op jit(solution)/shard_map/ppermute | solution.py:23
  19.0 3.3 %collective-permute-start.7 = (bf16[64,2048]{1,0:T(8,128)(2,1)S(1)}, bf16[64,2048]{1,0:T(8,128)(2,1)S(1)}, u32[]{:S(2)}, u32[]{:S(2)}) collective-permute-start(bf16[64,2048]{1,0:T(8,128)(2,1)S(1)} %collective-permute-done.6.refs_2_), channel_id=1, source_target_pairs={{0,56},{8,0},{16,8},{24,16},{32,24},{40,32},{48,40},{56,48},{1,57}... | collective-permute-start | bytes 786440 | tf_op jit(solution)/shard_map/ppermute | solution.py:23
  22.8 3.4 %collective-permute-done.7.refs_4_.refs_0_ = bf16[64,2048]{1,0:T(8,128)(2,1)S(1)} collective-permute-done((bf16[64,2048]{1,0:T(8,128)(2,1)S(1)}, bf16[64,2048]{1,0:T(8,128)(2,1)S(1)}, u32[]{:S(2)}, u32[]{:S(2)}) %collective-permute-start.7) | collective-permute-done | bytes 262176 | tf_op jit(solution)/shard_map/ppermute | solution.py:23
  26.2 3.7 %collective-permute-start.8 = (bf16[64,2048]{1,0:T(8,128)(2,1)S(1)}, bf16[64,2048]{1,0:T(8,128)(2,1)S(1)}, u32[]{:S(2)}, u32[]{:S(2)}) collective-permute-start(bf16[64,2048]{1,0:T(8,128)(2,1)S(1)} %collective-permute-done.7.refs_4_.refs_0_), channel_id=1, source_target_pairs={{0,56},{8,0},{16,8},{24,16},{32,24},{40,32},{48,40},{56,48},{1,57}... | collective-permute-start | bytes 786440 | tf_op jit(solution)/shard_map/ppermute | solution.py:23
  32.5 2.7 %shard_map.112 = (bf16[128,1920]{1,0:T(8,128)(2,1)S(1)}, bf16[128,1920]{1,0:T(8,128)(2,1)S(1)}, bf16[256,2048]{1,0:T(8,128)(2,1)S(1)}, f32[8,128]{1,0:T(8,128)S(1)}) custom-call(s32[4]{0:T(128)S(1)} %pad_add_fusion.idx, bf16[64,2048]{1,0:T(8,128)(2,1)S(1)} %shard_map.111.refs_0_, bf16[64,2048]{1,0:T(8,128)(2,1)S(1)} %collective-permute-done.3.refs_1_, ...), custom_call_target="tpu_custom_call" | custom-call | flops 939524096 | bytes 3670016 | tf_op jit(solution)/shard_map/pallas_call | solution.py:34
  35.2 2.8 %collective-permute-done.5.up.refs_1_ = bf16[64,2048]{1,0:T(8,128)(2,1)S(1)} collective-permute-done((bf16[64,2048]{1,0:T(8,128)(2,1)S(1)}, bf16[64,2048]{1,0:T(8,128)(2,1)S(1)}, u32[]{:S(2)}, u32[]{:S(2)}) %collective-permute-start.5) | collective-permute-done | bytes 262176 | tf_op jit(solution)/shard_map/ppermute | solution.py:23
  38.1 3.4 %collective-permute-start.14 = (bf16[32,2048]{1,0:T(8,128)(2,1)S(1)}, bf16[32,2048]{1,0:T(8,128)(2,1)S(1)}, u32[]{:S(2)}, u32[]{:S(2)}) collective-permute-start(bf16[32,2048]{1,0:T(8,128)(2,1)S(1)} %get-tuple-element.68), channel_id=1, source_target_pairs={{0,56},{8,0},{16,8},{24,16},{32,24},{40,32},{48,40},{56,48},{1,57}... | collective-permute-start | bytes 393224 | tf_op jit(solution)/shard_map/ppermute | solution.py:23
  43.3 3.9 %shard_map.115 = (bf16[128,1920]{1,0:T(8,128)(2,1)S(1)}, bf16[128,1920]{1,0:T(8,128)(2,1)S(1)}, bf16[128,1920]{1,0:T(8,128)(2,1)S(1)}) custom-call(s32[4]{0:T(128)S(1)} %pad_add_fusion.idx, bf16[64,2048]{1,0:T(8,128)(2,1)S(1)} %collective-permute-done.7.refs_4_.refs_0_, ...), custom_call_target="tpu_custom_call", output_to_operand_aliasing={{2}: (4, {})} | custom-call | flops 1409286144 | bytes 7340032 | tf_op jit(solution)/shard_map/pallas_call | solution.py:34
  47.4 3.0 %shard_map.117 = (bf16[128,1920]{1,0:T(8,128)(2,1)S(1)}, bf16[128,1920]{1,0:T(8,128)(2,1)S(1)}) custom-call(s32[4]{0:T(128)S(1)} %pad_add_fusion.idx, bf16[32,2048]{1,0:T(8,128)(2,1)S(1)} %collective-permute-done.13.low, bf16[32,2048]{1,0:T(8,128)(2,1)S(1)} %collective-permute-done.14.high, ...), custom_call_target="tpu_custom_call", output_to_operand_aliasing={{0}: (6, {}), {1}: (7, {})} | custom-call | flops 469762048 | bytes 7340032 | tf_op jit(solution)/shard_map/pallas_call | solution.py:34
  53.3 2.9 %collective-permute-start.11 = (bf16[32,1920]{1,0:T(8,128)(2,1)S(1)}, bf16[32,1920]{1,0:T(8,128)(2,1)S(1)}, u32[]{:S(2)}, u32[]{:S(2)}) collective-permute-start(bf16[32,1920]{1,0:T(8,128)(2,1)S(1)} %get-tuple-element.66), channel_id=1, source_target_pairs={{0,4},{2,6},{4,0},{6,2},{1,5},{3,7},{5,1},{7,3},{8,12},{10,14},{12... | collective-permute-start | bytes 368648 | tf_op jit(solution)/shard_map/ppermute | solution.py:23
  63.0 2.7 %collective-permute-done.16.refs_5_ = bf16[32,1920]{1,0:T(8,128)(2,1)S(1)} collective-permute-done((bf16[32,1920]{1,0:T(8,128)(2,1)S(1)}, bf16[32,1920]{1,0:T(8,128)(2,1)S(1)}, u32[]{:S(2)}, u32[]{:S(2)}) %collective-permute-start.16) | collective-permute-done | bytes 122912 | tf_op jit(solution)/shard_map/ppermute | solution.py:23
  71.6 2.8 %collective-permute-done.21.refs_3_ = bf16[64,896]{1,0:T(8,128)(2,1)S(1)} collective-permute-done((bf16[64,896]{1,0:T(8,128)(2,1)S(1)}, bf16[64,896]{1,0:T(8,128)(2,1)S(1)}, u32[]{:S(2)}, u32[]{:S(2)}) %collective-permute-start.21) | collective-permute-done | bytes 114720 | tf_op jit(solution)/shard_map/ppermute | solution.py:23
  74.4 2.5 %collective-permute-done.20.refs_2_ = bf16[64,896]{1,0:T(8,128)(2,1)S(1)} collective-permute-done((bf16[64,896]{1,0:T(8,128)(2,1)S(1)}, bf16[64,896]{1,0:T(8,128)(2,1)S(1)}, u32[]{:S(2)}, u32[]{:S(2)}) %collective-permute-start.20) | collective-permute-done | bytes 114720 | tf_op jit(solution)/shard_map/ppermute | solution.py:23
  79.2 2.6 %shard_map.121 = (bf16[32,2048]{1,0:T(8,128)(2,1)S(1)}, bf16[32,2048]{1,0:T(8,128)(2,1)S(1)}, bf16[32,2048]{1,0:T(8,128)(2,1)S(1)}, bf16[32,2048]{1,0:T(8,128)(2,1)S(1)}) custom-call(s32[4]{0:T(128)S(1)} %pad_add_fusion.idx, bf16[64,896]{1,0:T(8,128)(2,1)S(1)} %shard_map.119.refs_0_, bf16[64,896]{1,0:T(8,128)(2,1)S(1)} %collective-permute-done.19.refs_1_, ...), custom_call_target="tpu_custom_call" | custom-call | flops 469762048 | bytes 3670016 | tf_op jit(solution)/shard_map/pallas_call | solution.py:34
  84.0 2.8 %shard_map.122 = (bf16[32,2048]{1,0:T(8,128)(2,1)S(1)}, bf16[32,2048]{1,0:T(8,128)(2,1)S(1)}, bf16[32,2048]{1,0:T(8,128)(2,1)S(1)}, bf16[32,2048]{1,0:T(8,128)(2...) custom-call(s32[4]{0:T(128)S(1)} %pad_add_fusion.idx, bf16[64,896]{1,0:T(8,128)(2,1)S(1)} %shard_map.119.refs_0_, ...), custom_call_target="tpu_custom_call" | custom-call | flops 704643072 | bytes 3670016 | tf_op jit(solution)/shard_map/pallas_call | solution.py:34
  89.6 2.8 %collective-permute-start.38 = (bf16[32,2048]{1,0:T(8,128)(2,1)S(1)}, bf16[32,2048]{1,0:T(8,128)(2,1)S(1)}, u32[]{:S(2)}, u32[]{:S(2)}) collective-permute-start(bf16[32,2048]{1,0:T(8,128)(2,1)S(1)} %get-tuple-element.92), channel_id=1, source_target_pairs={{0,56},{8,0},{16,8},{24,16},{32,24},{40,32},{48,40},{56,48},{1,57}... | collective-permute-start | bytes 393224 | tf_op jit(solution)/shard_map/ppermute | solution.py:23
  96.6 3.4 %collective-permute-start.39 = (bf16[32,2048]{1,0:T(8,128)(2,1)S(1)}, bf16[32,2048]{1,0:T(8,128)(2,1)S(1)}, u32[]{:S(2)}, u32[]{:S(2)}) collective-permute-start(bf16[32,2048]{1,0:T(8,128)(2,1)S(1)} %shard_map.132), channel_id=1, source_target_pairs={{0,56},{8,0},{16,8},{24,16},{32,24},{40,32},{48,40},{56,48},{1,57}... | collective-permute-start | bytes 393224 | tf_op jit(solution)/shard_map/ppermute | solution.py:23
  100.1 2.8 %shard_map.120 = (bf16[32,2048]{1,0:T(8,128)(2,1)S(1)}, bf16[32,2048]{1,0:T(8,128)(2,1)S(1)}, bf16[32,2048]{1,0:T(8,128)(2,1)S(1)}, bf16[32,2048]{1,0:T(8,128)(2...) custom-call(s32[4]{0:T(128)S(1)} %pad_add_fusion.idx, bf16[64,896]{1,0:T(8,128)(2,1)S(1)} %shard_map.119.refs_0_, ...), custom_call_target="tpu_custom_call" | custom-call | flops 704643072 | bytes 3670016 | tf_op jit(solution)/shard_map/pallas_call | solution.py:34
  105.2 3.3 %collective-permute-start.40 = (bf16[32,2048]{1,0:T(8,128)(2,1)S(1)}, bf16[32,2048]{1,0:T(8,128)(2,1)S(1)}, u32[]{:S(2)}, u32[]{:S(2)}) collective-permute-start(bf16[32,2048]{1,0:T(8,128)(2,1)S(1)} %shard_map.133), channel_id=1, source_target_pairs={{0,56},{8,0},{16,8},{24,16},{32,24},{40,32},{48,40},{56,48},{1,57}... | collective-permute-start | bytes 393224 | tf_op jit(solution)/shard_map/ppermute | solution.py:23
  111.0 2.6 %collective-permute-done.37.one = bf16[32,2048]{1,0:T(8,128)(2,1)S(1)} collective-permute-done((bf16[32,2048]{1,0:T(8,128)(2,1)S(1)}, bf16[32,2048]{1,0:T(8,128)(2,1)S(1)}, u32[]{:S(2)}, u32[]{:S(2)}) %collective-permute-start.37) | collective-permute-done | bytes 131104 | tf_op jit(solution)/shard_map/ppermute | solution.py:23
  115.5 4.0 %collective-permute-done.41.two = bf16[16,2048]{1,0:T(8,128)(2,1)S(1)} collective-permute-done((bf16[16,2048]{1,0:T(8,128)(2,1)S(1)}, bf16[16,2048]{1,0:T(8,128)(2,1)S(1)}, u32[]{:S(2)}, u32[]{:S(2)}) %collective-permute-start.41) | collective-permute-done | bytes 65568 | tf_op jit(solution)/shard_map/ppermute | solution.py:23
  (104 shorter events, 47.0 us)
Async XLA Ops:
  12.2 6.9 %collective-permute-start.6 = (bf16[64,2048]{1,0:T(8,128)(2,1)S(1)}, bf16[64,2048]{1,0:T(8,128)(2,1)S(1)}, u32[]{:S(2)}, u32[]{:S(2)}) collective-permute-start(bf16[64,2048]{1,0:T(8,128)(2,1)S(1)} %shard_map.111.refs_0_), channel_id=1, source_target_pairs={{0,56},{8,0},{16,8},{24,16},{32,24},{40,32},{48,40},{56,48},{1,57}... | collective-permute-start | bytes 786440 | tf_op jit(solution)/shard_map/ppermute | solution.py:23
  12.3 10.4 %collective-permute-start.3 = (bf16[64,2048]{1,0:T(8,128)(2,1)S(1)}, bf16[64,2048]{1,0:T(8,128)(2,1)S(1)}, u32[]{:S(2)}, u32[]{:S(2)}) collective-permute-start(bf16[64,2048]{1,0:T(8,128)(2,1)S(1)} %shard_map.111.refs_0_), channel_id=1, source_target_pairs={{0,8},{8,16},{16,24},{24,32},{32,40},{40,48},{48,56},{56,0},{1,9},... | collective-permute-start | bytes 786440 | tf_op jit(solution)/shard_map/ppermute | solution.py:23
  19.0 7.2 %collective-permute-start.7 = (bf16[64,2048]{1,0:T(8,128)(2,1)S(1)}, bf16[64,2048]{1,0:T(8,128)(2,1)S(1)}, u32[]{:S(2)}, u32[]{:S(2)}) collective-permute-start(bf16[64,2048]{1,0:T(8,128)(2,1)S(1)} %collective-permute-done.6.refs_2_), channel_id=1, source_target_pairs={{0,56},{8,0},{16,8},{24,16},{32,24},{40,32},{48,40},{56,48},{1,57}... | collective-permute-start | bytes 786440 | tf_op jit(solution)/shard_map/ppermute | solution.py:23
  22.8 7.6 %collective-permute-start.4 = (bf16[64,2048]{1,0:T(8,128)(2,1)S(1)}, bf16[64,2048]{1,0:T(8,128)(2,1)S(1)}, u32[]{:S(2)}, u32[]{:S(2)}) collective-permute-start(bf16[64,2048]{1,0:T(8,128)(2,1)S(1)} %collective-permute-done.3.refs_1_), channel_id=1, source_target_pairs={{0,8},{8,16},{16,24},{24,32},{32,40},{40,48},{48,56},{56,0},{1,9},... | collective-permute-start | bytes 786440 | tf_op jit(solution)/shard_map/ppermute | solution.py:23
  26.2 9.0 %collective-permute-start.8 = (bf16[64,2048]{1,0:T(8,128)(2,1)S(1)}, bf16[64,2048]{1,0:T(8,128)(2,1)S(1)}, u32[]{:S(2)}, u32[]{:S(2)}) collective-permute-start(bf16[64,2048]{1,0:T(8,128)(2,1)S(1)} %collective-permute-done.7.refs_4_.refs_0_), channel_id=1, source_target_pairs={{0,56},{8,0},{16,8},{24,16},{32,24},{40,32},{48,40},{56,48},{1,57}... | collective-permute-start | bytes 786440 | tf_op jit(solution)/shard_map/ppermute | solution.py:23
  30.4 7.7 %collective-permute-start.5 = (bf16[64,2048]{1,0:T(8,128)(2,1)S(1)}, bf16[64,2048]{1,0:T(8,128)(2,1)S(1)}, u32[]{:S(2)}, u32[]{:S(2)}) collective-permute-start(bf16[64,2048]{1,0:T(8,128)(2,1)S(1)} %collective-permute-done.4.refs_3_), channel_id=1, source_target_pairs={{0,8},{8,16},{16,24},{24,32},{32,40},{40,48},{48,56},{56,0},{1,9},... | collective-permute-start | bytes 786440 | tf_op jit(solution)/shard_map/ppermute | solution.py:23
  38.1 9.3 %collective-permute-start.14 = (bf16[32,2048]{1,0:T(8,128)(2,1)S(1)}, bf16[32,2048]{1,0:T(8,128)(2,1)S(1)}, u32[]{:S(2)}, u32[]{:S(2)}) collective-permute-start(bf16[32,2048]{1,0:T(8,128)(2,1)S(1)} %get-tuple-element.68), channel_id=1, source_target_pairs={{0,56},{8,0},{16,8},{24,16},{32,24},{40,32},{48,40},{56,48},{1,57}... | collective-permute-start | bytes 393224 | tf_op jit(solution)/shard_map/ppermute | solution.py:23
  50.4 7.1 %collective-permute-start.15 = (bf16[128,1920]{1,0:T(8,128)(2,1)S(1)}, bf16[128,1920]{1,0:T(8,128)(2,1)S(1)}, u32[]{:S(2)}, u32[]{:S(2)}) collective-permute-start(bf16[128,1920]{1,0:T(8,128)(2,1)S(1)} %get-tuple-element.72), channel_id=1, source_target_pairs={{0,1},{1,0},{2,3},{3,2},{4,5},{5,4},{6,7},{7,6},{8,9},{9,8},{10,11... | collective-permute-start | bytes 1474568 | tf_op jit(solution)/shard_map/ppermute | solution.py:23
  51.6 8.1 %collective-permute-start.10 = (bf16[32,1920]{1,0:T(8,128)(2,1)S(1)}, bf16[32,1920]{1,0:T(8,128)(2,1)S(1)}, u32[]{:S(2)}, u32[]{:S(2)}) collective-permute-start(bf16[32,1920]{1,0:T(8,128)(2,1)S(1)} %get-tuple-element.65), channel_id=1, source_target_pairs={{0,2},{2,4},{4,6},{6,0},{1,3},{3,5},{5,7},{7,1},{8,10},{10,12},{12... | collective-permute-start | bytes 368648 | tf_op jit(solution)/shard_map/ppermute | solution.py:23
  53.3 9.7 %collective-permute-start.11 = (bf16[32,1920]{1,0:T(8,128)(2,1)S(1)}, bf16[32,1920]{1,0:T(8,128)(2,1)S(1)}, u32[]{:S(2)}, u32[]{:S(2)}) collective-permute-start(bf16[32,1920]{1,0:T(8,128)(2,1)S(1)} %get-tuple-element.66), channel_id=1, source_target_pairs={{0,4},{2,6},{4,0},{6,2},{1,5},{3,7},{5,1},{7,3},{8,12},{10,14},{12... | collective-permute-start | bytes 368648 | tf_op jit(solution)/shard_map/ppermute | solution.py:23
  56.2 6.8 %collective-permute-start.12 = (bf16[32,1920]{1,0:T(8,128)(2,1)S(1)}, bf16[32,1920]{1,0:T(8,128)(2,1)S(1)}, u32[]{:S(2)}, u32[]{:S(2)}) collective-permute-start(bf16[32,1920]{1,0:T(8,128)(2,1)S(1)} %get-tuple-element.67), channel_id=1, source_target_pairs={{0,6},{2,0},{4,2},{6,4},{1,7},{3,1},{5,3},{7,5},{8,14},{10,8},{12,... | collective-permute-start | bytes 368648 | tf_op jit(solution)/shard_map/ppermute | solution.py:23
  58.2 7.5 %collective-permute-start.16 = (bf16[32,1920]{1,0:T(8,128)(2,1)S(1)}, bf16[32,1920]{1,0:T(8,128)(2,1)S(1)}, u32[]{:S(2)}, u32[]{:S(2)}) collective-permute-start(bf16[32,1920]{1,0:T(8,128)(2,1)S(1)} %get-tuple-element.74), channel_id=1, source_target_pairs={{0,2},{2,4},{4,6},{6,0},{1,3},{3,5},{5,7},{7,1},{8,10},{10,12},{12... | collective-permute-start | bytes 368648 | tf_op jit(solution)/shard_map/ppermute | solution.py:23
  59.0 8.4 %collective-permute-start.17 = (bf16[32,1920]{1,0:T(8,128)(2,1)S(1)}, bf16[32,1920]{1,0:T(8,128)(2,1)S(1)}, u32[]{:S(2)}, u32[]{:S(2)}) collective-permute-start(bf16[32,1920]{1,0:T(8,128)(2,1)S(1)} %get-tuple-element.75), channel_id=1, source_target_pairs={{0,4},{2,6},{4,0},{6,2},{1,5},{3,7},{5,1},{7,3},{8,12},{10,14},{12... | collective-permute-start | bytes 368648 | tf_op jit(solution)/shard_map/ppermute | solution.py:23
  59.8 7.6 %collective-permute-start.18 = (bf16[32,1920]{1,0:T(8,128)(2,1)S(1)}, bf16[32,1920]{1,0:T(8,128)(2,1)S(1)}, u32[]{:S(2)}, u32[]{:S(2)}) collective-permute-start(bf16[32,1920]{1,0:T(8,128)(2,1)S(1)} %get-tuple-element.76), channel_id=1, source_target_pairs={{0,6},{2,0},{4,2},{6,4},{1,7},{3,1},{5,3},{7,5},{8,14},{10,8},{12,... | collective-permute-start | bytes 368648 | tf_op jit(solution)/shard_map/ppermute | solution.py:23
  70.0 6.9 %collective-permute-start.20 = (bf16[64,896]{1,0:T(8,128)(2,1)S(1)}, bf16[64,896]{1,0:T(8,128)(2,1)S(1)}, u32[]{:S(2)}, u32[]{:S(2)}) collective-permute-start(bf16[64,896]{1,0:T(8,128)(2,1)S(1)} %shard_map.119.refs_0_), channel_id=1, source_target_pairs={{0,4},{2,6},{4,0},{6,2},{1,5},{3,7},{5,1},{7,3},{8,12},{10,14},{12... | collective-permute-start | bytes 344072 | tf_op jit(solution)/shard_map/ppermute | solution.py:23
  71.0 7.0 %collective-permute-start.19 = (bf16[64,896]{1,0:T(8,128)(2,1)S(1)}, bf16[64,896]{1,0:T(8,128)(2,1)S(1)}, u32[]{:S(2)}, u32[]{:S(2)}) collective-permute-start(bf16[64,896]{1,0:T(8,128)(2,1)S(1)} %shard_map.119.refs_0_), channel_id=1, source_target_pairs={{0,2},{2,4},{4,6},{6,0},{1,3},{3,5},{5,7},{7,1},{8,10},{10,12},{12... | collective-permute-start | bytes 344072 | tf_op jit(solution)/shard_map/ppermute | solution.py:23
  83.9 8.5 %collective-permute-start.34 = (bf16[32,2048]{1,0:T(8,128)(2,1)S(1)}, bf16[32,2048]{1,0:T(8,128)(2,1)S(1)}, u32[]{:S(2)}, u32[]{:S(2)}) collective-permute-start(bf16[32,2048]{1,0:T(8,128)(2,1)S(1)} %get-tuple-element.88), channel_id=1, source_target_pairs={{0,8},{8,16},{16,24},{24,32},{32,40},{40,48},{48,56},{56,0},{1,9},... | collective-permute-start | bytes 393224 | tf_op jit(solution)/shard_map/ppermute | solution.py:23
  83.9 8.6 %collective-permute-start.30 = (bf16[32,2048]{1,0:T(8,128)(2,1)S(1)}, bf16[32,2048]{1,0:T(8,128)(2,1)S(1)}, u32[]{:S(2)}, u32[]{:S(2)}) collective-permute-start(bf16[32,2048]{1,0:T(8,128)(2,1)S(1)} %get-tuple-element.82), channel_id=1, source_target_pairs={{0,8},{8,16},{16,24},{24,32},{32,40},{40,48},{48,56},{56,0},{1,9},... | collective-permute-start | bytes 393224 | tf_op jit(solution)/shard_map/ppermute | solution.py:23
  89.6 6.9 %collective-permute-start.38 = (bf16[32,2048]{1,0:T(8,128)(2,1)S(1)}, bf16[32,2048]{1,0:T(8,128)(2,1)S(1)}, u32[]{:S(2)}, u32[]{:S(2)}) collective-permute-start(bf16[32,2048]{1,0:T(8,128)(2,1)S(1)} %get-tuple-element.92), channel_id=1, source_target_pairs={{0,56},{8,0},{16,8},{24,16},{32,24},{40,32},{48,40},{56,48},{1,57}... | collective-permute-start | bytes 393224 | tf_op jit(solution)/shard_map/ppermute | solution.py:23
  92.4 7.5 %collective-permute-start.35 = (bf16[32,2048]{1,0:T(8,128)(2,1)S(1)}, bf16[32,2048]{1,0:T(8,128)(2,1)S(1)}, u32[]{:S(2)}, u32[]{:S(2)}) collective-permute-start(bf16[32,2048]{1,0:T(8,128)(2,1)S(1)} %shard_map.129), channel_id=1, source_target_pairs={{0,8},{8,16},{16,24},{24,32},{32,40},{40,48},{48,56},{56,0},{1,9},... | collective-permute-start | bytes 393224 | tf_op jit(solution)/shard_map/ppermute | solution.py:23
  92.6 10.3 %collective-permute-start.31 = (bf16[32,2048]{1,0:T(8,128)(2,1)S(1)}, bf16[32,2048]{1,0:T(8,128)(2,1)S(1)}, u32[]{:S(2)}, u32[]{:S(2)}) collective-permute-start(bf16[32,2048]{1,0:T(8,128)(2,1)S(1)} %shard_map.126), channel_id=1, source_target_pairs={{0,8},{8,16},{16,24},{24,32},{32,40},{40,48},{48,56},{56,0},{1,9},... | collective-permute-start | bytes 393224 | tf_op jit(solution)/shard_map/ppermute | solution.py:23
  94.1 9.4 %collective-permute-start.28 = (bf16[32,2048]{1,0:T(8,128)(2,1)S(1)}, bf16[32,2048]{1,0:T(8,128)(2,1)S(1)}, u32[]{:S(2)}, u32[]{:S(2)}) collective-permute-start(bf16[32,2048]{1,0:T(8,128)(2,1)S(1)} %shard_map.124), channel_id=1, source_target_pairs={{0,56},{8,0},{16,8},{24,16},{32,24},{40,32},{48,40},{56,48},{1,57}... | collective-permute-start | bytes 393224 | tf_op jit(solution)/shard_map/ppermute | solution.py:23
  96.6 8.6 %collective-permute-start.39 = (bf16[32,2048]{1,0:T(8,128)(2,1)S(1)}, bf16[32,2048]{1,0:T(8,128)(2,1)S(1)}, u32[]{:S(2)}, u32[]{:S(2)}) collective-permute-start(bf16[32,2048]{1,0:T(8,128)(2,1)S(1)} %shard_map.132), channel_id=1, source_target_pairs={{0,56},{8,0},{16,8},{24,16},{32,24},{40,32},{48,40},{56,48},{1,57}... | collective-permute-start | bytes 393224 | tf_op jit(solution)/shard_map/ppermute | solution.py:23
  100.0 8.5 %collective-permute-start.36 = (bf16[32,2048]{1,0:T(8,128)(2,1)S(1)}, bf16[32,2048]{1,0:T(8,128)(2,1)S(1)}, u32[]{:S(2)}, u32[]{:S(2)}) collective-permute-start(bf16[32,2048]{1,0:T(8,128)(2,1)S(1)} %shard_map.130), channel_id=1, source_target_pairs={{0,8},{8,16},{16,24},{24,32},{32,40},{40,48},{48,56},{56,0},{1,9},... | collective-permute-start | bytes 393224 | tf_op jit(solution)/shard_map/ppermute | solution.py:23
  (26 other events, 172.5 us)

commit v5 on v4

--- a/solution.py
+++ b/solution.py
@@ -234,7 +234,7 @@
         hidden[pl.ds(i * block, block), :] = (gate / (1.0 + jnp.exp(-gate)) * up).astype(jnp.bfloat16)
 
 
-def second_matmul(groups, ranges, idx, *refs):
+def second_matmul(idx, *refs):
     same, refs = refs[:NY], refs[NY:]
     other, refs = refs[:NY], refs[NY:]
     weights, outs, hidden = refs[0], refs[1:-1], refs[-1]
@@ -243,16 +243,15 @@
     half = block // 2
     for k in range(NY):
         y = lax.rem(mine - k + NY, NY)
-        for g, i in enumerate(groups):
-            at = (g * NY + y) * block
+        for i in range(2):
+            at = (i * NY + y) * block
             hidden[rows_at(at + core * half, half), :] = same[k][pl.ds(i * half, half), :]
             hidden[rows_at(at + (1 - core) * half, half), :] = other[k][pl.ds(i * half, half), :]
 
     @pl.loop(0, weights.shape[1] // 256)
     def _(t):
         cols = pl.ds(pl.multiple_of(t * 256, 256), 256)
-        some = jnp.concatenate([hidden[pl.ds(at, size), :] for at, size in ranges], axis=0)
-        terms = jnp.dot(some, weights[:, cols], preferred_element_type=jnp.float32).astype(jnp.bfloat16)
+        terms = jnp.dot(hidden[...], weights[:, cols], preferred_element_type=jnp.float32).astype(jnp.bfloat16)
         for i, out in enumerate(outs):
             out[:, cols] = terms[i * half : (i + 1) * half]
 
@@ -403,31 +402,18 @@
 
     half = piece // 2
 
-    def expand(groups, halves_of):
-        starts = [(ORDER.index(j) - (groups[0] * NY)) * piece + h * half for j, h in halves_of]
-        ranges = []
-        for at in starts:
-            if ranges and sum(ranges[-1]) == at:
-                ranges[-1] = (ranges[-1][0], ranges[-1][1] + half)
-            else:
-                ranges.append((at, half))
-        size = half * len(starts)
-        got = call(
-            functools.partial(second_matmul, groups, ranges),
-            [shape(half, feats)] * len(starts),
-            [idx] + same + other + [w_down],
-            "s" + "v" * (2 * NY + 1),
-            scratch=[pltpu.VMEM((len(groups) * NY * piece, width), bf16)],
-            flops=2 * size * feats * width,
-            moved=2 * feats * width,
-        )
-        return dict(zip(halves_of, got))
-
-    terms = {
-        **expand((1,), [(-3, 1), (3, 0), (4, 0), (4, 1)]),
-        **expand((0, 1), [(-2, 0), (-2, 1), (2, 0), (2, 1), (-3, 0), (3, 1)]),
-        **expand((0,), [(0, 0), (0, 1), (-1, 0), (-1, 1), (1, 0), (1, 1)]),
-    }
+    keys = [(j, h) for j in ORDER for h in range(2)]
+    got = call(
+        second_matmul,
+        [shape(half, feats)] * len(keys),
+        [idx] + same + other + [w_down],
+        "s" + "v" * (2 * NY + 1),
+        scratch=[pltpu.VMEM((total, width), bf16)],
+        flops=2 * total * feats * width,
+        moved=2 * feats * width,
+        limit=20 * MIB,
+    )
+    terms = dict(zip(keys, got))
 
     def chain(half, way, steps):
         got = terms[way * steps if steps < NZ // 2 else steps, half]

time: 123 us -> 122 us (level)
  Pallas kernels: 24.8 us -> 20.8 us
  waiting for transfers between devices: 40.5 us -> 44.1 us
    pallas_call x27 -> x25, Pallas kernels: 24.8 us -> 20.8 us  [call(): pl.pallas_call(kernel, out_shape=whole, in_specs=[pl.BlockSpec(memory_spa...]
    ppermute x43, waiting for transfers between devices: 40.5 us -> 44.1 us  [shift(): return lax.ppermute(v, axis, [(i, (i + by) % n) for i in range(n)])]
  transfers between devices with their start and end apart: 43 -> 43, of which waited for: 23 -> 24; matrix products, arithmetic and copies ran while one was open for 0% -> 0% of each run, Pallas kernels for 15% -> 11%
where the time goes in v5:
time: 122 us; the launch traced here: 121 us
  starting transfers between devices  52.4 us (43%)
  waiting for transfers between devices  44.1 us (36%)
  Pallas kernels  20.8 us (17%)
  local copies, waits for them, and re-layouts  3.63 us (3%)
    ppermute x43, starting transfers between devices, shift(): return lax.ppermute(v, axis, [(i, (i + by) % n) for i in range(n)])  52.4 us
    ppermute x43, waiting for transfers between devices, shift(): return lax.ppermute(v, axis, [(i, (i + by) % n) for i in range(n)])  44.1 us
    pallas_call x25, Pallas kernels, call(): pl.pallas_call(kernel, out_shape=whole, in_specs=[pl.BlockSpec(memory_spa...  20.8 us
    unnamed x14, local copies, waits for them, and re-layouts  3.63 us
  transfers between devices with their start and end apart: 43, of which 24 were waited for; matrix products, arithmetic and copies ran while one was open for 0% of the time, Pallas kernels for 11%

profile of v5, /device:TPU:32, one launch (start us, length us, event | category | flops | bytes accessed | tf_op | source)
XLA Modules:
  0.0 121.3 jit_solution(734008851769367697)
XLA Ops:
  0.0 2.6 %shard_map.109 = (f32[16,2048]{1,0:T(8,128)}, f32[16,128]{1,0:T(8,128)}, bf16[16,2048]{1,0:T(8,128)(2,1)}) custom-call(s32[16]{0:T(128)} %lengths_in.1, bf16[16,2048]{1,0:T(8,128)(2,1)} %hidden_in.1, bf16[16,2048]{1,0:T(8,128)(2,1)} %queries_in.1, bf16[16,128,128]{2,1,0:T(8,128)(2,1)} %keys_in.1, bf16[16,128,128]{2,1,0:T(8,128)(2,1)} %values_in.1, ...), custom_call_target="tpu_custom_call" | custom-call | bytes 1048576 | tf_op jit(solution)/shard_map/pallas_call | solution.py:34
  2.6 2.8 %collective-permute-start.2 = (bf16[16,2048]{1,0:T(8,128)(2,1)}, bf16[16,2048]{1,0:T(8,128)(2,1)S(1)}, u32[]{:S(2)}, u32[]{:S(2)}) collective-permute-start(bf16[16,2048]{1,0:T(8,128)(2,1)} %get-tuple-element.52.own), channel_id=1, source_target_pairs={{0,192},{64,0},{128,64},{192,128},{1,193},{65,1},{129,65},{193,129... | collective-permute-start | bytes 196616 | tf_op jit(solution)/shard_map/ppermute | solution.py:23
  8.7 2.7 %collective-permute-done.1.refs_1_ = bf16[16,2048]{1,0:T(8,128)(2,1)S(1)} collective-permute-done((bf16[16,2048]{1,0:T(8,128)(2,1)}, bf16[16,2048]{1,0:T(8,128)(2,1)S(1)}, u32[]{:S(2)}, u32[]{:S(2)}) %collective-permute-start.1) | collective-permute-done | bytes 65568 | tf_op jit(solution)/shard_map/ppermute | solution.py:23
  14.3 4.8 %collective-permute-done.6.refs_2_ = bf16[64,2048]{1,0:T(8,128)(2,1)S(1)} collective-permute-done((bf16[64,2048]{1,0:T(8,128)(2,1)S(1)}, bf16[64,2048]{1,0:T(8,128)(2,1)S(1)}, u32[]{:S(2)}, u32[]{:S(2)}) %collective-permute-start.6) | collective-permute-done | bytes 262176 | tf_op jit(solution)/shard_map/ppermute | solution.py:23
  19.0 3.3 %collective-permute-start.7 = (bf16[64,2048]{1,0:T(8,128)(2,1)S(1)}, bf16[64,2048]{1,0:T(8,128)(2,1)S(1)}, u32[]{:S(2)}, u32[]{:S(2)}) collective-permute-start(bf16[64,2048]{1,0:T(8,128)(2,1)S(1)} %collective-permute-done.6.refs_2_), channel_id=1, source_target_pairs={{0,56},{8,0},{16,8},{24,16},{32,24},{40,32},{48,40},{56,48},{1,57}... | collective-permute-start | bytes 786440 | tf_op jit(solution)/shard_map/ppermute | solution.py:23
  22.8 3.4 %collective-permute-done.7.refs_4_.refs_0_ = bf16[64,2048]{1,0:T(8,128)(2,1)S(1)} collective-permute-done((bf16[64,2048]{1,0:T(8,128)(2,1)S(1)}, bf16[64,2048]{1,0:T(8,128)(2,1)S(1)}, u32[]{:S(2)}, u32[]{:S(2)}) %collective-permute-start.7) | collective-permute-done | bytes 262176 | tf_op jit(solution)/shard_map/ppermute | solution.py:23
  26.2 3.7 %collective-permute-start.8 = (bf16[64,2048]{1,0:T(8,128)(2,1)S(1)}, bf16[64,2048]{1,0:T(8,128)(2,1)S(1)}, u32[]{:S(2)}, u32[]{:S(2)}) collective-permute-start(bf16[64,2048]{1,0:T(8,128)(2,1)S(1)} %collective-permute-done.7.refs_4_.refs_0_), channel_id=1, source_target_pairs={{0,56},{8,0},{16,8},{24,16},{32,24},{40,32},{48,40},{56,48},{1,57}... | collective-permute-start | bytes 786440 | tf_op jit(solution)/shard_map/ppermute | solution.py:23
  32.5 2.7 %shard_map.112 = (bf16[128,1920]{1,0:T(8,128)(2,1)S(1)}, bf16[128,1920]{1,0:T(8,128)(2,1)S(1)}, bf16[256,2048]{1,0:T(8,128)(2,1)S(1)}, f32[8,128]{1,0:T(8,128)S(1)}) custom-call(s32[4]{0:T(128)S(1)} %pad_add_fusion.idx, bf16[64,2048]{1,0:T(8,128)(2,1)S(1)} %shard_map.111.refs_0_, bf16[64,2048]{1,0:T(8,128)(2,1)S(1)} %collective-permute-done.3.refs_1_, ...), custom_call_target="tpu_custom_call" | custom-call | flops 939524096 | bytes 3670016 | tf_op jit(solution)/shard_map/pallas_call | solution.py:34
  35.2 2.8 %collective-permute-done.5.up.refs_1_ = bf16[64,2048]{1,0:T(8,128)(2,1)S(1)} collective-permute-done((bf16[64,2048]{1,0:T(8,128)(2,1)S(1)}, bf16[64,2048]{1,0:T(8,128)(2,1)S(1)}, u32[]{:S(2)}, u32[]{:S(2)}) %collective-permute-start.5) | collective-permute-done | bytes 262176 | tf_op jit(solution)/shard_map/ppermute | solution.py:23
  38.1 3.4 %collective-permute-start.14 = (bf16[32,2048]{1,0:T(8,128)(2,1)S(1)}, bf16[32,2048]{1,0:T(8,128)(2,1)S(1)}, u32[]{:S(2)}, u32[]{:S(2)}) collective-permute-start(bf16[32,2048]{1,0:T(8,128)(2,1)S(1)} %get-tuple-element.68), channel_id=1, source_target_pairs={{0,56},{8,0},{16,8},{24,16},{32,24},{40,32},{48,40},{56,48},{1,57}... | collective-permute-start | bytes 393224 | tf_op jit(solution)/shard_map/ppermute | solution.py:23
  43.3 3.9 %shard_map.115 = (bf16[128,1920]{1,0:T(8,128)(2,1)S(1)}, bf16[128,1920]{1,0:T(8,128)(2,1)S(1)}, bf16[128,1920]{1,0:T(8,128)(2,1)S(1)}) custom-call(s32[4]{0:T(128)S(1)} %pad_add_fusion.idx, bf16[64,2048]{1,0:T(8,128)(2,1)S(1)} %collective-permute-done.7.refs_4_.refs_0_, ...), custom_call_target="tpu_custom_call", output_to_operand_aliasing={{2}: (4, {})} | custom-call | flops 1409286144 | bytes 7340032 | tf_op jit(solution)/shard_map/pallas_call | solution.py:34
  47.4 3.0 %shard_map.117 = (bf16[128,1920]{1,0:T(8,128)(2,1)S(1)}, bf16[128,1920]{1,0:T(8,128)(2,1)S(1)}) custom-call(s32[4]{0:T(128)S(1)} %pad_add_fusion.idx, bf16[32,2048]{1,0:T(8,128)(2,1)S(1)} %collective-permute-done.13.low, bf16[32,2048]{1,0:T(8,128)(2,1)S(1)} %collective-permute-done.14.high, ...), custom_call_target="tpu_custom_call", output_to_operand_aliasing={{0}: (6, {}), {1}: (7, {})} | custom-call | flops 469762048 | bytes 7340032 | tf_op jit(solution)/shard_map/pallas_call | solution.py:34
  53.3 2.9 %collective-permute-start.11 = (bf16[32,1920]{1,0:T(8,128)(2,1)S(1)}, bf16[32,1920]{1,0:T(8,128)(2,1)S(1)}, u32[]{:S(2)}, u32[]{:S(2)}) collective-permute-start(bf16[32,1920]{1,0:T(8,128)(2,1)S(1)} %get-tuple-element.66), channel_id=1, source_target_pairs={{0,4},{2,6},{4,0},{6,2},{1,5},{3,7},{5,1},{7,3},{8,12},{10,14},{12... | collective-permute-start | bytes 368648 | tf_op jit(solution)/shard_map/ppermute | solution.py:23
  63.0 2.7 %collective-permute-done.16.refs_5_ = bf16[32,1920]{1,0:T(8,128)(2,1)S(1)} collective-permute-done((bf16[32,1920]{1,0:T(8,128)(2,1)S(1)}, bf16[32,1920]{1,0:T(8,128)(2,1)S(1)}, u32[]{:S(2)}, u32[]{:S(2)}) %collective-permute-start.16) | collective-permute-done | bytes 122912 | tf_op jit(solution)/shard_map/ppermute | solution.py:23
  71.6 2.8 %collective-permute-done.21.refs_3_ = bf16[64,896]{1,0:T(8,128)(2,1)S(1)} collective-permute-done((bf16[64,896]{1,0:T(8,128)(2,1)S(1)}, bf16[64,896]{1,0:T(8,128)(2,1)S(1)}, u32[]{:S(2)}, u32[]{:S(2)}) %collective-permute-start.21) | collective-permute-done | bytes 114720 | tf_op jit(solution)/shard_map/ppermute | solution.py:23
  74.4 2.5 %collective-permute-done.20.refs_2_ = bf16[64,896]{1,0:T(8,128)(2,1)S(1)} collective-permute-done((bf16[64,896]{1,0:T(8,128)(2,1)S(1)}, bf16[64,896]{1,0:T(8,128)(2,1)S(1)}, u32[]{:S(2)}, u32[]{:S(2)}) %collective-permute-start.20) | collective-permute-done | bytes 114720 | tf_op jit(solution)/shard_map/ppermute | solution.py:23
  79.2 4.2 %shard_map.120 = (bf16[32,2048]{1,0:T(8,128)(2,1)S(1)}, bf16[32,2048]{1,0:T(8,128)(2,1)S(1)}, bf16[32,2048]{1,0:T(8,128)(2,1)S(1)}, bf16[32,2048]{1,0:T(8,128)(2...) custom-call(s32[4]{0:T(128)S(1)} %pad_add_fusion.idx, ...), custom_call_target="tpu_custom_call" | custom-call | flops 1879048192 | bytes 3670016 | tf_op jit(solution)/shard_map/pallas_call | solution.py:34
  85.6 3.5 %collective-permute-done.26.came = bf16[32,2048]{1,0:T(8,128)(2,1)S(1)} collective-permute-done((bf16[32,2048]{1,0:T(8,128)(2,1)S(1)}, bf16[32,2048]{1,0:T(8,128)(2,1)S(1)}, u32[]{:S(2)}, u32[]{:S(2)}) %collective-permute-start.26) | collective-permute-done | bytes 131104 | tf_op jit(solution)/shard_map/ppermute | solution.py:23
  91.2 2.8 %collective-permute-start.38 = (bf16[32,2048]{1,0:T(8,128)(2,1)S(1)}, bf16[32,2048]{1,0:T(8,128)(2,1)S(1)}, u32[]{:S(2)}, u32[]{:S(2)}) collective-permute-start(bf16[32,2048]{1,0:T(8,128)(2,1)S(1)} %get-tuple-element.92), channel_id=1, source_target_pairs={{0,56},{8,0},{16,8},{24,16},{32,24},{40,32},{48,40},{56,48},{1,57}... | collective-permute-start | bytes 393224 | tf_op jit(solution)/shard_map/ppermute | solution.py:23
  98.2 3.4 %collective-permute-start.39 = (bf16[32,2048]{1,0:T(8,128)(2,1)S(1)}, bf16[32,2048]{1,0:T(8,128)(2,1)S(1)}, u32[]{:S(2)}, u32[]{:S(2)}) collective-permute-start(bf16[32,2048]{1,0:T(8,128)(2,1)S(1)} %shard_map.130), channel_id=1, source_target_pairs={{0,56},{8,0},{16,8},{24,16},{32,24},{40,32},{48,40},{56,48},{1,57}... | collective-permute-start | bytes 393224 | tf_op jit(solution)/shard_map/ppermute | solution.py:23
  101.9 2.4 %collective-permute-start.29 = (bf16[32,2048]{1,0:T(8,128)(2,1)S(1)}, bf16[32,2048]{1,0:T(8,128)(2,1)S(1)}, u32[]{:S(2)}, u32[]{:S(2)}) collective-permute-start(bf16[32,2048]{1,0:T(8,128)(2,1)S(1)} %shard_map.123), channel_id=1, source_target_pairs={{0,56},{8,0},{16,8},{24,16},{32,24},{40,32},{48,40},{56,48},{1,57}... | collective-permute-start | bytes 393224 | tf_op jit(solution)/shard_map/ppermute | solution.py:23
  105.3 2.9 %collective-permute-start.40 = (bf16[32,2048]{1,0:T(8,128)(2,1)S(1)}, bf16[32,2048]{1,0:T(8,128)(2,1)S(1)}, u32[]{:S(2)}, u32[]{:S(2)}) collective-permute-start(bf16[32,2048]{1,0:T(8,128)(2,1)S(1)} %shard_map.131), channel_id=1, source_target_pairs={{0,56},{8,0},{16,8},{24,16},{32,24},{40,32},{48,40},{56,48},{1,57}... | collective-permute-start | bytes 393224 | tf_op jit(solution)/shard_map/ppermute | solution.py:23
  110.7 2.6 %collective-permute-done.37.one = bf16[32,2048]{1,0:T(8,128)(2,1)S(1)} collective-permute-done((bf16[32,2048]{1,0:T(8,128)(2,1)S(1)}, bf16[32,2048]{1,0:T(8,128)(2,1)S(1)}, u32[]{:S(2)}, u32[]{:S(2)}) %collective-permute-start.37) | collective-permute-done | bytes 131104 | tf_op jit(solution)/shard_map/ppermute | solution.py:23
  115.1 4.0 %collective-permute-done.41.two = bf16[16,2048]{1,0:T(8,128)(2,1)S(1)} collective-permute-done((bf16[16,2048]{1,0:T(8,128)(2,1)S(1)}, bf16[16,2048]{1,0:T(8,128)(2,1)S(1)}, u32[]{:S(2)}, u32[]{:S(2)}) %collective-permute-start.41) | collective-permute-done | bytes 65568 | tf_op jit(solution)/shard_map/ppermute | solution.py:23
  (102 shorter events, 45.1 us)
Async XLA Ops:
  12.2 6.9 %collective-permute-start.6 = (bf16[64,2048]{1,0:T(8,128)(2,1)S(1)}, bf16[64,2048]{1,0:T(8,128)(2,1)S(1)}, u32[]{:S(2)}, u32[]{:S(2)}) collective-permute-start(bf16[64,2048]{1,0:T(8,128)(2,1)S(1)} %shard_map.111.refs_0_), channel_id=1, source_target_pairs={{0,56},{8,0},{16,8},{24,16},{32,24},{40,32},{48,40},{56,48},{1,57}... | collective-permute-start | bytes 786440 | tf_op jit(solution)/shard_map/ppermute | solution.py:23
  12.3 10.4 %collective-permute-start.3 = (bf16[64,2048]{1,0:T(8,128)(2,1)S(1)}, bf16[64,2048]{1,0:T(8,128)(2,1)S(1)}, u32[]{:S(2)}, u32[]{:S(2)}) collective-permute-start(bf16[64,2048]{1,0:T(8,128)(2,1)S(1)} %shard_map.111.refs_0_), channel_id=1, source_target_pairs={{0,8},{8,16},{16,24},{24,32},{32,40},{40,48},{48,56},{56,0},{1,9},... | collective-permute-start | bytes 786440 | tf_op jit(solution)/shard_map/ppermute | solution.py:23
  19.0 7.2 %collective-permute-start.7 = (bf16[64,2048]{1,0:T(8,128)(2,1)S(1)}, bf16[64,2048]{1,0:T(8,128)(2,1)S(1)}, u32[]{:S(2)}, u32[]{:S(2)}) collective-permute-start(bf16[64,2048]{1,0:T(8,128)(2,1)S(1)} %collective-permute-done.6.refs_2_), channel_id=1, source_target_pairs={{0,56},{8,0},{16,8},{24,16},{32,24},{40,32},{48,40},{56,48},{1,57}... | collective-permute-start | bytes 786440 | tf_op jit(solution)/shard_map/ppermute | solution.py:23
  22.8 7.6 %collective-permute-start.4 = (bf16[64,2048]{1,0:T(8,128)(2,1)S(1)}, bf16[64,2048]{1,0:T(8,128)(2,1)S(1)}, u32[]{:S(2)}, u32[]{:S(2)}) collective-permute-start(bf16[64,2048]{1,0:T(8,128)(2,1)S(1)} %collective-permute-done.3.refs_1_), channel_id=1, source_target_pairs={{0,8},{8,16},{16,24},{24,32},{32,40},{40,48},{48,56},{56,0},{1,9},... | collective-permute-start | bytes 786440 | tf_op jit(solution)/shard_map/ppermute | solution.py:23
  26.2 9.0 %collective-permute-start.8 = (bf16[64,2048]{1,0:T(8,128)(2,1)S(1)}, bf16[64,2048]{1,0:T(8,128)(2,1)S(1)}, u32[]{:S(2)}, u32[]{:S(2)}) collective-permute-start(bf16[64,2048]{1,0:T(8,128)(2,1)S(1)} %collective-permute-done.7.refs_4_.refs_0_), channel_id=1, source_target_pairs={{0,56},{8,0},{16,8},{24,16},{32,24},{40,32},{48,40},{56,48},{1,57}... | collective-permute-start | bytes 786440 | tf_op jit(solution)/shard_map/ppermute | solution.py:23
  30.4 7.7 %collective-permute-start.5 = (bf16[64,2048]{1,0:T(8,128)(2,1)S(1)}, bf16[64,2048]{1,0:T(8,128)(2,1)S(1)}, u32[]{:S(2)}, u32[]{:S(2)}) collective-permute-start(bf16[64,2048]{1,0:T(8,128)(2,1)S(1)} %collective-permute-done.4.refs_3_), channel_id=1, source_target_pairs={{0,8},{8,16},{16,24},{24,32},{32,40},{40,48},{48,56},{56,0},{1,9},... | collective-permute-start | bytes 786440 | tf_op jit(solution)/shard_map/ppermute | solution.py:23
  38.1 9.3 %collective-permute-start.14 = (bf16[32,2048]{1,0:T(8,128)(2,1)S(1)}, bf16[32,2048]{1,0:T(8,128)(2,1)S(1)}, u32[]{:S(2)}, u32[]{:S(2)}) collective-permute-start(bf16[32,2048]{1,0:T(8,128)(2,1)S(1)} %get-tuple-element.68), channel_id=1, source_target_pairs={{0,56},{8,0},{16,8},{24,16},{32,24},{40,32},{48,40},{56,48},{1,57}... | collective-permute-start | bytes 393224 | tf_op jit(solution)/shard_map/ppermute | solution.py:23
  50.4 7.1 %collective-permute-start.15 = (bf16[128,1920]{1,0:T(8,128)(2,1)S(1)}, bf16[128,1920]{1,0:T(8,128)(2,1)S(1)}, u32[]{:S(2)}, u32[]{:S(2)}) collective-permute-start(bf16[128,1920]{1,0:T(8,128)(2,1)S(1)} %get-tuple-element.72), channel_id=1, source_target_pairs={{0,1},{1,0},{2,3},{3,2},{4,5},{5,4},{6,7},{7,6},{8,9},{9,8},{10,11... | collective-permute-start | bytes 1474568 | tf_op jit(solution)/shard_map/ppermute | solution.py:23
  51.6 8.1 %collective-permute-start.10 = (bf16[32,1920]{1,0:T(8,128)(2,1)S(1)}, bf16[32,1920]{1,0:T(8,128)(2,1)S(1)}, u32[]{:S(2)}, u32[]{:S(2)}) collective-permute-start(bf16[32,1920]{1,0:T(8,128)(2,1)S(1)} %get-tuple-element.65), channel_id=1, source_target_pairs={{0,2},{2,4},{4,6},{6,0},{1,3},{3,5},{5,7},{7,1},{8,10},{10,12},{12... | collective-permute-start | bytes 368648 | tf_op jit(solution)/shard_map/ppermute | solution.py:23
  53.3 9.7 %collective-permute-start.11 = (bf16[32,1920]{1,0:T(8,128)(2,1)S(1)}, bf16[32,1920]{1,0:T(8,128)(2,1)S(1)}, u32[]{:S(2)}, u32[]{:S(2)}) collective-permute-start(bf16[32,1920]{1,0:T(8,128)(2,1)S(1)} %get-tuple-element.66), channel_id=1, source_target_pairs={{0,4},{2,6},{4,0},{6,2},{1,5},{3,7},{5,1},{7,3},{8,12},{10,14},{12... | collective-permute-start | bytes 368648 | tf_op jit(solution)/shard_map/ppermute | solution.py:23
  56.2 6.8 %collective-permute-start.12 = (bf16[32,1920]{1,0:T(8,128)(2,1)S(1)}, bf16[32,1920]{1,0:T(8,128)(2,1)S(1)}, u32[]{:S(2)}, u32[]{:S(2)}) collective-permute-start(bf16[32,1920]{1,0:T(8,128)(2,1)S(1)} %get-tuple-element.67), channel_id=1, source_target_pairs={{0,6},{2,0},{4,2},{6,4},{1,7},{3,1},{5,3},{7,5},{8,14},{10,8},{12,... | collective-permute-start | bytes 368648 | tf_op jit(solution)/shard_map/ppermute | solution.py:23
  58.2 7.5 %collective-permute-start.16 = (bf16[32,1920]{1,0:T(8,128)(2,1)S(1)}, bf16[32,1920]{1,0:T(8,128)(2,1)S(1)}, u32[]{:S(2)}, u32[]{:S(2)}) collective-permute-start(bf16[32,1920]{1,0:T(8,128)(2,1)S(1)} %get-tuple-element.74), channel_id=1, source_target_pairs={{0,2},{2,4},{4,6},{6,0},{1,3},{3,5},{5,7},{7,1},{8,10},{10,12},{12... | collective-permute-start | bytes 368648 | tf_op jit(solution)/shard_map/ppermute | solution.py:23
  59.0 8.4 %collective-permute-start.17 = (bf16[32,1920]{1,0:T(8,128)(2,1)S(1)}, bf16[32,1920]{1,0:T(8,128)(2,1)S(1)}, u32[]{:S(2)}, u32[]{:S(2)}) collective-permute-start(bf16[32,1920]{1,0:T(8,128)(2,1)S(1)} %get-tuple-element.75), channel_id=1, source_target_pairs={{0,4},{2,6},{4,0},{6,2},{1,5},{3,7},{5,1},{7,3},{8,12},{10,14},{12... | collective-permute-start | bytes 368648 | tf_op jit(solution)/shard_map/ppermute | solution.py:23
  59.8 7.6 %collective-permute-start.18 = (bf16[32,1920]{1,0:T(8,128)(2,1)S(1)}, bf16[32,1920]{1,0:T(8,128)(2,1)S(1)}, u32[]{:S(2)}, u32[]{:S(2)}) collective-permute-start(bf16[32,1920]{1,0:T(8,128)(2,1)S(1)} %get-tuple-element.76), channel_id=1, source_target_pairs={{0,6},{2,0},{4,2},{6,4},{1,7},{3,1},{5,3},{7,5},{8,14},{10,8},{12,... | collective-permute-start | bytes 368648 | tf_op jit(solution)/shard_map/ppermute | solution.py:23
  67.6 6.8 %collective-permute-start.21 = (bf16[64,896]{1,0:T(8,128)(2,1)S(1)}, bf16[64,896]{1,0:T(8,128)(2,1)S(1)}, u32[]{:S(2)}, u32[]{:S(2)}) collective-permute-start(bf16[64,896]{1,0:T(8,128)(2,1)S(1)} %shard_map.119.refs_0_), channel_id=1, source_target_pairs={{0,6},{2,0},{4,2},{6,4},{1,7},{3,1},{5,3},{7,5},{8,14},{10,8},{12,... | collective-permute-start | bytes 344072 | tf_op jit(solution)/shard_map/ppermute | solution.py:23
  70.0 6.9 %collective-permute-start.20 = (bf16[64,896]{1,0:T(8,128)(2,1)S(1)}, bf16[64,896]{1,0:T(8,128)(2,1)S(1)}, u32[]{:S(2)}, u32[]{:S(2)}) collective-permute-start(bf16[64,896]{1,0:T(8,128)(2,1)S(1)} %shard_map.119.refs_0_), channel_id=1, source_target_pairs={{0,4},{2,6},{4,0},{6,2},{1,5},{3,7},{5,1},{7,3},{8,12},{10,14},{12... | collective-permute-start | bytes 344072 | tf_op jit(solution)/shard_map/ppermute | solution.py:23
  71.0 7.0 %collective-permute-start.19 = (bf16[64,896]{1,0:T(8,128)(2,1)S(1)}, bf16[64,896]{1,0:T(8,128)(2,1)S(1)}, u32[]{:S(2)}, u32[]{:S(2)}) collective-permute-start(bf16[64,896]{1,0:T(8,128)(2,1)S(1)} %shard_map.119.refs_0_), channel_id=1, source_target_pairs={{0,2},{2,4},{4,6},{6,0},{1,3},{3,5},{5,7},{7,1},{8,10},{10,12},{12... | collective-permute-start | bytes 344072 | tf_op jit(solution)/shard_map/ppermute | solution.py:23
  85.6 8.5 %collective-permute-start.34 = (bf16[32,2048]{1,0:T(8,128)(2,1)S(1)}, bf16[32,2048]{1,0:T(8,128)(2,1)S(1)}, u32[]{:S(2)}, u32[]{:S(2)}) collective-permute-start(bf16[32,2048]{1,0:T(8,128)(2,1)S(1)} %get-tuple-element.88), channel_id=1, source_target_pairs={{0,8},{8,16},{16,24},{24,32},{32,40},{40,48},{48,56},{56,0},{1,9},... | collective-permute-start | bytes 393224 | tf_op jit(solution)/shard_map/ppermute | solution.py:23
  85.6 8.6 %collective-permute-start.30 = (bf16[32,2048]{1,0:T(8,128)(2,1)S(1)}, bf16[32,2048]{1,0:T(8,128)(2,1)S(1)}, u32[]{:S(2)}, u32[]{:S(2)}) collective-permute-start(bf16[32,2048]{1,0:T(8,128)(2,1)S(1)} %get-tuple-element.82), channel_id=1, source_target_pairs={{0,8},{8,16},{16,24},{24,32},{32,40},{40,48},{48,56},{56,0},{1,9},... | collective-permute-start | bytes 393224 | tf_op jit(solution)/shard_map/ppermute | solution.py:23
  91.2 6.9 %collective-permute-start.38 = (bf16[32,2048]{1,0:T(8,128)(2,1)S(1)}, bf16[32,2048]{1,0:T(8,128)(2,1)S(1)}, u32[]{:S(2)}, u32[]{:S(2)}) collective-permute-start(bf16[32,2048]{1,0:T(8,128)(2,1)S(1)} %get-tuple-element.92), channel_id=1, source_target_pairs={{0,56},{8,0},{16,8},{24,16},{32,24},{40,32},{48,40},{56,48},{1,57}... | collective-permute-start | bytes 393224 | tf_op jit(solution)/shard_map/ppermute | solution.py:23
  94.1 7.5 %collective-permute-start.35 = (bf16[32,2048]{1,0:T(8,128)(2,1)S(1)}, bf16[32,2048]{1,0:T(8,128)(2,1)S(1)}, u32[]{:S(2)}, u32[]{:S(2)}) collective-permute-start(bf16[32,2048]{1,0:T(8,128)(2,1)S(1)} %shard_map.127), channel_id=1, source_target_pairs={{0,8},{8,16},{16,24},{24,32},{32,40},{40,48},{48,56},{56,0},{1,9},... | collective-permute-start | bytes 393224 | tf_op jit(solution)/shard_map/ppermute | solution.py:23
  94.2 7.5 %collective-permute-start.31 = (bf16[32,2048]{1,0:T(8,128)(2,1)S(1)}, bf16[32,2048]{1,0:T(8,128)(2,1)S(1)}, u32[]{:S(2)}, u32[]{:S(2)}) collective-permute-start(bf16[32,2048]{1,0:T(8,128)(2,1)S(1)} %shard_map.124), channel_id=1, source_target_pairs={{0,8},{8,16},{16,24},{24,32},{32,40},{40,48},{48,56},{56,0},{1,9},... | collective-permute-start | bytes 393224 | tf_op jit(solution)/shard_map/ppermute | solution.py:23
  98.2 7.0 %collective-permute-start.39 = (bf16[32,2048]{1,0:T(8,128)(2,1)S(1)}, bf16[32,2048]{1,0:T(8,128)(2,1)S(1)}, u32[]{:S(2)}, u32[]{:S(2)}) collective-permute-start(bf16[32,2048]{1,0:T(8,128)(2,1)S(1)} %shard_map.130), channel_id=1, source_target_pairs={{0,56},{8,0},{16,8},{24,16},{32,24},{40,32},{48,40},{56,48},{1,57}... | collective-permute-start | bytes 393224 | tf_op jit(solution)/shard_map/ppermute | solution.py:23
  101.8 6.7 %collective-permute-start.32 = (bf16[32,2048]{1,0:T(8,128)(2,1)S(1)}, bf16[32,2048]{1,0:T(8,128)(2,1)S(1)}, u32[]{:S(2)}, u32[]{:S(2)}) collective-permute-start(bf16[32,2048]{1,0:T(8,128)(2,1)S(1)} %shard_map.125), channel_id=1, source_target_pairs={{0,8},{8,16},{16,24},{24,32},{32,40},{40,48},{48,56},{56,0},{1,9},... | collective-permute-start | bytes 393224 | tf_op jit(solution)/shard_map/ppermute | solution.py:23
  (26 other events, 189.6 us)

commit v6 on v3

--- a/solution.py
+++ b/solution.py
@@ -18,6 +18,7 @@
 EARLY = 4
 FAR = 5
 AWAY = (2, 1, 3)
+SLOTS = (0, 2, 1, 3)
 
 
 def shift(v, axis, by, n):
@@ -122,8 +123,9 @@
         out[:, cols] = (got * scales[h : h + 1, :]).astype(bf16)
 
 
-def seat(own, out):
+def seat(own, inv_gain2, out, kept):
     out[pl.ds(0, own.shape[0]), :] = own[...]
+    kept[...] = inv_gain2[...]
 
 
 def join(first, *refs):
@@ -315,12 +317,14 @@
         limit=60 * MIB,
     )
 
-    own = call(seat, shape(piece, feats), [scaled], "v", moved=2 * rows * feats)
+    own, inv_gain2 = call(
+        seat, [shape(piece, feats), shape(per, HEAD_DIM, kind=f32)], [scaled, inv_gain2], "vv", moved=2 * rows * feats
+    )
     from_x = {k: shift(scaled, "x", k, NX) for k in AWAY}
     own = call(
         join,
         shape(piece, feats),
-        [own] + [from_x[k] for k in range(1, NX)],
+        [own] + [from_x[k] for k in SLOTS[1:]],
         "v" * NX,
         moved=4 * piece * feats,
         alias={0: 0},
@@ -427,10 +431,10 @@
     far = NZ // 2
     low = [chain(0, -1, far), chain(0, 1, far - 1)]
     high = [chain(1, 1, far), chain(1, -1, far - 1)]
-    mine, one = call(
+    mine, two = call(
         z_sum, [shape(rows, feats, kind=f32), shape(rows, feats)], [terms[0][0]] + low, "vvv", moved=4 * piece * feats
     )
-    two, three = call(z_sum, [shape(rows, feats)] * 2, [terms[0][1]] + high, "vvv", moved=4 * piece * feats)
+    one, three = call(z_sum, [shape(rows, feats)] * 2, [terms[0][1]] + high, "vvv", moved=4 * piece * feats)
     sent = {1: one, 2: two, 3: three}
     parts = {k: shift(sent[k], "x", -k, NX) for k in AWAY}
     return call(finish, shape(rows, feats), [stream, mine] + [parts[k] for k in range(1, NX)], "v" * 5, moved=20 * rows * feats)

time: 121 us -> 122 us (level)
  starting transfers between devices: 53.9 us -> 56.3 us
  waiting for transfers between devices: 40.3 us -> 39 us
    ppermute x43, starting transfers between devices: 53.9 us -> 56.3 us  [shift(): return lax.ppermute(v, axis, [(i, (i + by) % n) for i in range(n)])]
    ppermute x43, waiting for transfers between devices: 40.3 us -> 39 us  [shift(): return lax.ppermute(v, axis, [(i, (i + by) % n) for i in range(n)])]
    unnamed x16 -> x14, local copies, waits for them, and re-layouts: 3.63 us -> 3.63 us
  transfers between devices with their start and end apart: 43 -> 43, of which waited for: 23 -> 21; matrix products, arithmetic and copies ran while one was open for 0% -> 0% of each run, Pallas kernels for 14% -> 13%
where the time goes in v6:
time: 122 us
  starting transfers between devices  56.3 us (46%)
  waiting for transfers between devices  39 us (32%)
  Pallas kernels  22.8 us (19%)
  local copies, waits for them, and re-layouts  3.63 us (3%)
    ppermute x43, starting transfers between devices, shift(): return lax.ppermute(v, axis, [(i, (i + by) % n) for i in range(n)])  56.3 us
    ppermute x43, waiting for transfers between devices, shift(): return lax.ppermute(v, axis, [(i, (i + by) % n) for i in range(n)])  39 us
    pallas_call x26, Pallas kernels, call(): pl.pallas_call(kernel, out_shape=whole, in_specs=[pl.BlockSpec(memory_spa...  22.8 us
    unnamed x14, local copies, waits for them, and re-layouts  3.63 us
  transfers between devices with their start and end apart: 43, of which 21 were waited for; matrix products, arithmetic and copies ran while one was open for 0% of the time, Pallas kernels for 13%

profile of v6, /device:TPU:32, one launch (start us, length us, event | category | flops | bytes accessed | tf_op | source)
XLA Modules:
  0.0 122.0 jit_solution(17097722420264298629)
XLA Ops:
  0.0 2.6 %shard_map.109 = (f32[16,2048]{1,0:T(8,128)}, f32[16,128]{1,0:T(8,128)}, bf16[16,2048]{1,0:T(8,128)(2,1)}) custom-call(s32[16]{0:T(128)} %lengths_in.1, bf16[16,2048]{1,0:T(8,128)(2,1)} %hidden_in.1, bf16[16,2048]{1,0:T(8,128)(2,1)} %queries_in.1, bf16[16,128,128]{2,1,0:T(8,128)(2,1)} %keys_in.1, bf16[16,128,128]{2,1,0:T(8,128)(2,1)} %values_in.1, ...), custom_call_target="tpu_custom_call" | custom-call | bytes 1048576 | tf_op jit(solution)/shard_map/pallas_call | solution.py:36
  2.6 2.8 %collective-permute-start.2 = (bf16[16,2048]{1,0:T(8,128)(2,1)}, bf16[16,2048]{1,0:T(8,128)(2,1)S(1)}, u32[]{:S(2)}, u32[]{:S(2)}) collective-permute-start(bf16[16,2048]{1,0:T(8,128)(2,1)} %get-tuple-element.52.own), channel_id=1, source_target_pairs={{0,192},{64,0},{128,64},{192,128},{1,193},{65,1},{129,65},{193,129... | collective-permute-start | bytes 196616 | tf_op jit(solution)/shard_map/ppermute | solution.py:25
  9.3 2.6 %collective-permute-done.1.refs_1_ = bf16[16,2048]{1,0:T(8,128)(2,1)S(1)} collective-permute-done((bf16[16,2048]{1,0:T(8,128)(2,1)}, bf16[16,2048]{1,0:T(8,128)(2,1)S(1)}, u32[]{:S(2)}, u32[]{:S(2)}) %collective-permute-start.1) | collective-permute-done | bytes 65568 | tf_op jit(solution)/shard_map/ppermute | solution.py:25
  14.0 4.8 %collective-permute-done.6.refs_2_ = bf16[64,2048]{1,0:T(8,128)(2,1)S(1)} collective-permute-done((bf16[64,2048]{1,0:T(8,128)(2,1)S(1)}, bf16[64,2048]{1,0:T(8,128)(2,1)S(1)}, u32[]{:S(2)}, u32[]{:S(2)}) %collective-permute-start.6) | collective-permute-done | bytes 262176 | tf_op jit(solution)/shard_map/ppermute | solution.py:25
  18.9 3.3 %collective-permute-start.7 = (bf16[64,2048]{1,0:T(8,128)(2,1)S(1)}, bf16[64,2048]{1,0:T(8,128)(2,1)S(1)}, u32[]{:S(2)}, u32[]{:S(2)}) collective-permute-start(bf16[64,2048]{1,0:T(8,128)(2,1)S(1)} %collective-permute-done.6.refs_2_), channel_id=1, source_target_pairs={{0,56},{8,0},{16,8},{24,16},{32,24},{40,32},{48,40},{56,48},{1,57}... | collective-permute-start | bytes 786440 | tf_op jit(solution)/shard_map/ppermute | solution.py:25
  22.6 3.4 %collective-permute-done.7.refs_4_.refs_0_ = bf16[64,2048]{1,0:T(8,128)(2,1)S(1)} collective-permute-done((bf16[64,2048]{1,0:T(8,128)(2,1)S(1)}, bf16[64,2048]{1,0:T(8,128)(2,1)S(1)}, u32[]{:S(2)}, u32[]{:S(2)}) %collective-permute-start.7) | collective-permute-done | bytes 262176 | tf_op jit(solution)/shard_map/ppermute | solution.py:25
  26.1 3.7 %collective-permute-start.8 = (bf16[64,2048]{1,0:T(8,128)(2,1)S(1)}, bf16[64,2048]{1,0:T(8,128)(2,1)S(1)}, u32[]{:S(2)}, u32[]{:S(2)}) collective-permute-start(bf16[64,2048]{1,0:T(8,128)(2,1)S(1)} %collective-permute-done.7.refs_4_.refs_0_), channel_id=1, source_target_pairs={{0,56},{8,0},{16,8},{24,16},{32,24},{40,32},{48,40},{56,48},{1,57}... | collective-permute-start | bytes 786440 | tf_op jit(solution)/shard_map/ppermute | solution.py:25
  32.3 2.7 %shard_map.112 = (bf16[128,1920]{1,0:T(8,128)(2,1)S(1)}, bf16[128,1920]{1,0:T(8,128)(2,1)S(1)}, bf16[256,2048]{1,0:T(8,128)(2,1)S(1)}, f32[8,128]{1,0:T(8,128)S(1)}) custom-call(s32[4]{0:T(128)S(1)} %pad_add_fusion.idx, bf16[64,2048]{1,0:T(8,128)(2,1)S(1)} %shard_map.111.refs_0_, bf16[64,2048]{1,0:T(8,128)(2,1)S(1)} %collective-permute-done.3.refs_1_, ...), custom_call_target="tpu_custom_call" | custom-call | flops 939524096 | bytes 3670016 | tf_op jit(solution)/shard_map/pallas_call | solution.py:36
  35.0 2.8 %collective-permute-done.5.up.refs_1_ = bf16[64,2048]{1,0:T(8,128)(2,1)S(1)} collective-permute-done((bf16[64,2048]{1,0:T(8,128)(2,1)S(1)}, bf16[64,2048]{1,0:T(8,128)(2,1)S(1)}, u32[]{:S(2)}, u32[]{:S(2)}) %collective-permute-start.5) | collective-permute-done | bytes 262176 | tf_op jit(solution)/shard_map/ppermute | solution.py:25
  37.8 3.3 %collective-permute-start.14 = (bf16[32,2048]{1,0:T(8,128)(2,1)S(1)}, bf16[32,2048]{1,0:T(8,128)(2,1)S(1)}, u32[]{:S(2)}, u32[]{:S(2)}) collective-permute-start(bf16[32,2048]{1,0:T(8,128)(2,1)S(1)} %get-tuple-element.68), channel_id=1, source_target_pairs={{0,56},{8,0},{16,8},{24,16},{32,24},{40,32},{48,40},{56,48},{1,57}... | collective-permute-start | bytes 393224 | tf_op jit(solution)/shard_map/ppermute | solution.py:25
  42.9 3.9 %shard_map.115 = (bf16[128,1920]{1,0:T(8,128)(2,1)S(1)}, bf16[128,1920]{1,0:T(8,128)(2,1)S(1)}, bf16[128,1920]{1,0:T(8,128)(2,1)S(1)}) custom-call(s32[4]{0:T(128)S(1)} %pad_add_fusion.idx, bf16[64,2048]{1,0:T(8,128)(2,1)S(1)} %collective-permute-done.7.refs_4_.refs_0_, ...), custom_call_target="tpu_custom_call", output_to_operand_aliasing={{2}: (4, {})} | custom-call | flops 1409286144 | bytes 7340032 | tf_op jit(solution)/shard_map/pallas_call | solution.py:36
  47.1 3.0 %shard_map.117 = (bf16[128,1920]{1,0:T(8,128)(2,1)S(1)}, bf16[128,1920]{1,0:T(8,128)(2,1)S(1)}) custom-call(s32[4]{0:T(128)S(1)} %pad_add_fusion.idx, bf16[32,2048]{1,0:T(8,128)(2,1)S(1)} %collective-permute-done.13.low, bf16[32,2048]{1,0:T(8,128)(2,1)S(1)} %collective-permute-done.14.high, ...), custom_call_target="tpu_custom_call", output_to_operand_aliasing={{0}: (6, {}), {1}: (7, {})} | custom-call | flops 469762048 | bytes 7340032 | tf_op jit(solution)/shard_map/pallas_call | solution.py:36
  53.0 2.9 %collective-permute-start.11 = (bf16[32,1920]{1,0:T(8,128)(2,1)S(1)}, bf16[32,1920]{1,0:T(8,128)(2,1)S(1)}, u32[]{:S(2)}, u32[]{:S(2)}) collective-permute-start(bf16[32,1920]{1,0:T(8,128)(2,1)S(1)} %get-tuple-element.66), channel_id=1, source_target_pairs={{0,4},{2,6},{4,0},{6,2},{1,5},{3,7},{5,1},{7,3},{8,12},{10,14},{12... | collective-permute-start | bytes 368648 | tf_op jit(solution)/shard_map/ppermute | solution.py:25
  62.6 2.7 %collective-permute-done.16.refs_5_ = bf16[32,1920]{1,0:T(8,128)(2,1)S(1)} collective-permute-done((bf16[32,1920]{1,0:T(8,128)(2,1)S(1)}, bf16[32,1920]{1,0:T(8,128)(2,1)S(1)}, u32[]{:S(2)}, u32[]{:S(2)}) %collective-permute-start.16) | collective-permute-done | bytes 122912 | tf_op jit(solution)/shard_map/ppermute | solution.py:25
  71.3 2.8 %collective-permute-done.21.refs_3_ = bf16[64,896]{1,0:T(8,128)(2,1)S(1)} collective-permute-done((bf16[64,896]{1,0:T(8,128)(2,1)S(1)}, bf16[64,896]{1,0:T(8,128)(2,1)S(1)}, u32[]{:S(2)}, u32[]{:S(2)}) %collective-permute-start.21) | collective-permute-done | bytes 114720 | tf_op jit(solution)/shard_map/ppermute | solution.py:25
  74.1 2.5 %collective-permute-done.20.refs_2_ = bf16[64,896]{1,0:T(8,128)(2,1)S(1)} collective-permute-done((bf16[64,896]{1,0:T(8,128)(2,1)S(1)}, bf16[64,896]{1,0:T(8,128)(2,1)S(1)}, u32[]{:S(2)}, u32[]{:S(2)}) %collective-permute-start.20) | collective-permute-done | bytes 114720 | tf_op jit(solution)/shard_map/ppermute | solution.py:25
  78.9 2.8 %shard_map.121 = (bf16[32,2048]{1,0:T(8,128)(2,1)S(1)}, bf16[32,2048]{1,0:T(8,128)(2,1)S(1)}, bf16[32,2048]{1,0:T(8,128)(2,1)S(1)}, bf16[32,2048]{1,0:T(8,128)(2...) custom-call(s32[4]{0:T(128)S(1)} %pad_add_fusion.idx, bf16[64,896]{1,0:T(8,128)(2,1)S(1)} %shard_map.119.refs_0_, ...), custom_call_target="tpu_custom_call" | custom-call | flops 704643072 | bytes 3670016 | tf_op jit(solution)/shard_map/pallas_call | solution.py:36
  85.8 3.4 %shard_map.120 = (bf16[32,2048]{1,0:T(8,128)(2,1)S(1)}, bf16[32,2048]{1,0:T(8,128)(2,1)S(1)}, bf16[32,2048]{1,0:T(8,128)(2,1)S(1)}, bf16[32,2048]{1,0:T(8,128)(2...) custom-call(s32[4]{0:T(128)S(1)} %pad_add_fusion.idx, ...), custom_call_target="tpu_custom_call" | custom-call | flops 1174405120 | bytes 3670016 | tf_op jit(solution)/shard_map/pallas_call | solution.py:36
  89.3 3.3 %collective-permute-start.27 = (bf16[32,2048]{1,0:T(8,128)(2,1)S(1)}, bf16[32,2048]{1,0:T(8,128)(2,1)S(1)}, u32[]{:S(2)}, u32[]{:S(2)}) collective-permute-start(bf16[32,2048]{1,0:T(8,128)(2,1)S(1)} %shard_map.122), channel_id=1, source_target_pairs={{0,56},{8,0},{16,8},{24,16},{32,24},{40,32},{48,40},{56,48},{1,57}... | collective-permute-start | bytes 393224 | tf_op jit(solution)/shard_map/ppermute | solution.py:25
  96.1 2.6 %collective-permute-start.28 = (bf16[32,2048]{1,0:T(8,128)(2,1)S(1)}, bf16[32,2048]{1,0:T(8,128)(2,1)S(1)}, u32[]{:S(2)}, u32[]{:S(2)}) collective-permute-start(bf16[32,2048]{1,0:T(8,128)(2,1)S(1)} %shard_map.123), channel_id=1, source_target_pairs={{0,56},{8,0},{16,8},{24,16},{32,24},{40,32},{48,40},{56,48},{1,57}... | collective-permute-start | bytes 393224 | tf_op jit(solution)/shard_map/ppermute | solution.py:25
  101.2 2.5 %collective-permute-start.29 = (bf16[32,2048]{1,0:T(8,128)(2,1)S(1)}, bf16[32,2048]{1,0:T(8,128)(2,1)S(1)}, u32[]{:S(2)}, u32[]{:S(2)}) collective-permute-start(bf16[32,2048]{1,0:T(8,128)(2,1)S(1)} %shard_map.124), channel_id=1, source_target_pairs={{0,56},{8,0},{16,8},{24,16},{32,24},{40,32},{48,40},{56,48},{1,57}... | collective-permute-start | bytes 393224 | tf_op jit(solution)/shard_map/ppermute | solution.py:25
  103.8 3.1 %collective-permute-start.39 = (bf16[32,2048]{1,0:T(8,128)(2,1)S(1)}, bf16[32,2048]{1,0:T(8,128)(2,1)S(1)}, u32[]{:S(2)}, u32[]{:S(2)}) collective-permute-start(bf16[32,2048]{1,0:T(8,128)(2,1)S(1)} %shard_map.132), channel_id=1, source_target_pairs={{0,56},{8,0},{16,8},{24,16},{32,24},{40,32},{48,40},{56,48},{1,57}... | collective-permute-start | bytes 393224 | tf_op jit(solution)/shard_map/ppermute | solution.py:25
  112.0 3.8 %collective-permute-start.40 = (bf16[16,2048]{1,0:T(8,128)(2,1)S(1)}, bf16[16,2048]{1,0:T(8,128)(2,1)S(1)}, u32[]{:S(2)}, u32[]{:S(2)}) collective-permute-start(bf16[16,2048]{1,0:T(8,128)(2,1)S(1)} %get-tuple-element.94), channel_id=1, source_target_pairs={{0,192},{64,0},{128,64},{192,128},{1,193},{65,1},{129,65},{193,129... | collective-permute-start | bytes 196616 | tf_op jit(solution)/shard_map/ppermute | solution.py:25
  117.8 3.6 %collective-permute-done.42.three = bf16[16,2048]{1,0:T(8,128)(2,1)S(1)} collective-permute-done((bf16[16,2048]{1,0:T(8,128)(2,1)S(1)}, bf16[16,2048]{1,0:T(8,128)(2,1)S(1)}, u32[]{:S(2)}, u32[]{:S(2)}) %collective-permute-start.42) | collective-permute-done | bytes 65568 | tf_op jit(solution)/shard_map/ppermute | solution.py:25
  (103 shorter events, 46.8 us)
Async XLA Ops:
  11.9 6.9 %collective-permute-start.6 = (bf16[64,2048]{1,0:T(8,128)(2,1)S(1)}, bf16[64,2048]{1,0:T(8,128)(2,1)S(1)}, u32[]{:S(2)}, u32[]{:S(2)}) collective-permute-start(bf16[64,2048]{1,0:T(8,128)(2,1)S(1)} %shard_map.111.refs_0_), channel_id=1, source_target_pairs={{0,56},{8,0},{16,8},{24,16},{32,24},{40,32},{48,40},{56,48},{1,57}... | collective-permute-start | bytes 786440 | tf_op jit(solution)/shard_map/ppermute | solution.py:25
  12.6 10.0 %collective-permute-start.3 = (bf16[64,2048]{1,0:T(8,128)(2,1)S(1)}, bf16[64,2048]{1,0:T(8,128)(2,1)S(1)}, u32[]{:S(2)}, u32[]{:S(2)}) collective-permute-start(bf16[64,2048]{1,0:T(8,128)(2,1)S(1)} %shard_map.111.refs_0_), channel_id=1, source_target_pairs={{0,8},{8,16},{16,24},{24,32},{32,40},{40,48},{48,56},{56,0},{1,9},... | collective-permute-start | bytes 786440 | tf_op jit(solution)/shard_map/ppermute | solution.py:25
  18.9 7.2 %collective-permute-start.7 = (bf16[64,2048]{1,0:T(8,128)(2,1)S(1)}, bf16[64,2048]{1,0:T(8,128)(2,1)S(1)}, u32[]{:S(2)}, u32[]{:S(2)}) collective-permute-start(bf16[64,2048]{1,0:T(8,128)(2,1)S(1)} %collective-permute-done.6.refs_2_), channel_id=1, source_target_pairs={{0,56},{8,0},{16,8},{24,16},{32,24},{40,32},{48,40},{56,48},{1,57}... | collective-permute-start | bytes 786440 | tf_op jit(solution)/shard_map/ppermute | solution.py:25
  22.6 7.6 %collective-permute-start.4 = (bf16[64,2048]{1,0:T(8,128)(2,1)S(1)}, bf16[64,2048]{1,0:T(8,128)(2,1)S(1)}, u32[]{:S(2)}, u32[]{:S(2)}) collective-permute-start(bf16[64,2048]{1,0:T(8,128)(2,1)S(1)} %collective-permute-done.3.refs_1_), channel_id=1, source_target_pairs={{0,8},{8,16},{16,24},{24,32},{32,40},{40,48},{48,56},{56,0},{1,9},... | collective-permute-start | bytes 786440 | tf_op jit(solution)/shard_map/ppermute | solution.py:25
  26.1 9.0 %collective-permute-start.8 = (bf16[64,2048]{1,0:T(8,128)(2,1)S(1)}, bf16[64,2048]{1,0:T(8,128)(2,1)S(1)}, u32[]{:S(2)}, u32[]{:S(2)}) collective-permute-start(bf16[64,2048]{1,0:T(8,128)(2,1)S(1)} %collective-permute-done.7.refs_4_.refs_0_), channel_id=1, source_target_pairs={{0,56},{8,0},{16,8},{24,16},{32,24},{40,32},{48,40},{56,48},{1,57}... | collective-permute-start | bytes 786440 | tf_op jit(solution)/shard_map/ppermute | solution.py:25
  30.2 7.6 %collective-permute-start.5 = (bf16[64,2048]{1,0:T(8,128)(2,1)S(1)}, bf16[64,2048]{1,0:T(8,128)(2,1)S(1)}, u32[]{:S(2)}, u32[]{:S(2)}) collective-permute-start(bf16[64,2048]{1,0:T(8,128)(2,1)S(1)} %collective-permute-done.4.refs_3_), channel_id=1, source_target_pairs={{0,8},{8,16},{16,24},{24,32},{32,40},{40,48},{48,56},{56,0},{1,9},... | collective-permute-start | bytes 786440 | tf_op jit(solution)/shard_map/ppermute | solution.py:25
  37.8 9.2 %collective-permute-start.14 = (bf16[32,2048]{1,0:T(8,128)(2,1)S(1)}, bf16[32,2048]{1,0:T(8,128)(2,1)S(1)}, u32[]{:S(2)}, u32[]{:S(2)}) collective-permute-start(bf16[32,2048]{1,0:T(8,128)(2,1)S(1)} %get-tuple-element.68), channel_id=1, source_target_pairs={{0,56},{8,0},{16,8},{24,16},{32,24},{40,32},{48,40},{56,48},{1,57}... | collective-permute-start | bytes 393224 | tf_op jit(solution)/shard_map/ppermute | solution.py:25
  50.1 7.1 %collective-permute-start.15 = (bf16[128,1920]{1,0:T(8,128)(2,1)S(1)}, bf16[128,1920]{1,0:T(8,128)(2,1)S(1)}, u32[]{:S(2)}, u32[]{:S(2)}) collective-permute-start(bf16[128,1920]{1,0:T(8,128)(2,1)S(1)} %get-tuple-element.72), channel_id=1, source_target_pairs={{0,1},{1,0},{2,3},{3,2},{4,5},{5,4},{6,7},{7,6},{8,9},{9,8},{10,11... | collective-permute-start | bytes 1474568 | tf_op jit(solution)/shard_map/ppermute | solution.py:25
  51.3 8.1 %collective-permute-start.10 = (bf16[32,1920]{1,0:T(8,128)(2,1)S(1)}, bf16[32,1920]{1,0:T(8,128)(2,1)S(1)}, u32[]{:S(2)}, u32[]{:S(2)}) collective-permute-start(bf16[32,1920]{1,0:T(8,128)(2,1)S(1)} %get-tuple-element.65), channel_id=1, source_target_pairs={{0,2},{2,4},{4,6},{6,0},{1,3},{3,5},{5,7},{7,1},{8,10},{10,12},{12... | collective-permute-start | bytes 368648 | tf_op jit(solution)/shard_map/ppermute | solution.py:25
  53.0 9.7 %collective-permute-start.11 = (bf16[32,1920]{1,0:T(8,128)(2,1)S(1)}, bf16[32,1920]{1,0:T(8,128)(2,1)S(1)}, u32[]{:S(2)}, u32[]{:S(2)}) collective-permute-start(bf16[32,1920]{1,0:T(8,128)(2,1)S(1)} %get-tuple-element.66), channel_id=1, source_target_pairs={{0,4},{2,6},{4,0},{6,2},{1,5},{3,7},{5,1},{7,3},{8,12},{10,14},{12... | collective-permute-start | bytes 368648 | tf_op jit(solution)/shard_map/ppermute | solution.py:25
  57.9 7.5 %collective-permute-start.16 = (bf16[32,1920]{1,0:T(8,128)(2,1)S(1)}, bf16[32,1920]{1,0:T(8,128)(2,1)S(1)}, u32[]{:S(2)}, u32[]{:S(2)}) collective-permute-start(bf16[32,1920]{1,0:T(8,128)(2,1)S(1)} %get-tuple-element.74), channel_id=1, source_target_pairs={{0,2},{2,4},{4,6},{6,0},{1,3},{3,5},{5,7},{7,1},{8,10},{10,12},{12... | collective-permute-start | bytes 368648 | tf_op jit(solution)/shard_map/ppermute | solution.py:25
  58.6 8.4 %collective-permute-start.17 = (bf16[32,1920]{1,0:T(8,128)(2,1)S(1)}, bf16[32,1920]{1,0:T(8,128)(2,1)S(1)}, u32[]{:S(2)}, u32[]{:S(2)}) collective-permute-start(bf16[32,1920]{1,0:T(8,128)(2,1)S(1)} %get-tuple-element.75), channel_id=1, source_target_pairs={{0,4},{2,6},{4,0},{6,2},{1,5},{3,7},{5,1},{7,3},{8,12},{10,14},{12... | collective-permute-start | bytes 368648 | tf_op jit(solution)/shard_map/ppermute | solution.py:25
  59.4 7.6 %collective-permute-start.18 = (bf16[32,1920]{1,0:T(8,128)(2,1)S(1)}, bf16[32,1920]{1,0:T(8,128)(2,1)S(1)}, u32[]{:S(2)}, u32[]{:S(2)}) collective-permute-start(bf16[32,1920]{1,0:T(8,128)(2,1)S(1)} %get-tuple-element.76), channel_id=1, source_target_pairs={{0,6},{2,0},{4,2},{6,4},{1,7},{3,1},{5,3},{7,5},{8,14},{10,8},{12,... | collective-permute-start | bytes 368648 | tf_op jit(solution)/shard_map/ppermute | solution.py:25
  69.7 6.9 %collective-permute-start.20 = (bf16[64,896]{1,0:T(8,128)(2,1)S(1)}, bf16[64,896]{1,0:T(8,128)(2,1)S(1)}, u32[]{:S(2)}, u32[]{:S(2)}) collective-permute-start(bf16[64,896]{1,0:T(8,128)(2,1)S(1)} %shard_map.119.refs_0_), channel_id=1, source_target_pairs={{0,4},{2,6},{4,0},{6,2},{1,5},{3,7},{5,1},{7,3},{8,12},{10,14},{12... | collective-permute-start | bytes 344072 | tf_op jit(solution)/shard_map/ppermute | solution.py:25
  70.6 7.0 %collective-permute-start.19 = (bf16[64,896]{1,0:T(8,128)(2,1)S(1)}, bf16[64,896]{1,0:T(8,128)(2,1)S(1)}, u32[]{:S(2)}, u32[]{:S(2)}) collective-permute-start(bf16[64,896]{1,0:T(8,128)(2,1)S(1)} %shard_map.119.refs_0_), channel_id=1, source_target_pairs={{0,2},{2,4},{4,6},{6,0},{1,3},{3,5},{5,7},{7,1},{8,10},{10,12},{12... | collective-permute-start | bytes 344072 | tf_op jit(solution)/shard_map/ppermute | solution.py:25
  81.7 7.6 %collective-permute-start.26 = (bf16[32,2048]{1,0:T(8,128)(2,1)S(1)}, bf16[32,2048]{1,0:T(8,128)(2,1)S(1)}, u32[]{:S(2)}, u32[]{:S(2)}) collective-permute-start(bf16[32,2048]{1,0:T(8,128)(2,1)S(1)} %get-tuple-element.78), channel_id=1, source_target_pairs={{0,56},{8,0},{16,8},{24,16},{32,24},{40,32},{48,40},{56,48},{1,57}... | collective-permute-start | bytes 393224 | tf_op jit(solution)/shard_map/ppermute | solution.py:25
  83.8 8.8 %collective-permute-start.33 = (bf16[32,2048]{1,0:T(8,128)(2,1)S(1)}, bf16[32,2048]{1,0:T(8,128)(2,1)S(1)}, u32[]{:S(2)}, u32[]{:S(2)}) collective-permute-start(bf16[32,2048]{1,0:T(8,128)(2,1)S(1)} %get-tuple-element.87), channel_id=1, source_target_pairs={{0,8},{8,16},{16,24},{24,32},{32,40},{40,48},{48,56},{56,0},{1,9},... | collective-permute-start | bytes 393224 | tf_op jit(solution)/shard_map/ppermute | solution.py:25
  83.8 8.9 %collective-permute-start.30 = (bf16[32,2048]{1,0:T(8,128)(2,1)S(1)}, bf16[32,2048]{1,0:T(8,128)(2,1)S(1)}, u32[]{:S(2)}, u32[]{:S(2)}) collective-permute-start(bf16[32,2048]{1,0:T(8,128)(2,1)S(1)} %get-tuple-element.82), channel_id=1, source_target_pairs={{0,8},{8,16},{16,24},{24,32},{32,40},{40,48},{48,56},{56,0},{1,9},... | collective-permute-start | bytes 393224 | tf_op jit(solution)/shard_map/ppermute | solution.py:25
  83.8 9.1 %collective-permute-start.37 = (bf16[32,2048]{1,0:T(8,128)(2,1)S(1)}, bf16[32,2048]{1,0:T(8,128)(2,1)S(1)}, u32[]{:S(2)}, u32[]{:S(2)}) collective-permute-start(bf16[32,2048]{1,0:T(8,128)(2,1)S(1)} %get-tuple-element.91), channel_id=1, source_target_pairs={{0,56},{8,0},{16,8},{24,16},{32,24},{40,32},{48,40},{56,48},{1,57}... | collective-permute-start | bytes 393224 | tf_op jit(solution)/shard_map/ppermute | solution.py:25
  92.8 7.3 %collective-permute-start.31 = (bf16[32,2048]{1,0:T(8,128)(2,1)S(1)}, bf16[32,2048]{1,0:T(8,128)(2,1)S(1)}, u32[]{:S(2)}, u32[]{:S(2)}) collective-permute-start(bf16[32,2048]{1,0:T(8,128)(2,1)S(1)} %shard_map.125), channel_id=1, source_target_pairs={{0,8},{8,16},{16,24},{24,32},{32,40},{40,48},{48,56},{56,0},{1,9},... | collective-permute-start | bytes 393224 | tf_op jit(solution)/shard_map/ppermute | solution.py:25
  92.9 7.5 %collective-permute-start.38 = (bf16[32,2048]{1,0:T(8,128)(2,1)S(1)}, bf16[32,2048]{1,0:T(8,128)(2,1)S(1)}, u32[]{:S(2)}, u32[]{:S(2)}) collective-permute-start(bf16[32,2048]{1,0:T(8,128)(2,1)S(1)} %shard_map.131), channel_id=1, source_target_pairs={{0,56},{8,0},{16,8},{24,16},{32,24},{40,32},{48,40},{56,48},{1,57}... | collective-permute-start | bytes 393224 | tf_op jit(solution)/shard_map/ppermute | solution.py:25
  98.7 8.2 %collective-permute-start.35 = (bf16[32,2048]{1,0:T(8,128)(2,1)S(1)}, bf16[32,2048]{1,0:T(8,128)(2,1)S(1)}, u32[]{:S(2)}, u32[]{:S(2)}) collective-permute-start(bf16[32,2048]{1,0:T(8,128)(2,1)S(1)} %shard_map.129), channel_id=1, source_target_pairs={{0,8},{8,16},{16,24},{24,32},{32,40},{40,48},{48,56},{56,0},{1,9},... | collective-permute-start | bytes 393224 | tf_op jit(solution)/shard_map/ppermute | solution.py:25
  100.1 6.9 %collective-permute-start.32 = (bf16[32,2048]{1,0:T(8,128)(2,1)S(1)}, bf16[32,2048]{1,0:T(8,128)(2,1)S(1)}, u32[]{:S(2)}, u32[]{:S(2)}) collective-permute-start(bf16[32,2048]{1,0:T(8,128)(2,1)S(1)} %shard_map.126), channel_id=1, source_target_pairs={{0,8},{8,16},{16,24},{24,32},{32,40},{40,48},{48,56},{56,0},{1,9},... | collective-permute-start | bytes 393224 | tf_op jit(solution)/shard_map/ppermute | solution.py:25
  107.3 8.6 %collective-permute-start.41 = (bf16[16,2048]{1,0:T(8,128)(2,1)S(1)}, bf16[16,2048]{1,0:T(8,128)(2,1)S(1)}, u32[]{:S(2)}, u32[]{:S(2)}) collective-permute-start(bf16[16,2048]{1,0:T(8,128)(2,1)S(1)} %get-tuple-element.95), channel_id=1, source_target_pairs={{0,128},{64,192},{128,0},{192,64},{1,129},{65,193},{129,1},{193,65... | collective-permute-start | bytes 196616 | tf_op jit(solution)/shard_map/ppermute | solution.py:25
  (26 other events, 185.5 us)

commit v7 on v6

--- a/solution.py
+++ b/solution.py
@@ -123,9 +123,8 @@
         out[:, cols] = (got * scales[h : h + 1, :]).astype(bf16)
 
 
-def seat(own, inv_gain2, out, kept):
+def seat(own, out):
     out[pl.ds(0, own.shape[0]), :] = own[...]
-    kept[...] = inv_gain2[...]
 
 
 def join(first, *refs):
@@ -148,19 +147,23 @@
     top = part.shape[0] // 2
     step = 32
     lane = lax.broadcasted_iota(jnp.int32, (step, MARKS), 1)
-    for i in range(2 * top // step):
+
+    def some(start, out, i):
+        at = rows_at(start + i * step, step)
         sums = 0.0
         for h in range(part.shape[1] // HEAD_DIM):
-            wide = part[pl.ds(i * step, step), pl.ds(h * HEAD_DIM, HEAD_DIM)].astype(jnp.float32)
+            wide = part[at, pl.ds(h * HEAD_DIM, HEAD_DIM)].astype(jnp.float32)
             sums = sums + wide * wide * inv_gain2[pl.ds(h, 1), :]
         sums = jnp.sum(sums, axis=1, keepdims=True)
         high = sums.astype(jnp.bfloat16).astype(jnp.float32)
         marks = jnp.where(lane == 0, high, jnp.where(lane == 1, sums - high, 0.0))
-        out = keep if i * step < top else send
-        out[pl.ds(row + i * step % top, step), pl.ds(2 * width, MARKS)] = marks.astype(jnp.bfloat16)
-
-
-def project(weights, base, part, keep, send, row):
+        out[rows_at(row + i * step, step), pl.ds(2 * width, MARKS)] = marks.astype(jnp.bfloat16)
+
+    pl.loop(0, top // step)(lambda i: some(0, keep, i))
+    pl.loop(0, top // step)(lambda i: some(top, send, i))
+
+
+def project(weights, base, part, keep, send, row, wide=256):
     top, width = part.shape[0] // 2, weights.shape[1]
     to = pl.ds(row, top)
 
@@ -169,9 +172,10 @@
         keep[to, pl.ds(base + start, size)] = terms[:top].astype(jnp.bfloat16)
         send[to, pl.ds(base + start, size)] = terms[top:].astype(jnp.bfloat16)
 
-    pl.loop(0, width // 256)(lambda t: tile(pl.multiple_of(t * 256, 256), 256))
-    if width % 256:
-        tile(width // 256 * 256, width % 256)
+    if width > wide:
+        pl.loop(0, width // wide)(lambda t: tile(pl.multiple_of(t * wide, wide), wide))
+    if width % wide or width == wide:
+        tile((width - 1) // wide * wide, (width - 1) % wide + 1)
 
 
 def gate_matmul(width, idx, *refs):
@@ -201,8 +205,8 @@
     part[rows_at((1 - core) * half, half), :] = high[...]
     row = keep.shape[0] - half
     squares(width, part, inv_gain2, keep, send, row)
-    project(w_gate, 0, part, keep, send, row)
-    project(w_up, width, part, keep, send, row)
+    project(w_gate, 0, part, keep, send, row, width)
+    project(w_up, width, part, keep, send, row, width)
 
 
 def halves(up, down, _, up_half, down_half):
@@ -252,9 +256,9 @@
             hidden[rows_at(at + (1 - core) * half, half), :] = other[k][pl.ds(i * half, half), :]
     some = pl.ds((first - groups[0] * NY) * block, (last - first) * block)
 
-    @pl.loop(0, weights.shape[1] // 256)
+    @pl.loop(0, weights.shape[1] // 512)
     def _(t):
-        cols = pl.ds(pl.multiple_of(t * 256, 256), 256)
+        cols = pl.ds(pl.multiple_of(t * 512, 512), 512)
         terms = jnp.dot(hidden[some, :], weights[:, cols], preferred_element_type=jnp.float32).astype(jnp.bfloat16)
         for i, out in enumerate(outs):
             out[:, cols] = terms[i * half : (i + 1) * half]
@@ -317,9 +321,7 @@
         limit=60 * MIB,
     )
 
-    own, inv_gain2 = call(
-        seat, [shape(piece, feats), shape(per, HEAD_DIM, kind=f32)], [scaled, inv_gain2], "vv", moved=2 * rows * feats
-    )
+    own = call(seat, shape(piece, feats), [scaled], "v", moved=2 * rows * feats)
     from_x = {k: shift(scaled, "x", k, NX) for k in AWAY}
     own = call(
         join,

time: 122 us -> 121 us (level)
  starting transfers between devices: 56.3 us -> 58 us
  waiting for transfers between devices: 39 us -> 37.6 us
  Pallas kernels: 22.8 us -> 21.5 us
    ppermute x43, starting transfers between devices: 56.3 us -> 58 us  [shift(): return lax.ppermute(v, axis, [(i, (i + by) % n) for i in range(n)])]
    ppermute x43, waiting for transfers between devices: 39 us -> 37.6 us  [shift(): return lax.ppermute(v, axis, [(i, (i + by) % n) for i in range(n)])]
    pallas_call x26, Pallas kernels: 22.8 us -> 21.5 us  [call(): pl.pallas_call(kernel, out_shape=whole, in_specs=[pl.BlockSpec(memory_spa...]
    unnamed x14 -> x16, local copies, waits for them, and re-layouts: 3.63 us -> 3.63 us
  transfers between devices with their start and end apart: 43 -> 43, of which waited for: 21 -> 22; matrix products, arithmetic and copies ran while one was open for 0% -> 0% of each run, Pallas kernels for 13% -> 13%
where the time goes in v7:
time: 121 us
  starting transfers between devices  58 us (48%)
  waiting for transfers between devices  37.6 us (31%)
  Pallas kernels  21.5 us (18%)
  local copies, waits for them, and re-layouts  3.63 us (3%)
    ppermute x43, starting transfers between devices, shift(): return lax.ppermute(v, axis, [(i, (i + by) % n) for i in range(n)])  58 us
    ppermute x43, waiting for transfers between devices, shift(): return lax.ppermute(v, axis, [(i, (i + by) % n) for i in range(n)])  37.6 us
    pallas_call x26, Pallas kernels, call(): pl.pallas_call(kernel, out_shape=whole, in_specs=[pl.BlockSpec(memory_spa...  21.5 us
    unnamed x16, local copies, waits for them, and re-layouts  3.63 us
  transfers between devices with their start and end apart: 43, of which 22 were waited for; matrix products, arithmetic and copies ran while one was open for 0% of the time, Pallas kernels for 13%

profile of v7, /device:TPU:32, one launch (start us, length us, event | category | flops | bytes accessed | tf_op | source)
XLA Modules:
  0.0 121.1 jit_solution(1330099079690270084)
XLA Ops:
  0.0 2.6 %shard_map.109 = (f32[16,2048]{1,0:T(8,128)}, f32[16,128]{1,0:T(8,128)}, bf16[16,2048]{1,0:T(8,128)(2,1)}) custom-call(s32[16]{0:T(128)} %lengths_in.1, bf16[16,2048]{1,0:T(8,128)(2,1)} %hidden_in.1, bf16[16,2048]{1,0:T(8,128)(2,1)} %queries_in.1, bf16[16,128,128]{2,1,0:T(8,128)(2,1)} %keys_in.1, bf16[16,128,128]{2,1,0:T(8,128)(2,1)} %values_in.1, ...), custom_call_target="tpu_custom_call" | custom-call | bytes 1048576 | tf_op jit(solution)/shard_map/pallas_call | solution.py:36
  2.6 2.8 %collective-permute-start.2 = (bf16[16,2048]{1,0:T(8,128)(2,1)}, bf16[16,2048]{1,0:T(8,128)(2,1)S(1)}, u32[]{:S(2)}, u32[]{:S(2)}) collective-permute-start(bf16[16,2048]{1,0:T(8,128)(2,1)} %get-tuple-element.50.own), channel_id=1, source_target_pairs={{0,192},{64,0},{128,64},{192,128},{1,193},{65,1},{129,65},{193,129... | collective-permute-start | bytes 196616 | tf_op jit(solution)/shard_map/ppermute | solution.py:25
  8.6 3.3 %collective-permute-done.1.refs_1_ = bf16[16,2048]{1,0:T(8,128)(2,1)S(1)} collective-permute-done((bf16[16,2048]{1,0:T(8,128)(2,1)}, bf16[16,2048]{1,0:T(8,128)(2,1)S(1)}, u32[]{:S(2)}, u32[]{:S(2)}) %collective-permute-start.1) | collective-permute-done | bytes 65568 | tf_op jit(solution)/shard_map/ppermute | solution.py:25
  14.0 4.8 %collective-permute-done.6.refs_2_ = bf16[64,2048]{1,0:T(8,128)(2,1)S(1)} collective-permute-done((bf16[64,2048]{1,0:T(8,128)(2,1)S(1)}, bf16[64,2048]{1,0:T(8,128)(2,1)S(1)}, u32[]{:S(2)}, u32[]{:S(2)}) %collective-permute-start.6) | collective-permute-done | bytes 262176 | tf_op jit(solution)/shard_map/ppermute | solution.py:25
  18.9 3.3 %collective-permute-start.7 = (bf16[64,2048]{1,0:T(8,128)(2,1)S(1)}, bf16[64,2048]{1,0:T(8,128)(2,1)S(1)}, u32[]{:S(2)}, u32[]{:S(2)}) collective-permute-start(bf16[64,2048]{1,0:T(8,128)(2,1)S(1)} %collective-permute-done.6.refs_2_), channel_id=1, source_target_pairs={{0,56},{8,0},{16,8},{24,16},{32,24},{40,32},{48,40},{56,48},{1,57}... | collective-permute-start | bytes 786440 | tf_op jit(solution)/shard_map/ppermute | solution.py:25
  22.6 3.4 %collective-permute-done.7.refs_4_.refs_0_ = bf16[64,2048]{1,0:T(8,128)(2,1)S(1)} collective-permute-done((bf16[64,2048]{1,0:T(8,128)(2,1)S(1)}, bf16[64,2048]{1,0:T(8,128)(2,1)S(1)}, u32[]{:S(2)}, u32[]{:S(2)}) %collective-permute-start.7) | collective-permute-done | bytes 262176 | tf_op jit(solution)/shard_map/ppermute | solution.py:25
  26.1 3.7 %collective-permute-start.8 = (bf16[64,2048]{1,0:T(8,128)(2,1)S(1)}, bf16[64,2048]{1,0:T(8,128)(2,1)S(1)}, u32[]{:S(2)}, u32[]{:S(2)}) collective-permute-start(bf16[64,2048]{1,0:T(8,128)(2,1)S(1)} %collective-permute-done.7.refs_4_.refs_0_), channel_id=1, source_target_pairs={{0,56},{8,0},{16,8},{24,16},{32,24},{40,32},{48,40},{56,48},{1,57}... | collective-permute-start | bytes 786440 | tf_op jit(solution)/shard_map/ppermute | solution.py:25
  33.0 3.4 %shard_map.112 = (bf16[128,1920]{1,0:T(8,128)(2,1)S(1)}, bf16[128,1920]{1,0:T(8,128)(2,1)S(1)}, bf16[256,2048]{1,0:T(8,128)(2,1)S(1)}, f32[8,128]{1,0:T(8,128)S(1)}) custom-call(s32[4]{0:T(128)S(1)} %pad_add_fusion.idx, bf16[64,2048]{1,0:T(8,128)(2,1)S(1)} %shard_map.111.refs_0_, bf16[64,2048]{1,0:T(8,128)(2,1)S(1)} %collective-permute-done.3.refs_1_, ...), custom_call_target="tpu_custom_call" | custom-call | flops 939524096 | bytes 3670016 | tf_op jit(solution)/shard_map/pallas_call | solution.py:36
  37.8 3.3 %collective-permute-start.14 = (bf16[32,2048]{1,0:T(8,128)(2,1)S(1)}, bf16[32,2048]{1,0:T(8,128)(2,1)S(1)}, u32[]{:S(2)}, u32[]{:S(2)}) collective-permute-start(bf16[32,2048]{1,0:T(8,128)(2,1)S(1)} %get-tuple-element.64), channel_id=1, source_target_pairs={{0,56},{8,0},{16,8},{24,16},{32,24},{40,32},{48,40},{56,48},{1,57}... | collective-permute-start | bytes 393224 | tf_op jit(solution)/shard_map/ppermute | solution.py:25
  42.9 4.4 %shard_map.115 = (bf16[128,1920]{1,0:T(8,128)(2,1)S(1)}, bf16[128,1920]{1,0:T(8,128)(2,1)S(1)}, bf16[128,1920]{1,0:T(8,128)(2,1)S(1)}) custom-call(s32[4]{0:T(128)S(1)} %pad_add_fusion.idx, bf16[64,2048]{1,0:T(8,128)(2,1)S(1)} %collective-permute-done.7.refs_4_.refs_0_, ...), custom_call_target="tpu_custom_call", output_to_operand_aliasing={{2}: (4, {})} | custom-call | flops 1409286144 | bytes 7340032 | tf_op jit(solution)/shard_map/pallas_call | solution.py:36
  52.4 2.9 %collective-permute-start.11 = (bf16[32,1920]{1,0:T(8,128)(2,1)S(1)}, bf16[32,1920]{1,0:T(8,128)(2,1)S(1)}, u32[]{:S(2)}, u32[]{:S(2)}) collective-permute-start(bf16[32,1920]{1,0:T(8,128)(2,1)S(1)} %get-tuple-element.62), channel_id=1, source_target_pairs={{0,4},{2,6},{4,0},{6,2},{1,5},{3,7},{5,1},{7,3},{8,12},{10,14},{12... | collective-permute-start | bytes 368648 | tf_op jit(solution)/shard_map/ppermute | solution.py:25
  62.1 2.7 %collective-permute-done.16.refs_5_ = bf16[32,1920]{1,0:T(8,128)(2,1)S(1)} collective-permute-done((bf16[32,1920]{1,0:T(8,128)(2,1)S(1)}, bf16[32,1920]{1,0:T(8,128)(2,1)S(1)}, u32[]{:S(2)}, u32[]{:S(2)}) %collective-permute-start.16) | collective-permute-done | bytes 122912 | tf_op jit(solution)/shard_map/ppermute | solution.py:25
  66.7 2.4 %collective-permute-start.21 = (bf16[64,896]{1,0:T(8,128)(2,1)S(1)}, bf16[64,896]{1,0:T(8,128)(2,1)S(1)}, u32[]{:S(2)}, u32[]{:S(2)}) collective-permute-start(bf16[64,896]{1,0:T(8,128)(2,1)S(1)} %shard_map.119.refs_0_), channel_id=1, source_target_pairs={{0,6},{2,0},{4,2},{6,4},{1,7},{3,1},{5,3},{7,5},{8,14},{10,8},{12,... | collective-permute-start | bytes 344072 | tf_op jit(solution)/shard_map/ppermute | solution.py:25
  70.7 2.8 %collective-permute-done.21.refs_3_ = bf16[64,896]{1,0:T(8,128)(2,1)S(1)} collective-permute-done((bf16[64,896]{1,0:T(8,128)(2,1)S(1)}, bf16[64,896]{1,0:T(8,128)(2,1)S(1)}, u32[]{:S(2)}, u32[]{:S(2)}) %collective-permute-start.21) | collective-permute-done | bytes 114720 | tf_op jit(solution)/shard_map/ppermute | solution.py:25
  73.5 2.5 %collective-permute-done.20.refs_2_ = bf16[64,896]{1,0:T(8,128)(2,1)S(1)} collective-permute-done((bf16[64,896]{1,0:T(8,128)(2,1)S(1)}, bf16[64,896]{1,0:T(8,128)(2,1)S(1)}, u32[]{:S(2)}, u32[]{:S(2)}) %collective-permute-start.20) | collective-permute-done | bytes 114720 | tf_op jit(solution)/shard_map/ppermute | solution.py:25
  85.7 2.7 %shard_map.120 = (bf16[32,2048]{1,0:T(8,128)(2,1)S(1)}, bf16[32,2048]{1,0:T(8,128)(2,1)S(1)}, bf16[32,2048]{1,0:T(8,128)(2,1)S(1)}, bf16[32,2048]{1,0:T(8,128)(2...) custom-call(s32[4]{0:T(128)S(1)} %pad_add_fusion.idx, ...), custom_call_target="tpu_custom_call" | custom-call | flops 1174405120 | bytes 3670016 | tf_op jit(solution)/shard_map/pallas_call | solution.py:36
  88.4 3.3 %collective-permute-start.27 = (bf16[32,2048]{1,0:T(8,128)(2,1)S(1)}, bf16[32,2048]{1,0:T(8,128)(2,1)S(1)}, u32[]{:S(2)}, u32[]{:S(2)}) collective-permute-start(bf16[32,2048]{1,0:T(8,128)(2,1)S(1)} %shard_map.122), channel_id=1, source_target_pairs={{0,56},{8,0},{16,8},{24,16},{32,24},{40,32},{48,40},{56,48},{1,57}... | collective-permute-start | bytes 393224 | tf_op jit(solution)/shard_map/ppermute | solution.py:25
  92.2 3.0 %collective-permute-start.38 = (bf16[32,2048]{1,0:T(8,128)(2,1)S(1)}, bf16[32,2048]{1,0:T(8,128)(2,1)S(1)}, u32[]{:S(2)}, u32[]{:S(2)}) collective-permute-start(bf16[32,2048]{1,0:T(8,128)(2,1)S(1)} %shard_map.131), channel_id=1, source_target_pairs={{0,56},{8,0},{16,8},{24,16},{32,24},{40,32},{48,40},{56,48},{1,57}... | collective-permute-start | bytes 393224 | tf_op jit(solution)/shard_map/ppermute | solution.py:25
  95.3 3.3 %collective-permute-start.28 = (bf16[32,2048]{1,0:T(8,128)(2,1)S(1)}, bf16[32,2048]{1,0:T(8,128)(2,1)S(1)}, u32[]{:S(2)}, u32[]{:S(2)}) collective-permute-start(bf16[32,2048]{1,0:T(8,128)(2,1)S(1)} %shard_map.123), channel_id=1, source_target_pairs={{0,56},{8,0},{16,8},{24,16},{32,24},{40,32},{48,40},{56,48},{1,57}... | collective-permute-start | bytes 393224 | tf_op jit(solution)/shard_map/ppermute | solution.py:25
  101.1 2.5 %collective-permute-start.29 = (bf16[32,2048]{1,0:T(8,128)(2,1)S(1)}, bf16[32,2048]{1,0:T(8,128)(2,1)S(1)}, u32[]{:S(2)}, u32[]{:S(2)}) collective-permute-start(bf16[32,2048]{1,0:T(8,128)(2,1)S(1)} %shard_map.124), channel_id=1, source_target_pairs={{0,56},{8,0},{16,8},{24,16},{32,24},{40,32},{48,40},{56,48},{1,57}... | collective-permute-start | bytes 393224 | tf_op jit(solution)/shard_map/ppermute | solution.py:25
  103.6 3.1 %collective-permute-start.39 = (bf16[32,2048]{1,0:T(8,128)(2,1)S(1)}, bf16[32,2048]{1,0:T(8,128)(2,1)S(1)}, u32[]{:S(2)}, u32[]{:S(2)}) collective-permute-start(bf16[32,2048]{1,0:T(8,128)(2,1)S(1)} %shard_map.132), channel_id=1, source_target_pairs={{0,56},{8,0},{16,8},{24,16},{32,24},{40,32},{48,40},{56,48},{1,57}... | collective-permute-start | bytes 393224 | tf_op jit(solution)/shard_map/ppermute | solution.py:25
  109.2 2.6 %collective-permute-done.36.one = bf16[32,2048]{1,0:T(8,128)(2,1)S(1)} collective-permute-done((bf16[32,2048]{1,0:T(8,128)(2,1)S(1)}, bf16[32,2048]{1,0:T(8,128)(2,1)S(1)}, u32[]{:S(2)}, u32[]{:S(2)}) %collective-permute-start.36) | collective-permute-done | bytes 131104 | tf_op jit(solution)/shard_map/ppermute | solution.py:25
  111.8 3.1 %collective-permute-start.40 = (bf16[16,2048]{1,0:T(8,128)(2,1)S(1)}, bf16[16,2048]{1,0:T(8,128)(2,1)S(1)}, u32[]{:S(2)}, u32[]{:S(2)}) collective-permute-start(bf16[16,2048]{1,0:T(8,128)(2,1)S(1)} %get-tuple-element.90), channel_id=1, source_target_pairs={{0,192},{64,0},{128,64},{192,128},{1,193},{65,1},{129,65},{193,129... | collective-permute-start | bytes 196616 | tf_op jit(solution)/shard_map/ppermute | solution.py:25
  116.8 3.6 %collective-permute-done.42.three = bf16[16,2048]{1,0:T(8,128)(2,1)S(1)} collective-permute-done((bf16[16,2048]{1,0:T(8,128)(2,1)S(1)}, bf16[16,2048]{1,0:T(8,128)(2,1)S(1)}, u32[]{:S(2)}, u32[]{:S(2)}) %collective-permute-start.42) | collective-permute-done | bytes 65568 | tf_op jit(solution)/shard_map/ppermute | solution.py:25
  (105 shorter events, 45.3 us)
Async XLA Ops:
  11.9 6.9 %collective-permute-start.6 = (bf16[64,2048]{1,0:T(8,128)(2,1)S(1)}, bf16[64,2048]{1,0:T(8,128)(2,1)S(1)}, u32[]{:S(2)}, u32[]{:S(2)}) collective-permute-start(bf16[64,2048]{1,0:T(8,128)(2,1)S(1)} %shard_map.111.refs_0_), channel_id=1, source_target_pairs={{0,56},{8,0},{16,8},{24,16},{32,24},{40,32},{48,40},{56,48},{1,57}... | collective-permute-start | bytes 786440 | tf_op jit(solution)/shard_map/ppermute | solution.py:25
  12.6 10.0 %collective-permute-start.3 = (bf16[64,2048]{1,0:T(8,128)(2,1)S(1)}, bf16[64,2048]{1,0:T(8,128)(2,1)S(1)}, u32[]{:S(2)}, u32[]{:S(2)}) collective-permute-start(bf16[64,2048]{1,0:T(8,128)(2,1)S(1)} %shard_map.111.refs_0_), channel_id=1, source_target_pairs={{0,8},{8,16},{16,24},{24,32},{32,40},{40,48},{48,56},{56,0},{1,9},... | collective-permute-start | bytes 786440 | tf_op jit(solution)/shard_map/ppermute | solution.py:25
  18.9 7.2 %collective-permute-start.7 = (bf16[64,2048]{1,0:T(8,128)(2,1)S(1)}, bf16[64,2048]{1,0:T(8,128)(2,1)S(1)}, u32[]{:S(2)}, u32[]{:S(2)}) collective-permute-start(bf16[64,2048]{1,0:T(8,128)(2,1)S(1)} %collective-permute-done.6.refs_2_), channel_id=1, source_target_pairs={{0,56},{8,0},{16,8},{24,16},{32,24},{40,32},{48,40},{56,48},{1,57}... | collective-permute-start | bytes 786440 | tf_op jit(solution)/shard_map/ppermute | solution.py:25
  22.6 7.6 %collective-permute-start.4 = (bf16[64,2048]{1,0:T(8,128)(2,1)S(1)}, bf16[64,2048]{1,0:T(8,128)(2,1)S(1)}, u32[]{:S(2)}, u32[]{:S(2)}) collective-permute-start(bf16[64,2048]{1,0:T(8,128)(2,1)S(1)} %collective-permute-done.3.refs_1_), channel_id=1, source_target_pairs={{0,8},{8,16},{16,24},{24,32},{32,40},{40,48},{48,56},{56,0},{1,9},... | collective-permute-start | bytes 786440 | tf_op jit(solution)/shard_map/ppermute | solution.py:25
  26.1 10.4 %collective-permute-start.8 = (bf16[64,2048]{1,0:T(8,128)(2,1)S(1)}, bf16[64,2048]{1,0:T(8,128)(2,1)S(1)}, u32[]{:S(2)}, u32[]{:S(2)}) collective-permute-start(bf16[64,2048]{1,0:T(8,128)(2,1)S(1)} %collective-permute-done.7.refs_4_.refs_0_), channel_id=1, source_target_pairs={{0,56},{8,0},{16,8},{24,16},{32,24},{40,32},{48,40},{56,48},{1,57}... | collective-permute-start | bytes 786440 | tf_op jit(solution)/shard_map/ppermute | solution.py:25
  30.2 7.6 %collective-permute-start.5 = (bf16[64,2048]{1,0:T(8,128)(2,1)S(1)}, bf16[64,2048]{1,0:T(8,128)(2,1)S(1)}, u32[]{:S(2)}, u32[]{:S(2)}) collective-permute-start(bf16[64,2048]{1,0:T(8,128)(2,1)S(1)} %collective-permute-done.4.refs_3_), channel_id=1, source_target_pairs={{0,8},{8,16},{16,24},{24,32},{32,40},{40,48},{48,56},{56,0},{1,9},... | collective-permute-start | bytes 786440 | tf_op jit(solution)/shard_map/ppermute | solution.py:25
  37.8 9.7 %collective-permute-start.14 = (bf16[32,2048]{1,0:T(8,128)(2,1)S(1)}, bf16[32,2048]{1,0:T(8,128)(2,1)S(1)}, u32[]{:S(2)}, u32[]{:S(2)}) collective-permute-start(bf16[32,2048]{1,0:T(8,128)(2,1)S(1)} %get-tuple-element.64), channel_id=1, source_target_pairs={{0,56},{8,0},{16,8},{24,16},{32,24},{40,32},{48,40},{56,48},{1,57}... | collective-permute-start | bytes 393224 | tf_op jit(solution)/shard_map/ppermute | solution.py:25
  49.5 7.1 %collective-permute-start.15 = (bf16[128,1920]{1,0:T(8,128)(2,1)S(1)}, bf16[128,1920]{1,0:T(8,128)(2,1)S(1)}, u32[]{:S(2)}, u32[]{:S(2)}) collective-permute-start(bf16[128,1920]{1,0:T(8,128)(2,1)S(1)} %get-tuple-element.68), channel_id=1, source_target_pairs={{0,1},{1,0},{2,3},{3,2},{4,5},{5,4},{6,7},{7,6},{8,9},{9,8},{10,11... | collective-permute-start | bytes 1474568 | tf_op jit(solution)/shard_map/ppermute | solution.py:25
  50.7 8.1 %collective-permute-start.10 = (bf16[32,1920]{1,0:T(8,128)(2,1)S(1)}, bf16[32,1920]{1,0:T(8,128)(2,1)S(1)}, u32[]{:S(2)}, u32[]{:S(2)}) collective-permute-start(bf16[32,1920]{1,0:T(8,128)(2,1)S(1)} %get-tuple-element.61), channel_id=1, source_target_pairs={{0,2},{2,4},{4,6},{6,0},{1,3},{3,5},{5,7},{7,1},{8,10},{10,12},{12... | collective-permute-start | bytes 368648 | tf_op jit(solution)/shard_map/ppermute | solution.py:25
  52.4 9.7 %collective-permute-start.11 = (bf16[32,1920]{1,0:T(8,128)(2,1)S(1)}, bf16[32,1920]{1,0:T(8,128)(2,1)S(1)}, u32[]{:S(2)}, u32[]{:S(2)}) collective-permute-start(bf16[32,1920]{1,0:T(8,128)(2,1)S(1)} %get-tuple-element.62), channel_id=1, source_target_pairs={{0,4},{2,6},{4,0},{6,2},{1,5},{3,7},{5,1},{7,3},{8,12},{10,14},{12... | collective-permute-start | bytes 368648 | tf_op jit(solution)/shard_map/ppermute | solution.py:25
  57.3 7.5 %collective-permute-start.16 = (bf16[32,1920]{1,0:T(8,128)(2,1)S(1)}, bf16[32,1920]{1,0:T(8,128)(2,1)S(1)}, u32[]{:S(2)}, u32[]{:S(2)}) collective-permute-start(bf16[32,1920]{1,0:T(8,128)(2,1)S(1)} %get-tuple-element.70), channel_id=1, source_target_pairs={{0,2},{2,4},{4,6},{6,0},{1,3},{3,5},{5,7},{7,1},{8,10},{10,12},{12... | collective-permute-start | bytes 368648 | tf_op jit(solution)/shard_map/ppermute | solution.py:25
  58.1 8.4 %collective-permute-start.17 = (bf16[32,1920]{1,0:T(8,128)(2,1)S(1)}, bf16[32,1920]{1,0:T(8,128)(2,1)S(1)}, u32[]{:S(2)}, u32[]{:S(2)}) collective-permute-start(bf16[32,1920]{1,0:T(8,128)(2,1)S(1)} %get-tuple-element.71), channel_id=1, source_target_pairs={{0,4},{2,6},{4,0},{6,2},{1,5},{3,7},{5,1},{7,3},{8,12},{10,14},{12... | collective-permute-start | bytes 368648 | tf_op jit(solution)/shard_map/ppermute | solution.py:25
  58.9 7.6 %collective-permute-start.18 = (bf16[32,1920]{1,0:T(8,128)(2,1)S(1)}, bf16[32,1920]{1,0:T(8,128)(2,1)S(1)}, u32[]{:S(2)}, u32[]{:S(2)}) collective-permute-start(bf16[32,1920]{1,0:T(8,128)(2,1)S(1)} %get-tuple-element.72), channel_id=1, source_target_pairs={{0,6},{2,0},{4,2},{6,4},{1,7},{3,1},{5,3},{7,5},{8,14},{10,8},{12,... | collective-permute-start | bytes 368648 | tf_op jit(solution)/shard_map/ppermute | solution.py:25
  69.1 6.9 %collective-permute-start.20 = (bf16[64,896]{1,0:T(8,128)(2,1)S(1)}, bf16[64,896]{1,0:T(8,128)(2,1)S(1)}, u32[]{:S(2)}, u32[]{:S(2)}) collective-permute-start(bf16[64,896]{1,0:T(8,128)(2,1)S(1)} %shard_map.119.refs_0_), channel_id=1, source_target_pairs={{0,4},{2,6},{4,0},{6,2},{1,5},{3,7},{5,1},{7,3},{8,12},{10,14},{12... | collective-permute-start | bytes 344072 | tf_op jit(solution)/shard_map/ppermute | solution.py:25
  70.0 7.0 %collective-permute-start.19 = (bf16[64,896]{1,0:T(8,128)(2,1)S(1)}, bf16[64,896]{1,0:T(8,128)(2,1)S(1)}, u32[]{:S(2)}, u32[]{:S(2)}) collective-permute-start(bf16[64,896]{1,0:T(8,128)(2,1)S(1)} %shard_map.119.refs_0_), channel_id=1, source_target_pairs={{0,2},{2,4},{4,6},{6,0},{1,3},{3,5},{5,7},{7,1},{8,10},{10,12},{12... | collective-permute-start | bytes 344072 | tf_op jit(solution)/shard_map/ppermute | solution.py:25
  80.5 7.9 %collective-permute-start.26 = (bf16[32,2048]{1,0:T(8,128)(2,1)S(1)}, bf16[32,2048]{1,0:T(8,128)(2,1)S(1)}, u32[]{:S(2)}, u32[]{:S(2)}) collective-permute-start(bf16[32,2048]{1,0:T(8,128)(2,1)S(1)} %get-tuple-element.74), channel_id=1, source_target_pairs={{0,56},{8,0},{16,8},{24,16},{32,24},{40,32},{48,40},{56,48},{1,57}... | collective-permute-start | bytes 393224 | tf_op jit(solution)/shard_map/ppermute | solution.py:25
  82.6 9.2 %collective-permute-start.33 = (bf16[32,2048]{1,0:T(8,128)(2,1)S(1)}, bf16[32,2048]{1,0:T(8,128)(2,1)S(1)}, u32[]{:S(2)}, u32[]{:S(2)}) collective-permute-start(bf16[32,2048]{1,0:T(8,128)(2,1)S(1)} %get-tuple-element.83), channel_id=1, source_target_pairs={{0,8},{8,16},{16,24},{24,32},{32,40},{40,48},{48,56},{56,0},{1,9},... | collective-permute-start | bytes 393224 | tf_op jit(solution)/shard_map/ppermute | solution.py:25
  82.6 9.4 %collective-permute-start.30 = (bf16[32,2048]{1,0:T(8,128)(2,1)S(1)}, bf16[32,2048]{1,0:T(8,128)(2,1)S(1)}, u32[]{:S(2)}, u32[]{:S(2)}) collective-permute-start(bf16[32,2048]{1,0:T(8,128)(2,1)S(1)} %get-tuple-element.78), channel_id=1, source_target_pairs={{0,8},{8,16},{16,24},{24,32},{32,40},{40,48},{48,56},{56,0},{1,9},... | collective-permute-start | bytes 393224 | tf_op jit(solution)/shard_map/ppermute | solution.py:25
  83.8 8.3 %collective-permute-start.37 = (bf16[32,2048]{1,0:T(8,128)(2,1)S(1)}, bf16[32,2048]{1,0:T(8,128)(2,1)S(1)}, u32[]{:S(2)}, u32[]{:S(2)}) collective-permute-start(bf16[32,2048]{1,0:T(8,128)(2,1)S(1)} %get-tuple-element.87), channel_id=1, source_target_pairs={{0,56},{8,0},{16,8},{24,16},{32,24},{40,32},{48,40},{56,48},{1,57}... | collective-permute-start | bytes 393224 | tf_op jit(solution)/shard_map/ppermute | solution.py:25
  92.0 7.1 %collective-permute-start.31 = (bf16[32,2048]{1,0:T(8,128)(2,1)S(1)}, bf16[32,2048]{1,0:T(8,128)(2,1)S(1)}, u32[]{:S(2)}, u32[]{:S(2)}) collective-permute-start(bf16[32,2048]{1,0:T(8,128)(2,1)S(1)} %shard_map.125), channel_id=1, source_target_pairs={{0,8},{8,16},{16,24},{24,32},{32,40},{40,48},{48,56},{56,0},{1,9},... | collective-permute-start | bytes 393224 | tf_op jit(solution)/shard_map/ppermute | solution.py:25
  92.2 7.4 %collective-permute-start.38 = (bf16[32,2048]{1,0:T(8,128)(2,1)S(1)}, bf16[32,2048]{1,0:T(8,128)(2,1)S(1)}, u32[]{:S(2)}, u32[]{:S(2)}) collective-permute-start(bf16[32,2048]{1,0:T(8,128)(2,1)S(1)} %shard_map.131), channel_id=1, source_target_pairs={{0,56},{8,0},{16,8},{24,16},{32,24},{40,32},{48,40},{56,48},{1,57}... | collective-permute-start | bytes 393224 | tf_op jit(solution)/shard_map/ppermute | solution.py:25
  98.6 8.1 %collective-permute-start.35 = (bf16[32,2048]{1,0:T(8,128)(2,1)S(1)}, bf16[32,2048]{1,0:T(8,128)(2,1)S(1)}, u32[]{:S(2)}, u32[]{:S(2)}) collective-permute-start(bf16[32,2048]{1,0:T(8,128)(2,1)S(1)} %shard_map.129), channel_id=1, source_target_pairs={{0,8},{8,16},{16,24},{24,32},{32,40},{40,48},{48,56},{56,0},{1,9},... | collective-permute-start | bytes 393224 | tf_op jit(solution)/shard_map/ppermute | solution.py:25
  99.2 7.6 %collective-permute-start.32 = (bf16[32,2048]{1,0:T(8,128)(2,1)S(1)}, bf16[32,2048]{1,0:T(8,128)(2,1)S(1)}, u32[]{:S(2)}, u32[]{:S(2)}) collective-permute-start(bf16[32,2048]{1,0:T(8,128)(2,1)S(1)} %shard_map.126), channel_id=1, source_target_pairs={{0,8},{8,16},{16,24},{24,32},{32,40},{40,48},{48,56},{56,0},{1,9},... | collective-permute-start | bytes 393224 | tf_op jit(solution)/shard_map/ppermute | solution.py:25
  107.2 7.8 %collective-permute-start.41 = (bf16[16,2048]{1,0:T(8,128)(2,1)S(1)}, bf16[16,2048]{1,0:T(8,128)(2,1)S(1)}, u32[]{:S(2)}, u32[]{:S(2)}) collective-permute-start(bf16[16,2048]{1,0:T(8,128)(2,1)S(1)} %get-tuple-element.91), channel_id=1, source_target_pairs={{0,128},{64,192},{128,0},{192,64},{1,129},{65,193},{129,1},{193,65... | collective-permute-start | bytes 196616 | tf_op jit(solution)/shard_map/ppermute | solution.py:25
  (27 other events, 188.1 us)

commit v8 on v7

--- a/solution.py
+++ b/solution.py
@@ -18,7 +18,6 @@
 EARLY = 4
 FAR = 5
 AWAY = (2, 1, 3)
-SLOTS = (0, 2, 1, 3)
 
 
 def shift(v, axis, by, n):
@@ -145,11 +144,11 @@
 
 def squares(width, part, inv_gain2, keep, send, row):
     top = part.shape[0] // 2
-    step = 32
+    step = next(n for n in (64, 48, 32) if top % n == 0)
     lane = lax.broadcasted_iota(jnp.int32, (step, MARKS), 1)
 
     def some(start, out, i):
-        at = rows_at(start + i * step, step)
+        at = pl.ds(pl.multiple_of(start + i * step, 16), step)
         sums = 0.0
         for h in range(part.shape[1] // HEAD_DIM):
             wide = part[at, pl.ds(h * HEAD_DIM, HEAD_DIM)].astype(jnp.float32)
@@ -157,7 +156,7 @@
         sums = jnp.sum(sums, axis=1, keepdims=True)
         high = sums.astype(jnp.bfloat16).astype(jnp.float32)
         marks = jnp.where(lane == 0, high, jnp.where(lane == 1, sums - high, 0.0))
-        out[rows_at(row + i * step, step), pl.ds(2 * width, MARKS)] = marks.astype(jnp.bfloat16)
+        out[pl.ds(pl.multiple_of(row + i * step, 16), step), pl.ds(2 * width, MARKS)] = marks.astype(jnp.bfloat16)
 
     pl.loop(0, top // step)(lambda i: some(0, keep, i))
     pl.loop(0, top // step)(lambda i: some(top, send, i))
@@ -326,7 +325,7 @@
     own = call(
         join,
         shape(piece, feats),
-        [own] + [from_x[k] for k in SLOTS[1:]],
+        [own] + [from_x[k] for k in range(1, NX)],
         "v" * NX,
         moved=4 * piece * feats,
         alias={0: 0},
@@ -433,10 +432,10 @@
     far = NZ // 2
     low = [chain(0, -1, far), chain(0, 1, far - 1)]
     high = [chain(1, 1, far), chain(1, -1, far - 1)]
-    mine, two = call(
+    mine, one = call(
         z_sum, [shape(rows, feats, kind=f32), shape(rows, feats)], [terms[0][0]] + low, "vvv", moved=4 * piece * feats
     )
-    one, three = call(z_sum, [shape(rows, feats)] * 2, [terms[0][1]] + high, "vvv", moved=4 * piece * feats)
+    two, three = call(z_sum, [shape(rows, feats)] * 2, [terms[0][1]] + high, "vvv", moved=4 * piece * feats)
     sent = {1: one, 2: two, 3: three}
     parts = {k: shift(sent[k], "x", -k, NX) for k in AWAY}
     return call(finish, shape(rows, feats), [stream, mine] + [parts[k] for k in range(1, NX)], "v" * 5, moved=20 * rows * feats)

time: 121 us -> 120 us (level)
  starting transfers between devices: 58 us -> 54.7 us
  waiting for transfers between devices: 37.6 us -> 39.9 us
    ppermute x43, starting transfers between devices: 58 us -> 54.7 us  [shift(): return lax.ppermute(v, axis, [(i, (i + by) % n) for i in range(n)])]
    ppermute x43, waiting for transfers between devices: 37.6 us -> 39.9 us  [shift(): return lax.ppermute(v, axis, [(i, (i + by) % n) for i in range(n)])]
  transfers between devices with their start and end apart: 43 -> 43, of which waited for: 22 -> 23; matrix products, arithmetic and copies ran while one was open for 0% -> 0% of each run, Pallas kernels for 13% -> 13%
where the time goes in v8:
time: 120 us; the launch traced here: 119 us
  starting transfers between devices  54.7 us (46%)
  waiting for transfers between devices  39.9 us (33%)
  Pallas kernels  21 us (18%)
  local copies, waits for them, and re-layouts  3.63 us (3%)
    ppermute x43, starting transfers between devices, shift(): return lax.ppermute(v, axis, [(i, (i + by) % n) for i in range(n)])  54.7 us
    ppermute x43, waiting for transfers between devices, shift(): return lax.ppermute(v, axis, [(i, (i + by) % n) for i in range(n)])  39.9 us
    pallas_call x26, Pallas kernels, call(): pl.pallas_call(kernel, out_shape=whole, in_specs=[pl.BlockSpec(memory_spa...  21 us
    unnamed x16, local copies, waits for them, and re-layouts  3.63 us
  transfers between devices with their start and end apart: 43, of which 23 were waited for; matrix products, arithmetic and copies ran while one was open for 0% of the time, Pallas kernels for 13%

profile of v8, /device:TPU:32, one launch (start us, length us, event | category | flops | bytes accessed | tf_op | source)
XLA Modules:
  0.0 119.5 jit_solution(8312401755557684475)
XLA Ops:
  0.0 2.6 %shard_map.109 = (f32[16,2048]{1,0:T(8,128)}, f32[16,128]{1,0:T(8,128)}, bf16[16,2048]{1,0:T(8,128)(2,1)}) custom-call(s32[16]{0:T(128)} %lengths_in.1, bf16[16,2048]{1,0:T(8,128)(2,1)} %hidden_in.1, bf16[16,2048]{1,0:T(8,128)(2,1)} %queries_in.1, bf16[16,128,128]{2,1,0:T(8,128)(2,1)} %keys_in.1, bf16[16,128,128]{2,1,0:T(8,128)(2,1)} %values_in.1, ...), custom_call_target="tpu_custom_call" | custom-call | bytes 1048576 | tf_op jit(solution)/shard_map/pallas_call | solution.py:35
  2.6 2.8 %collective-permute-start.2 = (bf16[16,2048]{1,0:T(8,128)(2,1)}, bf16[16,2048]{1,0:T(8,128)(2,1)S(1)}, u32[]{:S(2)}, u32[]{:S(2)}) collective-permute-start(bf16[16,2048]{1,0:T(8,128)(2,1)} %get-tuple-element.50.own), channel_id=1, source_target_pairs={{0,192},{64,0},{128,64},{192,128},{1,193},{65,1},{129,65},{193,129... | collective-permute-start | bytes 196616 | tf_op jit(solution)/shard_map/ppermute | solution.py:24
  8.0 3.4 %collective-permute-done.1.refs_1_ = bf16[16,2048]{1,0:T(8,128)(2,1)S(1)} collective-permute-done((bf16[16,2048]{1,0:T(8,128)(2,1)}, bf16[16,2048]{1,0:T(8,128)(2,1)S(1)}, u32[]{:S(2)}, u32[]{:S(2)}) %collective-permute-start.1) | collective-permute-done | bytes 65568 | tf_op jit(solution)/shard_map/ppermute | solution.py:24
  14.3 4.8 %collective-permute-done.6.refs_2_ = bf16[64,2048]{1,0:T(8,128)(2,1)S(1)} collective-permute-done((bf16[64,2048]{1,0:T(8,128)(2,1)S(1)}, bf16[64,2048]{1,0:T(8,128)(2,1)S(1)}, u32[]{:S(2)}, u32[]{:S(2)}) %collective-permute-start.6) | collective-permute-done | bytes 262176 | tf_op jit(solution)/shard_map/ppermute | solution.py:24
  19.0 3.3 %collective-permute-start.7 = (bf16[64,2048]{1,0:T(8,128)(2,1)S(1)}, bf16[64,2048]{1,0:T(8,128)(2,1)S(1)}, u32[]{:S(2)}, u32[]{:S(2)}) collective-permute-start(bf16[64,2048]{1,0:T(8,128)(2,1)S(1)} %collective-permute-done.6.refs_2_), channel_id=1, source_target_pairs={{0,56},{8,0},{16,8},{24,16},{32,24},{40,32},{48,40},{56,48},{1,57}... | collective-permute-start | bytes 786440 | tf_op jit(solution)/shard_map/ppermute | solution.py:24
  22.8 3.4 %collective-permute-done.7.refs_4_.refs_0_ = bf16[64,2048]{1,0:T(8,128)(2,1)S(1)} collective-permute-done((bf16[64,2048]{1,0:T(8,128)(2,1)S(1)}, bf16[64,2048]{1,0:T(8,128)(2,1)S(1)}, u32[]{:S(2)}, u32[]{:S(2)}) %collective-permute-start.7) | collective-permute-done | bytes 262176 | tf_op jit(solution)/shard_map/ppermute | solution.py:24
  26.2 3.7 %collective-permute-start.8 = (bf16[64,2048]{1,0:T(8,128)(2,1)S(1)}, bf16[64,2048]{1,0:T(8,128)(2,1)S(1)}, u32[]{:S(2)}, u32[]{:S(2)}) collective-permute-start(bf16[64,2048]{1,0:T(8,128)(2,1)S(1)} %collective-permute-done.7.refs_4_.refs_0_), channel_id=1, source_target_pairs={{0,56},{8,0},{16,8},{24,16},{32,24},{40,32},{48,40},{56,48},{1,57}... | collective-permute-start | bytes 786440 | tf_op jit(solution)/shard_map/ppermute | solution.py:24
  33.2 3.0 %shard_map.112 = (bf16[128,1920]{1,0:T(8,128)(2,1)S(1)}, bf16[128,1920]{1,0:T(8,128)(2,1)S(1)}, bf16[256,2048]{1,0:T(8,128)(2,1)S(1)}, f32[8,128]{1,0:T(8,128)S(1)}) custom-call(s32[4]{0:T(128)S(1)} %pad_add_fusion.idx, bf16[64,2048]{1,0:T(8,128)(2,1)S(1)} %shard_map.111.refs_0_, bf16[64,2048]{1,0:T(8,128)(2,1)S(1)} %collective-permute-done.3.refs_1_, ...), custom_call_target="tpu_custom_call" | custom-call | flops 939524096 | bytes 3670016 | tf_op jit(solution)/shard_map/pallas_call | solution.py:35
  38.1 3.3 %collective-permute-start.14 = (bf16[32,2048]{1,0:T(8,128)(2,1)S(1)}, bf16[32,2048]{1,0:T(8,128)(2,1)S(1)}, u32[]{:S(2)}, u32[]{:S(2)}) collective-permute-start(bf16[32,2048]{1,0:T(8,128)(2,1)S(1)} %get-tuple-element.64), channel_id=1, source_target_pairs={{0,56},{8,0},{16,8},{24,16},{32,24},{40,32},{48,40},{56,48},{1,57}... | collective-permute-start | bytes 393224 | tf_op jit(solution)/shard_map/ppermute | solution.py:24
  43.2 4.2 %shard_map.115 = (bf16[128,1920]{1,0:T(8,128)(2,1)S(1)}, bf16[128,1920]{1,0:T(8,128)(2,1)S(1)}, bf16[128,1920]{1,0:T(8,128)(2,1)S(1)}) custom-call(s32[4]{0:T(128)S(1)} %pad_add_fusion.idx, bf16[64,2048]{1,0:T(8,128)(2,1)S(1)} %collective-permute-done.7.refs_4_.refs_0_, ...), custom_call_target="tpu_custom_call", output_to_operand_aliasing={{2}: (4, {})} | custom-call | flops 1409286144 | bytes 7340032 | tf_op jit(solution)/shard_map/pallas_call | solution.py:35
  52.5 2.9 %collective-permute-start.11 = (bf16[32,1920]{1,0:T(8,128)(2,1)S(1)}, bf16[32,1920]{1,0:T(8,128)(2,1)S(1)}, u32[]{:S(2)}, u32[]{:S(2)}) collective-permute-start(bf16[32,1920]{1,0:T(8,128)(2,1)S(1)} %get-tuple-element.62), channel_id=1, source_target_pairs={{0,4},{2,6},{4,0},{6,2},{1,5},{3,7},{5,1},{7,3},{8,12},{10,14},{12... | collective-permute-start | bytes 368648 | tf_op jit(solution)/shard_map/ppermute | solution.py:24
  62.1 2.7 %collective-permute-done.16.refs_5_ = bf16[32,1920]{1,0:T(8,128)(2,1)S(1)} collective-permute-done((bf16[32,1920]{1,0:T(8,128)(2,1)S(1)}, bf16[32,1920]{1,0:T(8,128)(2,1)S(1)}, u32[]{:S(2)}, u32[]{:S(2)}) %collective-permute-start.16) | collective-permute-done | bytes 122912 | tf_op jit(solution)/shard_map/ppermute | solution.py:24
  66.8 2.4 %collective-permute-start.21 = (bf16[64,896]{1,0:T(8,128)(2,1)S(1)}, bf16[64,896]{1,0:T(8,128)(2,1)S(1)}, u32[]{:S(2)}, u32[]{:S(2)}) collective-permute-start(bf16[64,896]{1,0:T(8,128)(2,1)S(1)} %shard_map.119.refs_0_), channel_id=1, source_target_pairs={{0,6},{2,0},{4,2},{6,4},{1,7},{3,1},{5,3},{7,5},{8,14},{10,8},{12,... | collective-permute-start | bytes 344072 | tf_op jit(solution)/shard_map/ppermute | solution.py:24
  70.8 2.8 %collective-permute-done.21.refs_3_ = bf16[64,896]{1,0:T(8,128)(2,1)S(1)} collective-permute-done((bf16[64,896]{1,0:T(8,128)(2,1)S(1)}, bf16[64,896]{1,0:T(8,128)(2,1)S(1)}, u32[]{:S(2)}, u32[]{:S(2)}) %collective-permute-start.21) | collective-permute-done | bytes 114720 | tf_op jit(solution)/shard_map/ppermute | solution.py:24
  73.6 2.5 %collective-permute-done.20.refs_2_ = bf16[64,896]{1,0:T(8,128)(2,1)S(1)} collective-permute-done((bf16[64,896]{1,0:T(8,128)(2,1)S(1)}, bf16[64,896]{1,0:T(8,128)(2,1)S(1)}, u32[]{:S(2)}, u32[]{:S(2)}) %collective-permute-start.20) | collective-permute-done | bytes 114720 | tf_op jit(solution)/shard_map/ppermute | solution.py:24
  78.4 2.1 %shard_map.121 = (bf16[32,2048]{1,0:T(8,128)(2,1)S(1)}, bf16[32,2048]{1,0:T(8,128)(2,1)S(1)}, bf16[32,2048]{1,0:T(8,128)(2,1)S(1)}, bf16[32,2048]{1,0:T(8,128)(2...) custom-call(s32[4]{0:T(128)S(1)} %pad_add_fusion.idx, bf16[64,896]{1,0:T(8,128)(2,1)S(1)} %shard_map.119.refs_0_, ...), custom_call_target="tpu_custom_call" | custom-call | flops 704643072 | bytes 3670016 | tf_op jit(solution)/shard_map/pallas_call | solution.py:35
  85.4 2.7 %shard_map.120 = (bf16[32,2048]{1,0:T(8,128)(2,1)S(1)}, bf16[32,2048]{1,0:T(8,128)(2,1)S(1)}, bf16[32,2048]{1,0:T(8,128)(2,1)S(1)}, bf16[32,2048]{1,0:T(8,128)(2...) custom-call(s32[4]{0:T(128)S(1)} %pad_add_fusion.idx, ...), custom_call_target="tpu_custom_call" | custom-call | flops 1174405120 | bytes 3670016 | tf_op jit(solution)/shard_map/pallas_call | solution.py:35
  88.1 3.3 %collective-permute-start.27 = (bf16[32,2048]{1,0:T(8,128)(2,1)S(1)}, bf16[32,2048]{1,0:T(8,128)(2,1)S(1)}, u32[]{:S(2)}, u32[]{:S(2)}) collective-permute-start(bf16[32,2048]{1,0:T(8,128)(2,1)S(1)} %shard_map.122), channel_id=1, source_target_pairs={{0,56},{8,0},{16,8},{24,16},{32,24},{40,32},{48,40},{56,48},{1,57}... | collective-permute-start | bytes 393224 | tf_op jit(solution)/shard_map/ppermute | solution.py:24
  91.9 3.0 %collective-permute-start.39 = (bf16[32,2048]{1,0:T(8,128)(2,1)S(1)}, bf16[32,2048]{1,0:T(8,128)(2,1)S(1)}, u32[]{:S(2)}, u32[]{:S(2)}) collective-permute-start(bf16[32,2048]{1,0:T(8,128)(2,1)S(1)} %shard_map.131), channel_id=1, source_target_pairs={{0,56},{8,0},{16,8},{24,16},{32,24},{40,32},{48,40},{56,48},{1,57}... | collective-permute-start | bytes 393224 | tf_op jit(solution)/shard_map/ppermute | solution.py:24
  95.0 3.3 %collective-permute-start.28 = (bf16[32,2048]{1,0:T(8,128)(2,1)S(1)}, bf16[32,2048]{1,0:T(8,128)(2,1)S(1)}, u32[]{:S(2)}, u32[]{:S(2)}) collective-permute-start(bf16[32,2048]{1,0:T(8,128)(2,1)S(1)} %shard_map.123), channel_id=1, source_target_pairs={{0,56},{8,0},{16,8},{24,16},{32,24},{40,32},{48,40},{56,48},{1,57}... | collective-permute-start | bytes 393224 | tf_op jit(solution)/shard_map/ppermute | solution.py:24
  100.8 2.5 %collective-permute-start.29 = (bf16[32,2048]{1,0:T(8,128)(2,1)S(1)}, bf16[32,2048]{1,0:T(8,128)(2,1)S(1)}, u32[]{:S(2)}, u32[]{:S(2)}) collective-permute-start(bf16[32,2048]{1,0:T(8,128)(2,1)S(1)} %shard_map.124), channel_id=1, source_target_pairs={{0,56},{8,0},{16,8},{24,16},{32,24},{40,32},{48,40},{56,48},{1,57}... | collective-permute-start | bytes 393224 | tf_op jit(solution)/shard_map/ppermute | solution.py:24
  103.3 3.1 %collective-permute-start.40 = (bf16[32,2048]{1,0:T(8,128)(2,1)S(1)}, bf16[32,2048]{1,0:T(8,128)(2,1)S(1)}, u32[]{:S(2)}, u32[]{:S(2)}) collective-permute-start(bf16[32,2048]{1,0:T(8,128)(2,1)S(1)} %shard_map.132), channel_id=1, source_target_pairs={{0,56},{8,0},{16,8},{24,16},{32,24},{40,32},{48,40},{56,48},{1,57}... | collective-permute-start | bytes 393224 | tf_op jit(solution)/shard_map/ppermute | solution.py:24
  108.9 2.6 %collective-permute-done.37.one = bf16[32,2048]{1,0:T(8,128)(2,1)S(1)} collective-permute-done((bf16[32,2048]{1,0:T(8,128)(2,1)S(1)}, bf16[32,2048]{1,0:T(8,128)(2,1)S(1)}, u32[]{:S(2)}, u32[]{:S(2)}) %collective-permute-start.37) | collective-permute-done | bytes 131104 | tf_op jit(solution)/shard_map/ppermute | solution.py:24
  113.3 4.0 %collective-permute-done.41.two = bf16[16,2048]{1,0:T(8,128)(2,1)S(1)} collective-permute-done((bf16[16,2048]{1,0:T(8,128)(2,1)S(1)}, bf16[16,2048]{1,0:T(8,128)(2,1)S(1)}, u32[]{:S(2)}, u32[]{:S(2)}) %collective-permute-start.41) | collective-permute-done | bytes 65568 | tf_op jit(solution)/shard_map/ppermute | solution.py:24
  (105 shorter events, 44.6 us)
Async XLA Ops:
  12.2 6.9 %collective-permute-start.6 = (bf16[64,2048]{1,0:T(8,128)(2,1)S(1)}, bf16[64,2048]{1,0:T(8,128)(2,1)S(1)}, u32[]{:S(2)}, u32[]{:S(2)}) collective-permute-start(bf16[64,2048]{1,0:T(8,128)(2,1)S(1)} %shard_map.111.refs_0_), channel_id=1, source_target_pairs={{0,56},{8,0},{16,8},{24,16},{32,24},{40,32},{48,40},{56,48},{1,57}... | collective-permute-start | bytes 786440 | tf_op jit(solution)/shard_map/ppermute | solution.py:24
  12.3 10.4 %collective-permute-start.3 = (bf16[64,2048]{1,0:T(8,128)(2,1)S(1)}, bf16[64,2048]{1,0:T(8,128)(2,1)S(1)}, u32[]{:S(2)}, u32[]{:S(2)}) collective-permute-start(bf16[64,2048]{1,0:T(8,128)(2,1)S(1)} %shard_map.111.refs_0_), channel_id=1, source_target_pairs={{0,8},{8,16},{16,24},{24,32},{32,40},{40,48},{48,56},{56,0},{1,9},... | collective-permute-start | bytes 786440 | tf_op jit(solution)/shard_map/ppermute | solution.py:24
  19.0 7.2 %collective-permute-start.7 = (bf16[64,2048]{1,0:T(8,128)(2,1)S(1)}, bf16[64,2048]{1,0:T(8,128)(2,1)S(1)}, u32[]{:S(2)}, u32[]{:S(2)}) collective-permute-start(bf16[64,2048]{1,0:T(8,128)(2,1)S(1)} %collective-permute-done.6.refs_2_), channel_id=1, source_target_pairs={{0,56},{8,0},{16,8},{24,16},{32,24},{40,32},{48,40},{56,48},{1,57}... | collective-permute-start | bytes 786440 | tf_op jit(solution)/shard_map/ppermute | solution.py:24
  22.8 7.6 %collective-permute-start.4 = (bf16[64,2048]{1,0:T(8,128)(2,1)S(1)}, bf16[64,2048]{1,0:T(8,128)(2,1)S(1)}, u32[]{:S(2)}, u32[]{:S(2)}) collective-permute-start(bf16[64,2048]{1,0:T(8,128)(2,1)S(1)} %collective-permute-done.3.refs_1_), channel_id=1, source_target_pairs={{0,8},{8,16},{16,24},{24,32},{32,40},{40,48},{48,56},{56,0},{1,9},... | collective-permute-start | bytes 786440 | tf_op jit(solution)/shard_map/ppermute | solution.py:24
  26.2 10.0 %collective-permute-start.8 = (bf16[64,2048]{1,0:T(8,128)(2,1)S(1)}, bf16[64,2048]{1,0:T(8,128)(2,1)S(1)}, u32[]{:S(2)}, u32[]{:S(2)}) collective-permute-start(bf16[64,2048]{1,0:T(8,128)(2,1)S(1)} %collective-permute-done.7.refs_4_.refs_0_), channel_id=1, source_target_pairs={{0,56},{8,0},{16,8},{24,16},{32,24},{40,32},{48,40},{56,48},{1,57}... | collective-permute-start | bytes 786440 | tf_op jit(solution)/shard_map/ppermute | solution.py:24
  30.4 7.7 %collective-permute-start.5 = (bf16[64,2048]{1,0:T(8,128)(2,1)S(1)}, bf16[64,2048]{1,0:T(8,128)(2,1)S(1)}, u32[]{:S(2)}, u32[]{:S(2)}) collective-permute-start(bf16[64,2048]{1,0:T(8,128)(2,1)S(1)} %collective-permute-done.4.refs_3_), channel_id=1, source_target_pairs={{0,8},{8,16},{16,24},{24,32},{32,40},{40,48},{48,56},{56,0},{1,9},... | collective-permute-start | bytes 786440 | tf_op jit(solution)/shard_map/ppermute | solution.py:24
  38.1 9.6 %collective-permute-start.14 = (bf16[32,2048]{1,0:T(8,128)(2,1)S(1)}, bf16[32,2048]{1,0:T(8,128)(2,1)S(1)}, u32[]{:S(2)}, u32[]{:S(2)}) collective-permute-start(bf16[32,2048]{1,0:T(8,128)(2,1)S(1)} %get-tuple-element.64), channel_id=1, source_target_pairs={{0,56},{8,0},{16,8},{24,16},{32,24},{40,32},{48,40},{56,48},{1,57}... | collective-permute-start | bytes 393224 | tf_op jit(solution)/shard_map/ppermute | solution.py:24
  49.6 7.1 %collective-permute-start.15 = (bf16[128,1920]{1,0:T(8,128)(2,1)S(1)}, bf16[128,1920]{1,0:T(8,128)(2,1)S(1)}, u32[]{:S(2)}, u32[]{:S(2)}) collective-permute-start(bf16[128,1920]{1,0:T(8,128)(2,1)S(1)} %get-tuple-element.68), channel_id=1, source_target_pairs={{0,1},{1,0},{2,3},{3,2},{4,5},{5,4},{6,7},{7,6},{8,9},{9,8},{10,11... | collective-permute-start | bytes 1474568 | tf_op jit(solution)/shard_map/ppermute | solution.py:24
  50.8 8.1 %collective-permute-start.10 = (bf16[32,1920]{1,0:T(8,128)(2,1)S(1)}, bf16[32,1920]{1,0:T(8,128)(2,1)S(1)}, u32[]{:S(2)}, u32[]{:S(2)}) collective-permute-start(bf16[32,1920]{1,0:T(8,128)(2,1)S(1)} %get-tuple-element.61), channel_id=1, source_target_pairs={{0,2},{2,4},{4,6},{6,0},{1,3},{3,5},{5,7},{7,1},{8,10},{10,12},{12... | collective-permute-start | bytes 368648 | tf_op jit(solution)/shard_map/ppermute | solution.py:24
  52.5 9.7 %collective-permute-start.11 = (bf16[32,1920]{1,0:T(8,128)(2,1)S(1)}, bf16[32,1920]{1,0:T(8,128)(2,1)S(1)}, u32[]{:S(2)}, u32[]{:S(2)}) collective-permute-start(bf16[32,1920]{1,0:T(8,128)(2,1)S(1)} %get-tuple-element.62), channel_id=1, source_target_pairs={{0,4},{2,6},{4,0},{6,2},{1,5},{3,7},{5,1},{7,3},{8,12},{10,14},{12... | collective-permute-start | bytes 368648 | tf_op jit(solution)/shard_map/ppermute | solution.py:24
  55.3 6.8 %collective-permute-start.12 = (bf16[32,1920]{1,0:T(8,128)(2,1)S(1)}, bf16[32,1920]{1,0:T(8,128)(2,1)S(1)}, u32[]{:S(2)}, u32[]{:S(2)}) collective-permute-start(bf16[32,1920]{1,0:T(8,128)(2,1)S(1)} %get-tuple-element.63), channel_id=1, source_target_pairs={{0,6},{2,0},{4,2},{6,4},{1,7},{3,1},{5,3},{7,5},{8,14},{10,8},{12,... | collective-permute-start | bytes 368648 | tf_op jit(solution)/shard_map/ppermute | solution.py:24
  57.4 7.5 %collective-permute-start.16 = (bf16[32,1920]{1,0:T(8,128)(2,1)S(1)}, bf16[32,1920]{1,0:T(8,128)(2,1)S(1)}, u32[]{:S(2)}, u32[]{:S(2)}) collective-permute-start(bf16[32,1920]{1,0:T(8,128)(2,1)S(1)} %get-tuple-element.70), channel_id=1, source_target_pairs={{0,2},{2,4},{4,6},{6,0},{1,3},{3,5},{5,7},{7,1},{8,10},{10,12},{12... | collective-permute-start | bytes 368648 | tf_op jit(solution)/shard_map/ppermute | solution.py:24
  58.1 8.4 %collective-permute-start.17 = (bf16[32,1920]{1,0:T(8,128)(2,1)S(1)}, bf16[32,1920]{1,0:T(8,128)(2,1)S(1)}, u32[]{:S(2)}, u32[]{:S(2)}) collective-permute-start(bf16[32,1920]{1,0:T(8,128)(2,1)S(1)} %get-tuple-element.71), channel_id=1, source_target_pairs={{0,4},{2,6},{4,0},{6,2},{1,5},{3,7},{5,1},{7,3},{8,12},{10,14},{12... | collective-permute-start | bytes 368648 | tf_op jit(solution)/shard_map/ppermute | solution.py:24
  58.9 7.6 %collective-permute-start.18 = (bf16[32,1920]{1,0:T(8,128)(2,1)S(1)}, bf16[32,1920]{1,0:T(8,128)(2,1)S(1)}, u32[]{:S(2)}, u32[]{:S(2)}) collective-permute-start(bf16[32,1920]{1,0:T(8,128)(2,1)S(1)} %get-tuple-element.72), channel_id=1, source_target_pairs={{0,6},{2,0},{4,2},{6,4},{1,7},{3,1},{5,3},{7,5},{8,14},{10,8},{12,... | collective-permute-start | bytes 368648 | tf_op jit(solution)/shard_map/ppermute | solution.py:24
  69.2 6.9 %collective-permute-start.20 = (bf16[64,896]{1,0:T(8,128)(2,1)S(1)}, bf16[64,896]{1,0:T(8,128)(2,1)S(1)}, u32[]{:S(2)}, u32[]{:S(2)}) collective-permute-start(bf16[64,896]{1,0:T(8,128)(2,1)S(1)} %shard_map.119.refs_0_), channel_id=1, source_target_pairs={{0,4},{2,6},{4,0},{6,2},{1,5},{3,7},{5,1},{7,3},{8,12},{10,14},{12... | collective-permute-start | bytes 344072 | tf_op jit(solution)/shard_map/ppermute | solution.py:24
  70.1 7.0 %collective-permute-start.19 = (bf16[64,896]{1,0:T(8,128)(2,1)S(1)}, bf16[64,896]{1,0:T(8,128)(2,1)S(1)}, u32[]{:S(2)}, u32[]{:S(2)}) collective-permute-start(bf16[64,896]{1,0:T(8,128)(2,1)S(1)} %shard_map.119.refs_0_), channel_id=1, source_target_pairs={{0,2},{2,4},{4,6},{6,0},{1,3},{3,5},{5,7},{7,1},{8,10},{10,12},{12... | collective-permute-start | bytes 344072 | tf_op jit(solution)/shard_map/ppermute | solution.py:24
  80.5 7.6 %collective-permute-start.26 = (bf16[32,2048]{1,0:T(8,128)(2,1)S(1)}, bf16[32,2048]{1,0:T(8,128)(2,1)S(1)}, u32[]{:S(2)}, u32[]{:S(2)}) collective-permute-start(bf16[32,2048]{1,0:T(8,128)(2,1)S(1)} %get-tuple-element.74), channel_id=1, source_target_pairs={{0,56},{8,0},{16,8},{24,16},{32,24},{40,32},{48,40},{56,48},{1,57}... | collective-permute-start | bytes 393224 | tf_op jit(solution)/shard_map/ppermute | solution.py:24
  82.6 8.8 %collective-permute-start.34 = (bf16[32,2048]{1,0:T(8,128)(2,1)S(1)}, bf16[32,2048]{1,0:T(8,128)(2,1)S(1)}, u32[]{:S(2)}, u32[]{:S(2)}) collective-permute-start(bf16[32,2048]{1,0:T(8,128)(2,1)S(1)} %get-tuple-element.84), channel_id=1, source_target_pairs={{0,8},{8,16},{16,24},{24,32},{32,40},{40,48},{48,56},{56,0},{1,9},... | collective-permute-start | bytes 393224 | tf_op jit(solution)/shard_map/ppermute | solution.py:24
  82.6 9.1 %collective-permute-start.30 = (bf16[32,2048]{1,0:T(8,128)(2,1)S(1)}, bf16[32,2048]{1,0:T(8,128)(2,1)S(1)}, u32[]{:S(2)}, u32[]{:S(2)}) collective-permute-start(bf16[32,2048]{1,0:T(8,128)(2,1)S(1)} %get-tuple-element.78), channel_id=1, source_target_pairs={{0,8},{8,16},{16,24},{24,32},{32,40},{40,48},{48,56},{56,0},{1,9},... | collective-permute-start | bytes 393224 | tf_op jit(solution)/shard_map/ppermute | solution.py:24
  83.4 8.4 %collective-permute-start.38 = (bf16[32,2048]{1,0:T(8,128)(2,1)S(1)}, bf16[32,2048]{1,0:T(8,128)(2,1)S(1)}, u32[]{:S(2)}, u32[]{:S(2)}) collective-permute-start(bf16[32,2048]{1,0:T(8,128)(2,1)S(1)} %get-tuple-element.88), channel_id=1, source_target_pairs={{0,56},{8,0},{16,8},{24,16},{32,24},{40,32},{48,40},{56,48},{1,57}... | collective-permute-start | bytes 393224 | tf_op jit(solution)/shard_map/ppermute | solution.py:24
  91.7 7.1 %collective-permute-start.31 = (bf16[32,2048]{1,0:T(8,128)(2,1)S(1)}, bf16[32,2048]{1,0:T(8,128)(2,1)S(1)}, u32[]{:S(2)}, u32[]{:S(2)}) collective-permute-start(bf16[32,2048]{1,0:T(8,128)(2,1)S(1)} %shard_map.125), channel_id=1, source_target_pairs={{0,8},{8,16},{16,24},{24,32},{32,40},{40,48},{48,56},{56,0},{1,9},... | collective-permute-start | bytes 393224 | tf_op jit(solution)/shard_map/ppermute | solution.py:24
  91.9 7.4 %collective-permute-start.39 = (bf16[32,2048]{1,0:T(8,128)(2,1)S(1)}, bf16[32,2048]{1,0:T(8,128)(2,1)S(1)}, u32[]{:S(2)}, u32[]{:S(2)}) collective-permute-start(bf16[32,2048]{1,0:T(8,128)(2,1)S(1)} %shard_map.131), channel_id=1, source_target_pairs={{0,56},{8,0},{16,8},{24,16},{32,24},{40,32},{48,40},{56,48},{1,57}... | collective-permute-start | bytes 393224 | tf_op jit(solution)/shard_map/ppermute | solution.py:24
  98.3 8.1 %collective-permute-start.36 = (bf16[32,2048]{1,0:T(8,128)(2,1)S(1)}, bf16[32,2048]{1,0:T(8,128)(2,1)S(1)}, u32[]{:S(2)}, u32[]{:S(2)}) collective-permute-start(bf16[32,2048]{1,0:T(8,128)(2,1)S(1)} %shard_map.129), channel_id=1, source_target_pairs={{0,8},{8,16},{16,24},{24,32},{32,40},{40,48},{48,56},{56,0},{1,9},... | collective-permute-start | bytes 393224 | tf_op jit(solution)/shard_map/ppermute | solution.py:24
  98.9 7.6 %collective-permute-start.32 = (bf16[32,2048]{1,0:T(8,128)(2,1)S(1)}, bf16[32,2048]{1,0:T(8,128)(2,1)S(1)}, u32[]{:S(2)}, u32[]{:S(2)}) collective-permute-start(bf16[32,2048]{1,0:T(8,128)(2,1)S(1)} %shard_map.126), channel_id=1, source_target_pairs={{0,8},{8,16},{16,24},{24,32},{32,40},{40,48},{48,56},{56,0},{1,9},... | collective-permute-start | bytes 393224 | tf_op jit(solution)/shard_map/ppermute | solution.py:24
  (27 other events, 186.5 us)

commit v9 on v8

--- a/solution.py
+++ b/solution.py
@@ -18,6 +18,7 @@
 EARLY = 4
 FAR = 5
 AWAY = (2, 1, 3)
+SLOTS = (0, 2, 1, 3)
 
 
 def shift(v, axis, by, n):
@@ -130,7 +131,7 @@
     parts, out = refs[:-1], refs[-1]
     size = parts[0].shape[0]
     for k, part in enumerate(parts, 1):
-        out[pl.ds(k * size, size), :] = part[...]
+        out[pl.ds(SLOTS[k] * size, size), :] = part[...]
 
 
 def place(core, pieces, part):
@@ -432,10 +433,10 @@
     far = NZ // 2
     low = [chain(0, -1, far), chain(0, 1, far - 1)]
     high = [chain(1, 1, far), chain(1, -1, far - 1)]
-    mine, one = call(
+    mine, two = call(
         z_sum, [shape(rows, feats, kind=f32), shape(rows, feats)], [terms[0][0]] + low, "vvv", moved=4 * piece * feats
     )
-    two, three = call(z_sum, [shape(rows, feats)] * 2, [terms[0][1]] + high, "vvv", moved=4 * piece * feats)
+    one, three = call(z_sum, [shape(rows, feats)] * 2, [terms[0][1]] + high, "vvv", moved=4 * piece * feats)
     sent = {1: one, 2: two, 3: three}
     parts = {k: shift(sent[k], "x", -k, NX) for k in AWAY}
     return call(finish, shape(rows, feats), [stream, mine] + [parts[k] for k in range(1, NX)], "v" * 5, moved=20 * rows * feats)

time: 120 us -> 119 us (level)
  waiting for transfers between devices: 39.9 us -> 37.7 us
    ppermute x43, waiting for transfers between devices: 39.9 us -> 37.7 us  [shift(): return lax.ppermute(v, axis, [(i, (i + by) % n) for i in range(n)])]
    ppermute x43, starting transfers between devices: 54.7 us -> 55.9 us  [shift(): return lax.ppermute(v, axis, [(i, (i + by) % n) for i in range(n)])]
where the time goes in v9:
time: 119 us
  starting transfers between devices  55.9 us (47%)
  waiting for transfers between devices  37.7 us (32%)
  Pallas kernels  21 us (18%)
  local copies, waits for them, and re-layouts  3.63 us (3%)
    ppermute x43, starting transfers between devices, shift(): return lax.ppermute(v, axis, [(i, (i + by) % n) for i in range(n)])  55.9 us
    ppermute x43, waiting for transfers between devices, shift(): return lax.ppermute(v, axis, [(i, (i + by) % n) for i in range(n)])  37.7 us
    pallas_call x26, Pallas kernels, call(): pl.pallas_call(kernel, out_shape=whole, in_specs=[pl.BlockSpec(memory_spa...  21 us
    unnamed x16, local copies, waits for them, and re-layouts  3.63 us
  transfers between devices with their start and end apart: 43, of which 23 were waited for; matrix products, arithmetic and copies ran while one was open for 0% of the time, Pallas kernels for 13%

profile of v9, /device:TPU:32, one launch (start us, length us, event | category | flops | bytes accessed | tf_op | source)
XLA Modules:
  0.0 118.5 jit_solution(6040392173194897917)
XLA Ops:
  0.0 2.6 %shard_map.109 = (f32[16,2048]{1,0:T(8,128)}, f32[16,128]{1,0:T(8,128)}, bf16[16,2048]{1,0:T(8,128)(2,1)}) custom-call(s32[16]{0:T(128)} %lengths_in.1, bf16[16,2048]{1,0:T(8,128)(2,1)} %hidden_in.1, bf16[16,2048]{1,0:T(8,128)(2,1)} %queries_in.1, bf16[16,128,128]{2,1,0:T(8,128)(2,1)} %keys_in.1, bf16[16,128,128]{2,1,0:T(8,128)(2,1)} %values_in.1, ...), custom_call_target="tpu_custom_call" | custom-call | bytes 1048576 | tf_op jit(solution)/shard_map/pallas_call | solution.py:36
  2.6 2.8 %collective-permute-start.2 = (bf16[16,2048]{1,0:T(8,128)(2,1)}, bf16[16,2048]{1,0:T(8,128)(2,1)S(1)}, u32[]{:S(2)}, u32[]{:S(2)}) collective-permute-start(bf16[16,2048]{1,0:T(8,128)(2,1)} %get-tuple-element.50.own), channel_id=1, source_target_pairs={{0,192},{64,0},{128,64},{192,128},{1,193},{65,1},{129,65},{193,129... | collective-permute-start | bytes 196616 | tf_op jit(solution)/shard_map/ppermute | solution.py:25
  8.0 3.4 %collective-permute-done.1.refs_1_ = bf16[16,2048]{1,0:T(8,128)(2,1)S(1)} collective-permute-done((bf16[16,2048]{1,0:T(8,128)(2,1)}, bf16[16,2048]{1,0:T(8,128)(2,1)S(1)}, u32[]{:S(2)}, u32[]{:S(2)}) %collective-permute-start.1) | collective-permute-done | bytes 65568 | tf_op jit(solution)/shard_map/ppermute | solution.py:25
  14.3 4.8 %collective-permute-done.6.refs_2_ = bf16[64,2048]{1,0:T(8,128)(2,1)S(1)} collective-permute-done((bf16[64,2048]{1,0:T(8,128)(2,1)S(1)}, bf16[64,2048]{1,0:T(8,128)(2,1)S(1)}, u32[]{:S(2)}, u32[]{:S(2)}) %collective-permute-start.6) | collective-permute-done | bytes 262176 | tf_op jit(solution)/shard_map/ppermute | solution.py:25
  19.0 3.3 %collective-permute-start.7 = (bf16[64,2048]{1,0:T(8,128)(2,1)S(1)}, bf16[64,2048]{1,0:T(8,128)(2,1)S(1)}, u32[]{:S(2)}, u32[]{:S(2)}) collective-permute-start(bf16[64,2048]{1,0:T(8,128)(2,1)S(1)} %collective-permute-done.6.refs_2_), channel_id=1, source_target_pairs={{0,56},{8,0},{16,8},{24,16},{32,24},{40,32},{48,40},{56,48},{1,57}... | collective-permute-start | bytes 786440 | tf_op jit(solution)/shard_map/ppermute | solution.py:25
  22.8 3.4 %collective-permute-done.7.refs_4_.refs_0_ = bf16[64,2048]{1,0:T(8,128)(2,1)S(1)} collective-permute-done((bf16[64,2048]{1,0:T(8,128)(2,1)S(1)}, bf16[64,2048]{1,0:T(8,128)(2,1)S(1)}, u32[]{:S(2)}, u32[]{:S(2)}) %collective-permute-start.7) | collective-permute-done | bytes 262176 | tf_op jit(solution)/shard_map/ppermute | solution.py:25
  26.2 3.7 %collective-permute-start.8 = (bf16[64,2048]{1,0:T(8,128)(2,1)S(1)}, bf16[64,2048]{1,0:T(8,128)(2,1)S(1)}, u32[]{:S(2)}, u32[]{:S(2)}) collective-permute-start(bf16[64,2048]{1,0:T(8,128)(2,1)S(1)} %collective-permute-done.7.refs_4_.refs_0_), channel_id=1, source_target_pairs={{0,56},{8,0},{16,8},{24,16},{32,24},{40,32},{48,40},{56,48},{1,57}... | collective-permute-start | bytes 786440 | tf_op jit(solution)/shard_map/ppermute | solution.py:25
  33.2 3.0 %shard_map.112 = (bf16[128,1920]{1,0:T(8,128)(2,1)S(1)}, bf16[128,1920]{1,0:T(8,128)(2,1)S(1)}, bf16[256,2048]{1,0:T(8,128)(2,1)S(1)}, f32[8,128]{1,0:T(8,128)S(1)}) custom-call(s32[4]{0:T(128)S(1)} %pad_add_fusion.idx, bf16[64,2048]{1,0:T(8,128)(2,1)S(1)} %shard_map.111.refs_0_, bf16[64,2048]{1,0:T(8,128)(2,1)S(1)} %collective-permute-done.3.refs_1_, ...), custom_call_target="tpu_custom_call" | custom-call | flops 939524096 | bytes 3670016 | tf_op jit(solution)/shard_map/pallas_call | solution.py:36
  38.1 3.3 %collective-permute-start.14 = (bf16[32,2048]{1,0:T(8,128)(2,1)S(1)}, bf16[32,2048]{1,0:T(8,128)(2,1)S(1)}, u32[]{:S(2)}, u32[]{:S(2)}) collective-permute-start(bf16[32,2048]{1,0:T(8,128)(2,1)S(1)} %get-tuple-element.64), channel_id=1, source_target_pairs={{0,56},{8,0},{16,8},{24,16},{32,24},{40,32},{48,40},{56,48},{1,57}... | collective-permute-start | bytes 393224 | tf_op jit(solution)/shard_map/ppermute | solution.py:25
  43.2 4.2 %shard_map.115 = (bf16[128,1920]{1,0:T(8,128)(2,1)S(1)}, bf16[128,1920]{1,0:T(8,128)(2,1)S(1)}, bf16[128,1920]{1,0:T(8,128)(2,1)S(1)}) custom-call(s32[4]{0:T(128)S(1)} %pad_add_fusion.idx, bf16[64,2048]{1,0:T(8,128)(2,1)S(1)} %collective-permute-done.7.refs_4_.refs_0_, ...), custom_call_target="tpu_custom_call", output_to_operand_aliasing={{2}: (4, {})} | custom-call | flops 1409286144 | bytes 7340032 | tf_op jit(solution)/shard_map/pallas_call | solution.py:36
  52.5 2.9 %collective-permute-start.11 = (bf16[32,1920]{1,0:T(8,128)(2,1)S(1)}, bf16[32,1920]{1,0:T(8,128)(2,1)S(1)}, u32[]{:S(2)}, u32[]{:S(2)}) collective-permute-start(bf16[32,1920]{1,0:T(8,128)(2,1)S(1)} %get-tuple-element.62), channel_id=1, source_target_pairs={{0,4},{2,6},{4,0},{6,2},{1,5},{3,7},{5,1},{7,3},{8,12},{10,14},{12... | collective-permute-start | bytes 368648 | tf_op jit(solution)/shard_map/ppermute | solution.py:25
  62.1 2.7 %collective-permute-done.16.refs_5_ = bf16[32,1920]{1,0:T(8,128)(2,1)S(1)} collective-permute-done((bf16[32,1920]{1,0:T(8,128)(2,1)S(1)}, bf16[32,1920]{1,0:T(8,128)(2,1)S(1)}, u32[]{:S(2)}, u32[]{:S(2)}) %collective-permute-start.16) | collective-permute-done | bytes 122912 | tf_op jit(solution)/shard_map/ppermute | solution.py:25
  66.8 2.4 %collective-permute-start.21 = (bf16[64,896]{1,0:T(8,128)(2,1)S(1)}, bf16[64,896]{1,0:T(8,128)(2,1)S(1)}, u32[]{:S(2)}, u32[]{:S(2)}) collective-permute-start(bf16[64,896]{1,0:T(8,128)(2,1)S(1)} %shard_map.119.refs_0_), channel_id=1, source_target_pairs={{0,6},{2,0},{4,2},{6,4},{1,7},{3,1},{5,3},{7,5},{8,14},{10,8},{12,... | collective-permute-start | bytes 344072 | tf_op jit(solution)/shard_map/ppermute | solution.py:25
  70.8 2.8 %collective-permute-done.21.refs_3_ = bf16[64,896]{1,0:T(8,128)(2,1)S(1)} collective-permute-done((bf16[64,896]{1,0:T(8,128)(2,1)S(1)}, bf16[64,896]{1,0:T(8,128)(2,1)S(1)}, u32[]{:S(2)}, u32[]{:S(2)}) %collective-permute-start.21) | collective-permute-done | bytes 114720 | tf_op jit(solution)/shard_map/ppermute | solution.py:25
  73.6 2.5 %collective-permute-done.20.refs_2_ = bf16[64,896]{1,0:T(8,128)(2,1)S(1)} collective-permute-done((bf16[64,896]{1,0:T(8,128)(2,1)S(1)}, bf16[64,896]{1,0:T(8,128)(2,1)S(1)}, u32[]{:S(2)}, u32[]{:S(2)}) %collective-permute-start.20) | collective-permute-done | bytes 114720 | tf_op jit(solution)/shard_map/ppermute | solution.py:25
  78.4 2.1 %shard_map.121 = (bf16[32,2048]{1,0:T(8,128)(2,1)S(1)}, bf16[32,2048]{1,0:T(8,128)(2,1)S(1)}, bf16[32,2048]{1,0:T(8,128)(2,1)S(1)}, bf16[32,2048]{1,0:T(8,128)(2...) custom-call(s32[4]{0:T(128)S(1)} %pad_add_fusion.idx, bf16[64,896]{1,0:T(8,128)(2,1)S(1)} %shard_map.119.refs_0_, ...), custom_call_target="tpu_custom_call" | custom-call | flops 704643072 | bytes 3670016 | tf_op jit(solution)/shard_map/pallas_call | solution.py:36
  85.4 2.7 %shard_map.120 = (bf16[32,2048]{1,0:T(8,128)(2,1)S(1)}, bf16[32,2048]{1,0:T(8,128)(2,1)S(1)}, bf16[32,2048]{1,0:T(8,128)(2,1)S(1)}, bf16[32,2048]{1,0:T(8,128)(2...) custom-call(s32[4]{0:T(128)S(1)} %pad_add_fusion.idx, ...), custom_call_target="tpu_custom_call" | custom-call | flops 1174405120 | bytes 3670016 | tf_op jit(solution)/shard_map/pallas_call | solution.py:36
  88.1 3.3 %collective-permute-start.27 = (bf16[32,2048]{1,0:T(8,128)(2,1)S(1)}, bf16[32,2048]{1,0:T(8,128)(2,1)S(1)}, u32[]{:S(2)}, u32[]{:S(2)}) collective-permute-start(bf16[32,2048]{1,0:T(8,128)(2,1)S(1)} %shard_map.122), channel_id=1, source_target_pairs={{0,56},{8,0},{16,8},{24,16},{32,24},{40,32},{48,40},{56,48},{1,57}... | collective-permute-start | bytes 393224 | tf_op jit(solution)/shard_map/ppermute | solution.py:25
  91.9 3.0 %collective-permute-start.38 = (bf16[32,2048]{1,0:T(8,128)(2,1)S(1)}, bf16[32,2048]{1,0:T(8,128)(2,1)S(1)}, u32[]{:S(2)}, u32[]{:S(2)}) collective-permute-start(bf16[32,2048]{1,0:T(8,128)(2,1)S(1)} %shard_map.131), channel_id=1, source_target_pairs={{0,56},{8,0},{16,8},{24,16},{32,24},{40,32},{48,40},{56,48},{1,57}... | collective-permute-start | bytes 393224 | tf_op jit(solution)/shard_map/ppermute | solution.py:25
  95.0 3.3 %collective-permute-start.28 = (bf16[32,2048]{1,0:T(8,128)(2,1)S(1)}, bf16[32,2048]{1,0:T(8,128)(2,1)S(1)}, u32[]{:S(2)}, u32[]{:S(2)}) collective-permute-start(bf16[32,2048]{1,0:T(8,128)(2,1)S(1)} %shard_map.123), channel_id=1, source_target_pairs={{0,56},{8,0},{16,8},{24,16},{32,24},{40,32},{48,40},{56,48},{1,57}... | collective-permute-start | bytes 393224 | tf_op jit(solution)/shard_map/ppermute | solution.py:25
  100.8 2.5 %collective-permute-start.29 = (bf16[32,2048]{1,0:T(8,128)(2,1)S(1)}, bf16[32,2048]{1,0:T(8,128)(2,1)S(1)}, u32[]{:S(2)}, u32[]{:S(2)}) collective-permute-start(bf16[32,2048]{1,0:T(8,128)(2,1)S(1)} %shard_map.124), channel_id=1, source_target_pairs={{0,56},{8,0},{16,8},{24,16},{32,24},{40,32},{48,40},{56,48},{1,57}... | collective-permute-start | bytes 393224 | tf_op jit(solution)/shard_map/ppermute | solution.py:25
  103.3 3.1 %collective-permute-start.39 = (bf16[32,2048]{1,0:T(8,128)(2,1)S(1)}, bf16[32,2048]{1,0:T(8,128)(2,1)S(1)}, u32[]{:S(2)}, u32[]{:S(2)}) collective-permute-start(bf16[32,2048]{1,0:T(8,128)(2,1)S(1)} %shard_map.132), channel_id=1, source_target_pairs={{0,56},{8,0},{16,8},{24,16},{32,24},{40,32},{48,40},{56,48},{1,57}... | collective-permute-start | bytes 393224 | tf_op jit(solution)/shard_map/ppermute | solution.py:25
  108.9 2.6 %collective-permute-done.36.one = bf16[32,2048]{1,0:T(8,128)(2,1)S(1)} collective-permute-done((bf16[32,2048]{1,0:T(8,128)(2,1)S(1)}, bf16[32,2048]{1,0:T(8,128)(2,1)S(1)}, u32[]{:S(2)}, u32[]{:S(2)}) %collective-permute-start.36) | collective-permute-done | bytes 131104 | tf_op jit(solution)/shard_map/ppermute | solution.py:25
  113.6 2.2 %collective-permute-done.40.one = bf16[16,2048]{1,0:T(8,128)(2,1)S(1)} collective-permute-done((bf16[16,2048]{1,0:T(8,128)(2,1)S(1)}, bf16[16,2048]{1,0:T(8,128)(2,1)S(1)}, u32[]{:S(2)}, u32[]{:S(2)}) %collective-permute-start.40) | collective-permute-done | bytes 65568 | tf_op jit(solution)/shard_map/ppermute | solution.py:25
  (105 shorter events, 45.5 us)
Async XLA Ops:
  12.2 6.9 %collective-permute-start.6 = (bf16[64,2048]{1,0:T(8,128)(2,1)S(1)}, bf16[64,2048]{1,0:T(8,128)(2,1)S(1)}, u32[]{:S(2)}, u32[]{:S(2)}) collective-permute-start(bf16[64,2048]{1,0:T(8,128)(2,1)S(1)} %shard_map.111.refs_0_), channel_id=1, source_target_pairs={{0,56},{8,0},{16,8},{24,16},{32,24},{40,32},{48,40},{56,48},{1,57}... | collective-permute-start | bytes 786440 | tf_op jit(solution)/shard_map/ppermute | solution.py:25
  12.3 10.4 %collective-permute-start.3 = (bf16[64,2048]{1,0:T(8,128)(2,1)S(1)}, bf16[64,2048]{1,0:T(8,128)(2,1)S(1)}, u32[]{:S(2)}, u32[]{:S(2)}) collective-permute-start(bf16[64,2048]{1,0:T(8,128)(2,1)S(1)} %shard_map.111.refs_0_), channel_id=1, source_target_pairs={{0,8},{8,16},{16,24},{24,32},{32,40},{40,48},{48,56},{56,0},{1,9},... | collective-permute-start | bytes 786440 | tf_op jit(solution)/shard_map/ppermute | solution.py:25
  19.0 7.2 %collective-permute-start.7 = (bf16[64,2048]{1,0:T(8,128)(2,1)S(1)}, bf16[64,2048]{1,0:T(8,128)(2,1)S(1)}, u32[]{:S(2)}, u32[]{:S(2)}) collective-permute-start(bf16[64,2048]{1,0:T(8,128)(2,1)S(1)} %collective-permute-done.6.refs_2_), channel_id=1, source_target_pairs={{0,56},{8,0},{16,8},{24,16},{32,24},{40,32},{48,40},{56,48},{1,57}... | collective-permute-start | bytes 786440 | tf_op jit(solution)/shard_map/ppermute | solution.py:25
  22.8 7.6 %collective-permute-start.4 = (bf16[64,2048]{1,0:T(8,128)(2,1)S(1)}, bf16[64,2048]{1,0:T(8,128)(2,1)S(1)}, u32[]{:S(2)}, u32[]{:S(2)}) collective-permute-start(bf16[64,2048]{1,0:T(8,128)(2,1)S(1)} %collective-permute-done.3.refs_1_), channel_id=1, source_target_pairs={{0,8},{8,16},{16,24},{24,32},{32,40},{40,48},{48,56},{56,0},{1,9},... | collective-permute-start | bytes 786440 | tf_op jit(solution)/shard_map/ppermute | solution.py:25
  26.2 10.0 %collective-permute-start.8 = (bf16[64,2048]{1,0:T(8,128)(2,1)S(1)}, bf16[64,2048]{1,0:T(8,128)(2,1)S(1)}, u32[]{:S(2)}, u32[]{:S(2)}) collective-permute-start(bf16[64,2048]{1,0:T(8,128)(2,1)S(1)} %collective-permute-done.7.refs_4_.refs_0_), channel_id=1, source_target_pairs={{0,56},{8,0},{16,8},{24,16},{32,24},{40,32},{48,40},{56,48},{1,57}... | collective-permute-start | bytes 786440 | tf_op jit(solution)/shard_map/ppermute | solution.py:25
  30.4 7.7 %collective-permute-start.5 = (bf16[64,2048]{1,0:T(8,128)(2,1)S(1)}, bf16[64,2048]{1,0:T(8,128)(2,1)S(1)}, u32[]{:S(2)}, u32[]{:S(2)}) collective-permute-start(bf16[64,2048]{1,0:T(8,128)(2,1)S(1)} %collective-permute-done.4.refs_3_), channel_id=1, source_target_pairs={{0,8},{8,16},{16,24},{24,32},{32,40},{40,48},{48,56},{56,0},{1,9},... | collective-permute-start | bytes 786440 | tf_op jit(solution)/shard_map/ppermute | solution.py:25
  38.1 9.6 %collective-permute-start.14 = (bf16[32,2048]{1,0:T(8,128)(2,1)S(1)}, bf16[32,2048]{1,0:T(8,128)(2,1)S(1)}, u32[]{:S(2)}, u32[]{:S(2)}) collective-permute-start(bf16[32,2048]{1,0:T(8,128)(2,1)S(1)} %get-tuple-element.64), channel_id=1, source_target_pairs={{0,56},{8,0},{16,8},{24,16},{32,24},{40,32},{48,40},{56,48},{1,57}... | collective-permute-start | bytes 393224 | tf_op jit(solution)/shard_map/ppermute | solution.py:25
  49.6 7.1 %collective-permute-start.15 = (bf16[128,1920]{1,0:T(8,128)(2,1)S(1)}, bf16[128,1920]{1,0:T(8,128)(2,1)S(1)}, u32[]{:S(2)}, u32[]{:S(2)}) collective-permute-start(bf16[128,1920]{1,0:T(8,128)(2,1)S(1)} %get-tuple-element.68), channel_id=1, source_target_pairs={{0,1},{1,0},{2,3},{3,2},{4,5},{5,4},{6,7},{7,6},{8,9},{9,8},{10,11... | collective-permute-start | bytes 1474568 | tf_op jit(solution)/shard_map/ppermute | solution.py:25
  50.8 8.1 %collective-permute-start.10 = (bf16[32,1920]{1,0:T(8,128)(2,1)S(1)}, bf16[32,1920]{1,0:T(8,128)(2,1)S(1)}, u32[]{:S(2)}, u32[]{:S(2)}) collective-permute-start(bf16[32,1920]{1,0:T(8,128)(2,1)S(1)} %get-tuple-element.61), channel_id=1, source_target_pairs={{0,2},{2,4},{4,6},{6,0},{1,3},{3,5},{5,7},{7,1},{8,10},{10,12},{12... | collective-permute-start | bytes 368648 | tf_op jit(solution)/shard_map/ppermute | solution.py:25
  52.5 9.7 %collective-permute-start.11 = (bf16[32,1920]{1,0:T(8,128)(2,1)S(1)}, bf16[32,1920]{1,0:T(8,128)(2,1)S(1)}, u32[]{:S(2)}, u32[]{:S(2)}) collective-permute-start(bf16[32,1920]{1,0:T(8,128)(2,1)S(1)} %get-tuple-element.62), channel_id=1, source_target_pairs={{0,4},{2,6},{4,0},{6,2},{1,5},{3,7},{5,1},{7,3},{8,12},{10,14},{12... | collective-permute-start | bytes 368648 | tf_op jit(solution)/shard_map/ppermute | solution.py:25
  55.3 6.8 %collective-permute-start.12 = (bf16[32,1920]{1,0:T(8,128)(2,1)S(1)}, bf16[32,1920]{1,0:T(8,128)(2,1)S(1)}, u32[]{:S(2)}, u32[]{:S(2)}) collective-permute-start(bf16[32,1920]{1,0:T(8,128)(2,1)S(1)} %get-tuple-element.63), channel_id=1, source_target_pairs={{0,6},{2,0},{4,2},{6,4},{1,7},{3,1},{5,3},{7,5},{8,14},{10,8},{12,... | collective-permute-start | bytes 368648 | tf_op jit(solution)/shard_map/ppermute | solution.py:25
  57.4 7.5 %collective-permute-start.16 = (bf16[32,1920]{1,0:T(8,128)(2,1)S(1)}, bf16[32,1920]{1,0:T(8,128)(2,1)S(1)}, u32[]{:S(2)}, u32[]{:S(2)}) collective-permute-start(bf16[32,1920]{1,0:T(8,128)(2,1)S(1)} %get-tuple-element.70), channel_id=1, source_target_pairs={{0,2},{2,4},{4,6},{6,0},{1,3},{3,5},{5,7},{7,1},{8,10},{10,12},{12... | collective-permute-start | bytes 368648 | tf_op jit(solution)/shard_map/ppermute | solution.py:25
  58.1 8.4 %collective-permute-start.17 = (bf16[32,1920]{1,0:T(8,128)(2,1)S(1)}, bf16[32,1920]{1,0:T(8,128)(2,1)S(1)}, u32[]{:S(2)}, u32[]{:S(2)}) collective-permute-start(bf16[32,1920]{1,0:T(8,128)(2,1)S(1)} %get-tuple-element.71), channel_id=1, source_target_pairs={{0,4},{2,6},{4,0},{6,2},{1,5},{3,7},{5,1},{7,3},{8,12},{10,14},{12... | collective-permute-start | bytes 368648 | tf_op jit(solution)/shard_map/ppermute | solution.py:25
  58.9 7.6 %collective-permute-start.18 = (bf16[32,1920]{1,0:T(8,128)(2,1)S(1)}, bf16[32,1920]{1,0:T(8,128)(2,1)S(1)}, u32[]{:S(2)}, u32[]{:S(2)}) collective-permute-start(bf16[32,1920]{1,0:T(8,128)(2,1)S(1)} %get-tuple-element.72), channel_id=1, source_target_pairs={{0,6},{2,0},{4,2},{6,4},{1,7},{3,1},{5,3},{7,5},{8,14},{10,8},{12,... | collective-permute-start | bytes 368648 | tf_op jit(solution)/shard_map/ppermute | solution.py:25
  69.2 6.9 %collective-permute-start.20 = (bf16[64,896]{1,0:T(8,128)(2,1)S(1)}, bf16[64,896]{1,0:T(8,128)(2,1)S(1)}, u32[]{:S(2)}, u32[]{:S(2)}) collective-permute-start(bf16[64,896]{1,0:T(8,128)(2,1)S(1)} %shard_map.119.refs_0_), channel_id=1, source_target_pairs={{0,4},{2,6},{4,0},{6,2},{1,5},{3,7},{5,1},{7,3},{8,12},{10,14},{12... | collective-permute-start | bytes 344072 | tf_op jit(solution)/shard_map/ppermute | solution.py:25
  70.1 7.0 %collective-permute-start.19 = (bf16[64,896]{1,0:T(8,128)(2,1)S(1)}, bf16[64,896]{1,0:T(8,128)(2,1)S(1)}, u32[]{:S(2)}, u32[]{:S(2)}) collective-permute-start(bf16[64,896]{1,0:T(8,128)(2,1)S(1)} %shard_map.119.refs_0_), channel_id=1, source_target_pairs={{0,2},{2,4},{4,6},{6,0},{1,3},{3,5},{5,7},{7,1},{8,10},{10,12},{12... | collective-permute-start | bytes 344072 | tf_op jit(solution)/shard_map/ppermute | solution.py:25
  80.5 7.6 %collective-permute-start.26 = (bf16[32,2048]{1,0:T(8,128)(2,1)S(1)}, bf16[32,2048]{1,0:T(8,128)(2,1)S(1)}, u32[]{:S(2)}, u32[]{:S(2)}) collective-permute-start(bf16[32,2048]{1,0:T(8,128)(2,1)S(1)} %get-tuple-element.74), channel_id=1, source_target_pairs={{0,56},{8,0},{16,8},{24,16},{32,24},{40,32},{48,40},{56,48},{1,57}... | collective-permute-start | bytes 393224 | tf_op jit(solution)/shard_map/ppermute | solution.py:25
  82.6 8.8 %collective-permute-start.33 = (bf16[32,2048]{1,0:T(8,128)(2,1)S(1)}, bf16[32,2048]{1,0:T(8,128)(2,1)S(1)}, u32[]{:S(2)}, u32[]{:S(2)}) collective-permute-start(bf16[32,2048]{1,0:T(8,128)(2,1)S(1)} %get-tuple-element.83), channel_id=1, source_target_pairs={{0,8},{8,16},{16,24},{24,32},{32,40},{40,48},{48,56},{56,0},{1,9},... | collective-permute-start | bytes 393224 | tf_op jit(solution)/shard_map/ppermute | solution.py:25
  82.6 9.1 %collective-permute-start.30 = (bf16[32,2048]{1,0:T(8,128)(2,1)S(1)}, bf16[32,2048]{1,0:T(8,128)(2,1)S(1)}, u32[]{:S(2)}, u32[]{:S(2)}) collective-permute-start(bf16[32,2048]{1,0:T(8,128)(2,1)S(1)} %get-tuple-element.78), channel_id=1, source_target_pairs={{0,8},{8,16},{16,24},{24,32},{32,40},{40,48},{48,56},{56,0},{1,9},... | collective-permute-start | bytes 393224 | tf_op jit(solution)/shard_map/ppermute | solution.py:25
  83.4 8.4 %collective-permute-start.37 = (bf16[32,2048]{1,0:T(8,128)(2,1)S(1)}, bf16[32,2048]{1,0:T(8,128)(2,1)S(1)}, u32[]{:S(2)}, u32[]{:S(2)}) collective-permute-start(bf16[32,2048]{1,0:T(8,128)(2,1)S(1)} %get-tuple-element.87), channel_id=1, source_target_pairs={{0,56},{8,0},{16,8},{24,16},{32,24},{40,32},{48,40},{56,48},{1,57}... | collective-permute-start | bytes 393224 | tf_op jit(solution)/shard_map/ppermute | solution.py:25
  91.7 7.1 %collective-permute-start.31 = (bf16[32,2048]{1,0:T(8,128)(2,1)S(1)}, bf16[32,2048]{1,0:T(8,128)(2,1)S(1)}, u32[]{:S(2)}, u32[]{:S(2)}) collective-permute-start(bf16[32,2048]{1,0:T(8,128)(2,1)S(1)} %shard_map.125), channel_id=1, source_target_pairs={{0,8},{8,16},{16,24},{24,32},{32,40},{40,48},{48,56},{56,0},{1,9},... | collective-permute-start | bytes 393224 | tf_op jit(solution)/shard_map/ppermute | solution.py:25
  91.9 7.4 %collective-permute-start.38 = (bf16[32,2048]{1,0:T(8,128)(2,1)S(1)}, bf16[32,2048]{1,0:T(8,128)(2,1)S(1)}, u32[]{:S(2)}, u32[]{:S(2)}) collective-permute-start(bf16[32,2048]{1,0:T(8,128)(2,1)S(1)} %shard_map.131), channel_id=1, source_target_pairs={{0,56},{8,0},{16,8},{24,16},{32,24},{40,32},{48,40},{56,48},{1,57}... | collective-permute-start | bytes 393224 | tf_op jit(solution)/shard_map/ppermute | solution.py:25
  98.3 8.1 %collective-permute-start.35 = (bf16[32,2048]{1,0:T(8,128)(2,1)S(1)}, bf16[32,2048]{1,0:T(8,128)(2,1)S(1)}, u32[]{:S(2)}, u32[]{:S(2)}) collective-permute-start(bf16[32,2048]{1,0:T(8,128)(2,1)S(1)} %shard_map.129), channel_id=1, source_target_pairs={{0,8},{8,16},{16,24},{24,32},{32,40},{40,48},{48,56},{56,0},{1,9},... | collective-permute-start | bytes 393224 | tf_op jit(solution)/shard_map/ppermute | solution.py:25
  98.9 7.6 %collective-permute-start.32 = (bf16[32,2048]{1,0:T(8,128)(2,1)S(1)}, bf16[32,2048]{1,0:T(8,128)(2,1)S(1)}, u32[]{:S(2)}, u32[]{:S(2)}) collective-permute-start(bf16[32,2048]{1,0:T(8,128)(2,1)S(1)} %shard_map.126), channel_id=1, source_target_pairs={{0,8},{8,16},{16,24},{24,32},{32,40},{40,48},{48,56},{56,0},{1,9},... | collective-permute-start | bytes 393224 | tf_op jit(solution)/shard_map/ppermute | solution.py:25
  (27 other events, 184.3 us)
